TPU v7x, 256 devices: a whole 4x4x8 slice. The times are simulated.
256 devices in a mesh: ctx: 8 (over z), dp: 32 (over y, x, core).
Axes of the slice: x: 4, y: 4, z: 8, core: 2. Of those that a mesh axis runs over, the one named last changes fastest.
Arguments:
- layer_input: bfloat16 [32, 1024, 8192], P('dp', 'ctx'), may hold values from -6 to 6
- query: bfloat16 [32, 1024, 4096], P('dp', 'ctx'), may hold values from -6 to 6
- key: bfloat16 [32, 1024, 512], P('dp', 'ctx'), may hold values from -6 to 6
- value: bfloat16 [32, 1024, 512], P('dp', 'ctx'), may hold values from -6 to 6
- grad_out: bfloat16 [32, 1024, 4096], P('dp', 'ctx'), may hold values from -6 to 6
- doc_lengths: int32 [32, 8], P('dp'), may hold values from 1 to 512, 1024 in all within a row
- prefix_lengths: int32 [32, 8], P('dp'), may hold values from 1 to 512
- stretch_order: int32 [32, 16], P('dp'), may hold values from 0 to 15, each once within a row
Outputs:
- attn_out: bfloat16 [32, 1024, 4096], P('dp', 'ctx')
- grad_query: bfloat16 [32, 1024, 4096], P('dp', 'ctx')
- grad_key: bfloat16 [32, 1024, 512], P('dp', 'ctx')
- grad_wvalue: float32 [8192, 512], P(('dp', 'ctx'))
Inputs may be any that keep to these rules, and one draw needn't show every extreme that they name: `doc_lengths`: each row sums to 1024, and its longest document has exactly 512 tokens. `prefix_lengths`: a span longer than its document covers all of it. `stretch_order`: each row names every query stretch once.
All inputs are finite; a program needn't handle non-finite values.
Results may differ from a plain program's by a relative error of at most 0.025.
Values may be sent and summed in bfloat16 or wider, within the bound.
No kernel may reach another device: no remote copies, remote signals or barrier semaphores. Data moves between devices by JAX's collectives and lax.ppermute only.
A program may use at most 128 MiB of HBM per device.

v0:
```python
import math

import jax
import jax.numpy as jnp
from jax import lax
from jax.sharding import PartitionSpec as P

HEADS = 32
KV_HEADS = 4
HEAD_DIM = 128
GROUP = 8
CH = 64
NDOC = 8


neg_big = -1e30


def layout(order, lengths, prefix):
    within = jnp.arange(CH, dtype=jnp.int32)
    places = (order[:, None] * CH + within[None, :]).reshape(-1)
    starts = jnp.cumsum(lengths) - lengths
    owners = jnp.sum((starts[None, :] <= places[:, None]).astype(jnp.int32), axis=1) - 1
    ends = starts + jnp.minimum(prefix, lengths)
    match = owners[:, None] == jnp.arange(NDOC, dtype=jnp.int32)[None, :]
    open_end = jnp.sum(jnp.where(match, ends[None, :], 0), axis=1)
    return (places, owners, open_end)


def visible(q_places, q_owners, k_places, k_owners, k_open):
    same = q_owners[:, None] == k_owners[None, :]
    seen = (k_places[None, :] <= q_places[:, None]) | (k_places[None, :] < k_open[None, :])
    return same & seen


def on_device(layer_input, query, key, value, grad_out, doc_lengths, prefix_lengths, stretch_order):
    n_ctx = lax.axis_size("ctx")
    rows = query.shape[1]
    kv_width = key.shape[2]
    total = rows * n_ctx
    scale = HEAD_DIM ** (-0.5)
    places, owners, open_end = layout(stretch_order[0], doc_lengths[0], prefix_lengths[0])
    offset = lax.axis_index("ctx") * rows
    my_places = lax.dynamic_slice_in_dim(places, offset, rows)
    my_owners = lax.dynamic_slice_in_dim(owners, offset, rows)
    mask_all = visible(my_places, my_owners, places, owners, open_end)
    q4 = query[0].reshape(rows, KV_HEADS, GROUP, HEAD_DIM)
    g4 = grad_out[0].reshape(rows, KV_HEADS, GROUP, HEAD_DIM)

    def run_blocks(step, carry, arrays, start):
        count = arrays[0].shape[0]
        size = math.gcd(count, min(rows, 256))
        number = count // size
        shaped = tuple((a.reshape((number, size) + a.shape[1:]) for a in arrays))
        firsts = start + size * jnp.arange(number, dtype=jnp.int32)

        def advance(inner, items):
            result = step(inner, items[:-1], items[-1])
            return (result, None)

        carry, unused = lax.scan(advance, carry, shaped + (firsts,))
        return carry

    def scores_for(key_rows, first):
        k3 = key_rows.reshape(-1, KV_HEADS, HEAD_DIM)
        raw = jnp.einsum("qhgd,khd->hgqk", q4, k3, preferred_element_type=jnp.float32) * scale
        live = lax.dynamic_slice_in_dim(mask_all, first, key_rows.shape[0], 1)[None, None]
        return (jnp.where(live, raw, neg_big), live)

    def stats_step(carry, pieces, first):
        top, mass = carry
        masked, live = scores_for(pieces[0], first)
        new_top = jnp.maximum(top, jnp.max(masked, axis=-1))
        fresh = jnp.sum(jnp.where(live, jnp.exp(masked - new_top[..., None]), 0.0), axis=-1)
        return (new_top, mass * jnp.exp(top - new_top) + fresh)

    start_stats = (
        jnp.full((KV_HEADS, GROUP, rows), neg_big, jnp.float32),
        jnp.zeros((KV_HEADS, GROUP, rows), jnp.float32),
    )
    whole = (
        lax.all_gather(key[0], "ctx", axis=0, tiled=True),
        lax.all_gather(value[0], "ctx", axis=0, tiled=True),
    )
    top, mass = run_blocks(stats_step, start_stats, (whole[0],), 0)
    lse = top + jnp.log(mass)

    def probs_for(key_rows, first):
        masked, live = scores_for(key_rows, first)
        return jnp.where(live, jnp.exp(masked - lse[..., None]), 0.0).astype(jnp.bfloat16)

    def out_step(carry, pieces, first):
        weights = probs_for(pieces[0], first)
        v3 = pieces[1].reshape(-1, KV_HEADS, HEAD_DIM)
        return carry + jnp.einsum("hgqk,khd->qhgd", weights, v3, preferred_element_type=jnp.float32)

    empty_out = jnp.zeros((rows, KV_HEADS, GROUP, HEAD_DIM), jnp.float32)
    output = run_blocks(out_step, empty_out, whole, 0)
    delta = jnp.transpose(jnp.sum(g4 * output, axis=-1), (1, 2, 0))

    def back_step(carry, pieces, first):
        grad_q, grad_k, grad_v = carry
        weights = probs_for(pieces[0], first)
        k3 = pieces[0].reshape(-1, KV_HEADS, HEAD_DIM)
        v3 = pieces[1].reshape(-1, KV_HEADS, HEAD_DIM)
        dots = jnp.einsum("qhgd,khd->hgqk", g4, v3, preferred_element_type=jnp.float32)
        slopes = (weights.astype(jnp.float32) * (dots - delta[..., None]) * scale).astype(
            jnp.bfloat16
        )
        grad_q = grad_q + jnp.einsum(
            "hgqk,khd->qhgd", slopes, k3, preferred_element_type=jnp.float32
        )
        key_part = jnp.einsum(
            "hgqk,qhgd->khd", slopes, q4, preferred_element_type=jnp.float32
        ).reshape(-1, kv_width)
        value_part = jnp.einsum(
            "hgqk,qhgd->khd", weights, g4, preferred_element_type=jnp.float32
        ).reshape(-1, kv_width)
        grad_k = lax.dynamic_update_slice_in_dim(grad_k, key_part, first, 0)
        grad_v = lax.dynamic_update_slice_in_dim(grad_v, value_part, first, 0)
        return (grad_q, grad_k, grad_v)

    start_back = (
        empty_out,
        jnp.zeros((total, kv_width), jnp.float32),
        jnp.zeros((total, kv_width), jnp.float32),
    )
    grad_q, grad_k, grad_v = run_blocks(back_step, start_back, whole, 0)
    key_sum, value_sum = (
        lax.psum_scatter(
            grad_k.astype(jnp.bfloat16), "ctx", scatter_dimension=0, tiled=True
        ).astype(jnp.float32),
        lax.psum_scatter(
            grad_v.astype(jnp.bfloat16), "ctx", scatter_dimension=0, tiled=True
        ).astype(jnp.float32),
    )
    grad_key = key_sum.astype(jnp.bfloat16)
    grad_value = value_sum.astype(jnp.bfloat16)
    inputs = layer_input[0]
    partial_rows = lax.psum_scatter(
        lax.dot_general(
            inputs, grad_value, (((0,), (0,)), ((), ())), preferred_element_type=jnp.float32
        ).astype(jnp.bfloat16),
        "dp",
        scatter_dimension=0,
        tiled=True,
    )
    weight_grad = lax.psum_scatter(partial_rows, "ctx", scatter_dimension=0, tiled=True).astype(
        jnp.float32
    )
    attn_out = output.astype(jnp.bfloat16).reshape(1, rows, HEADS * HEAD_DIM)
    grad_query = grad_q.astype(jnp.bfloat16).reshape(1, rows, HEADS * HEAD_DIM)
    return (attn_out, grad_query, grad_key.reshape(1, rows, kv_width), weight_grad)


def solution(mesh):
    placed = (
        P("dp", "ctx", None),
        P("dp", "ctx", None),
        P("dp", "ctx", None),
        P("dp", "ctx", None),
        P("dp", "ctx", None),
        P("dp", None),
        P("dp", None),
        P("dp", None),
    )
    return jax.shard_map(
        on_device,
        mesh=mesh,
        in_specs=placed,
        out_specs=(
            P("dp", "ctx", None),
            P("dp", "ctx", None),
            P("dp", "ctx", None),
            P(("dp", "ctx"), None),
        ),
        check_vma=False,
    )
```

profile of v0, /device:TPU:2, one launch (start us, length us, event | category | flops | bytes accessed | tf_op | source)
XLA Modules:
  0.0 621.5 jit_solution(9893992279333227888)
XLA Ops:
  18.3 33.2 %all-gather.5.cloned.1.call-done = bf16[1,1024,512]{2,1,0:T(8,128)(2,1)} async-done(((bf16[1,128,512]{2,1,0:T(8,128)(2,1)}), bf16[1,1024,512]{2,1,0:T(8,128)(2,1)}) %all-gather.5.cloned.1.call-update) | async-done | bytes 1048592 | tf_op jit(solution)/shard_map/all_gather | solution.py:83
  53.8 36.8 %all-gather.7.cloned.1.call-done = bf16[1,1024,512]{2,1,0:T(8,128)(2,1)} async-done(((bf16[1,128,512]{2,1,0:T(8,128)(2,1)}), bf16[1,1024,512]{2,1,0:T(8,128)(2,1)}) %all-gather.7.cloned.1.call-update) | async-done | bytes 1048592 | tf_op jit(solution)/shard_map/all_gather | solution.py:82
  92.8 74.6 %while.39 = (s32[]{:T(128)}, f32[4,8,128]{2,1,0:T(8,128)S(1)}, f32[4,8,128]{2,1,0:T(8,128)S(1)}, s32[8]{0:T(128)}, pred[128,1024]{0,1:T(8,128)(4,1)S(1)}, /*inde...) while((s32[]{:T(128)}, f32[4,8,128]{2,1,0:T(8,128)S(1)}, ...), condition=%wide.region_6.7_spmd.clone, body=%wide.region_3.6_spmd.clone.sunk | while | flops 138432512 | bytes 5914798 | solution.py:61
  96.9 3.0 fusion.64
  106.2 3.0 fusion.64
  115.5 3.0 fusion.64
  134.2 3.0 fusion.64
  143.5 3.0 fusion.64
  162.2 3.0 fusion.64
  168.0 67.2 %while.40 = (s32[]{:T(128)}, f32[128,4,8,128]{0,3,2,1:T(8,128)}, bf16[8,128,512]{1,2,0:T(8,128)(2,1)}, s32[8]{0:T(128)}, pred[128,1024]{0,1:T(8,128)(4,1)S(1)}, ...) while((s32[]{:T(128)}, f32[128,4,8,128]{0,3,2,1:T(8,128)}, ...), condition=%wide.region_8.9_spmd.clone, body=%wide.region_7.8_spmd.clone.sunk | while | flops 272105472 | bytes 6095029 | solution.py:61
  172.2 3.6 bitcast_add_fusion.4
  180.0 4.3 bitcast_add_fusion.4
  188.5 4.3 bitcast_add_fusion.4
  197.0 4.3 bitcast_add_fusion.4
  205.5 4.3 bitcast_add_fusion.4
  214.0 4.3 bitcast_add_fusion.4
  222.5 4.3 bitcast_add_fusion.4
  230.9 4.3 bitcast_add_fusion.4
  235.3 3.7 multiply_reduce_fusion
  241.1 151.5 %while.41 = (s32[]{:T(128)}, f32[128,4,8,128]{0,3,2,1:T(8,128)}, bf16[1024,512]{1,0:T(8,128)(2,1)}, bf16[1024,512]{1,0:T(8,128)(2,1)}, bf16[8,128,512]{1,2,0:T(8...) while((s32[]{:T(128)}, f32[128,4,8,128]{0,3,2,1:T(8,128)}, ...), condition=%wide.region_11.12_spmd.clone, body=%wide.region_10.11_spmd.clone.sunk | while | flops 677380096 | bytes 33767756 | solution.py:61
  267.9 3.5 bitcast_add_fusion.5
  287.1 3.5 bitcast_add_fusion.5
  306.3 3.5 bitcast_add_fusion.5
  325.5 3.5 bitcast_add_fusion.5
  344.7 3.5 bitcast_add_fusion.5
  363.9 3.5 bitcast_add_fusion.5
  383.1 3.5 bitcast_add_fusion.5
  392.8 37.2 %reduce-scatter.13.cloned.1.call-done = bf16[128,512]{1,0:T(8,128)(2,1)} async-done(((bf16[1024,512]{1,0:T(8,128)(2,1)}), bf16[128,512]{1,0:T(8,128)(2,1)}) %reduce-scatter.13.cloned.1.call-update) | async-done | bytes 131088
  430.0 6.5 %fusion.21 = bf16[8192,512]{0,1:T(8,128)(2,1)} fusion(bf16[128,512]{1,0:T(8,128)(2,1)} %reduce-scatter.13.cloned.1.call-done, bf16[1,128,8192]{2,1,0:T(8,128)(2,1)S(1)} %copy-done), kind=kOutput, calls=%fused_computation.39 | convolution fusion | flops 1077936128 | bytes 10616832 | tf_op jit(solution)/shard_map/dot_general | solution.py:141
  436.6 98.9 %reduce-scatter.11.cloned.1.call-done = bf16[256,512]{0,1:T(8,128)(2,1)} async-done(((bf16[8192,512]{0,1:T(8,128)(2,1)}), bf16[256,512]{0,1:T(8,128)(2,1)}) %reduce-scatter.11.cloned.1.call-update) | async-done | bytes 262160 | tf_op jit(solution)/shard_map/reduce_scatter | solution.py:140
  542.2 32.2 %reduce-scatter.15.cloned.1.call-done = bf16[32,512]{1,0:T(8,128)(2,1)} async-done(((bf16[256,512]{1,0:T(8,128)(2,1)}), bf16[32,512]{1,0:T(8,128)(2,1)}) %reduce-scatter.15.cloned.1.call-update) | async-done | bytes 32784
  576.0 38.7 %reduce-scatter.9.cloned.1.call-done = bf16[128,512]{1,0:T(8,128)(2,1)} async-done(((bf16[1024,512]{1,0:T(8,128)(2,1)}), bf16[128,512]{1,0:T(8,128)(2,1)}) %reduce-scatter.9.cloned.1.call-update) | async-done | bytes 131088 | tf_op jit(solution)/shard_map/reduce_scatter | solution.py:130
  (284 shorter events, 197.1 us)
Async XLA Ops:
  7.2 422.8 %copy-start = (bf16[1,128,8192]{2,1,0:T(8,128)(2,1)S(1)}, bf16[1,128,8192]{2,1,0:T(8,128)(2,1)}, u32[]{:S(2)}) copy-start(bf16[1,128,8192]{2,1,0:T(8,128)(2,1)} %param.14) | copy-start | bytes 6291460
  7.2 44.3 %all-gather.5.cloned.1.call-start = ((), (), s32[]{:S(2)}) async-start(), calls=%async_computation.6 | async-start | bytes 1179648 | tf_op jit(solution)/shard_map/all_gather | solution.py:83
  7.9 82.6 %all-gather.7.cloned.1.call-start = ((), (), s32[]{:S(2)}) async-start(), calls=%async_computation.7 | async-start | bytes 1179648 | tf_op jit(solution)/shard_map/all_gather | solution.py:82
  8.7 421.3 %reduce-scatter.13.cloned.1.call-start = ((), (), s32[]{:S(2)}) async-start(), calls=%async_computation.8 | async-start | bytes 1179648
  241.1 6.5 %copy-start.1 = (bf16[128,4,8,128]{0,3,2,1:T(8,128)(2,1)}, bf16[128,4,8,128]{0,3,2,1:T(8,128)(2,1)S(1)}, u32[]{:S(2)}) copy-start(bf16[128,4,8,128]{0,3,2,1:T(8,128)(2,1)S(1)} %get-tuple-element.750) | copy-start | bytes 3145732 | tf_op jit(solution)/shard_map/while
  250.4 1.8 copy-start.5
  252.7 6.0 copy-start.2
  258.6 6.5 %copy-start.1 = (bf16[128,4,8,128]{0,3,2,1:T(8,128)(2,1)}, bf16[128,4,8,128]{0,3,2,1:T(8,128)(2,1)S(1)}, u32[]{:S(2)}) copy-start(bf16[128,4,8,128]{0,3,2,1:T(8,128)(2,1)S(1)} %get-tuple-element.750) | copy-start | bytes 3145732 | tf_op jit(solution)/shard_map/while
  267.9 3.5 copy-start.5
  271.8 6.0 copy-start.2
  277.8 6.5 %copy-start.1 = (bf16[128,4,8,128]{0,3,2,1:T(8,128)(2,1)}, bf16[128,4,8,128]{0,3,2,1:T(8,128)(2,1)S(1)}, u32[]{:S(2)}) copy-start(bf16[128,4,8,128]{0,3,2,1:T(8,128)(2,1)S(1)} %get-tuple-element.750) | copy-start | bytes 3145732 | tf_op jit(solution)/shard_map/while
  287.1 3.5 copy-start.5
  291.0 6.0 copy-start.2
  297.0 6.5 %copy-start.1 = (bf16[128,4,8,128]{0,3,2,1:T(8,128)(2,1)}, bf16[128,4,8,128]{0,3,2,1:T(8,128)(2,1)S(1)}, u32[]{:S(2)}) copy-start(bf16[128,4,8,128]{0,3,2,1:T(8,128)(2,1)S(1)} %get-tuple-element.750) | copy-start | bytes 3145732 | tf_op jit(solution)/shard_map/while
  306.3 3.5 copy-start.5
  310.2 6.0 copy-start.2
  316.2 6.5 %copy-start.1 = (bf16[128,4,8,128]{0,3,2,1:T(8,128)(2,1)}, bf16[128,4,8,128]{0,3,2,1:T(8,128)(2,1)S(1)}, u32[]{:S(2)}) copy-start(bf16[128,4,8,128]{0,3,2,1:T(8,128)(2,1)S(1)} %get-tuple-element.750) | copy-start | bytes 3145732 | tf_op jit(solution)/shard_map/while
  325.5 3.5 copy-start.5
  329.4 6.0 copy-start.2
  335.4 6.5 %copy-start.1 = (bf16[128,4,8,128]{0,3,2,1:T(8,128)(2,1)}, bf16[128,4,8,128]{0,3,2,1:T(8,128)(2,1)S(1)}, u32[]{:S(2)}) copy-start(bf16[128,4,8,128]{0,3,2,1:T(8,128)(2,1)S(1)} %get-tuple-element.750) | copy-start | bytes 3145732 | tf_op jit(solution)/shard_map/while
  344.7 3.5 copy-start.5
  348.6 6.0 copy-start.2
  354.6 6.5 %copy-start.1 = (bf16[128,4,8,128]{0,3,2,1:T(8,128)(2,1)}, bf16[128,4,8,128]{0,3,2,1:T(8,128)(2,1)S(1)}, u32[]{:S(2)}) copy-start(bf16[128,4,8,128]{0,3,2,1:T(8,128)(2,1)S(1)} %get-tuple-element.750) | copy-start | bytes 3145732 | tf_op jit(solution)/shard_map/while
  363.9 3.5 copy-start.5
  367.8 6.0 copy-start.2
  373.8 6.5 %copy-start.1 = (bf16[128,4,8,128]{0,3,2,1:T(8,128)(2,1)}, bf16[128,4,8,128]{0,3,2,1:T(8,128)(2,1)S(1)}, u32[]{:S(2)}) copy-start(bf16[128,4,8,128]{0,3,2,1:T(8,128)(2,1)S(1)} %get-tuple-element.750) | copy-start | bytes 3145732 | tf_op jit(solution)/shard_map/while
  383.1 3.5 copy-start.5
  387.0 5.7 copy-start.2
  392.7 142.8 %reduce-scatter.11.cloned.1.call-start = ((), (), s32[]{:S(2)}) async-start(), calls=%async_computation.5 | async-start | bytes 8650752 | tf_op jit(solution)/shard_map/reduce_scatter | solution.py:140
  436.5 101.3 %copy-start.6 = (bf16[128,4,8,128]{0,3,2,1:T(8,128)(2,1)S(1)}, bf16[128,4,8,128]{0,3,2,1:T(8,128)(2,1)}, u32[]{:S(2)}) copy-start(bf16[128,4,8,128]{0,3,2,1:T(8,128)(2,1)} %get-tuple-element.467) | copy-start | bytes 3145732
  436.5 137.9 %reduce-scatter.15.cloned.1.call-start = ((), (), s32[]{:S(2)}) async-start(), calls=%async_computation.9 | async-start | bytes 294912
  537.3 77.4 %reduce-scatter.9.cloned.1.call-start = ((), (), s32[]{:S(2)}) async-start(), calls=%async_computation.4 | async-start | bytes 1179648 | tf_op jit(solution)/shard_map/reduce_scatter | solution.py:130
  (9 other events, 9.0 us)
Sparse Core Ops, SparseCore 0:
  9.8 41.6 all-gather.4
  53.3 37.1 all-gather.6
  392.8 37.1 reduce-scatter.12
  436.6 98.7 reduce-scatter.10
  538.0 36.3 reduce-scatter.14
  577.4 37.2 reduce-scatter.8
where the time goes:
time: 625 us; the launch traced here: 622 us
  waiting for transfers between devices  279 us (45%)
  matrix products  140 us (22%)
  local copies, waits for them, and re-layouts  114 us (18%)
  loops' own time  46.6 us (7%)
  other arithmetic  27.2 us (4%)
  between operations  14.2 us (2%)
    reduce_scatter x1, waiting for transfers between devices, on_device(): lax.psum_scatter(lax.dot_general(inputs, grad_value, (((0,), (0,)), ((),...  98.9 us
    unnamed x8, waiting for transfers between devices  71.3 us
    dynamic_slice x48, local copies, waits for them, and re-layouts, run_blocks(): carry, unused = lax.scan(advance, carry, shaped + (firsts,))  55.6 us
    another operation x3, loops' own time, run_blocks(): carry, unused = lax.scan(advance, carry, shaped + (firsts,))  46.6 us
    dot_general x16, matrix products, scores_for(): jnp.einsum('qhgd,khd->hgqk', q4, k3, preferred_element_type=jnp.float32)  40.3 us
    reduce_scatter x1, waiting for transfers between devices, on_device(): lax.psum_scatter(grad_k.astype(jnp.bfloat16), 'ctx', scatter_dimension=0,...  38.7 us
    all_gather x1, waiting for transfers between devices, on_device(): lax.all_gather(key[0], 'ctx', axis=0, tiled=True)  36.8 us
    dot_general x8, matrix products, out_step(): jnp.einsum('hgqk,khd->qhgd', weights, v3, preferred_element_type=jnp.floa...  33.9 us
  transfers between devices with their start and end apart: 6, of which 6 were waited for; matrix products, arithmetic and copies ran while one was open for 3% of the time, Pallas kernels for 0%

commit v1 on v0

v1 whole, which is shorter than its diff:
```python
import functools
import math

import jax
import jax.numpy as jnp
from jax import lax
from jax.experimental import pallas as pl
from jax.experimental.pallas import tpu as pltpu
from jax.sharding import PartitionSpec as P

HEADS = 32
KV_HEADS = 4
HEAD_DIM = 128
GROUP = 8
CH = 64
NDOC = 8

NT = (((1,), (1,)), ((), ()))
NN = (((1,), (0,)), ((), ()))
TN = (((0,), (0,)), ((), ()))


def dot(a, b, dims):
    return lax.dot_general(a, b, dims, preferred_element_type=jnp.float32)


def fill_bias(lens, prefix, order, ctx, bias):
    rows = bias.shape[1]
    lane = lax.broadcasted_iota(jnp.int32, (8, rows), 1)
    place = lane
    for s in range(rows // CH):
        moved = order[0, ctx * (rows // CH) + s] * CH - s * CH
        place = jnp.where(lane >= s * CH, lane + moved, place)
    low = jnp.zeros((8, rows), jnp.int32)
    open_end = jnp.zeros((8, rows), jnp.int32)
    start = jnp.int32(0)
    for d in range(NDOC):
        hit = place >= start
        low = jnp.where(hit, start, low)
        open_end = jnp.where(hit, start + jnp.minimum(prefix[0, d], lens[0, d]), open_end)
        start = start + lens[0, d]
    high = jnp.maximum(place + 1, open_end)
    sub = lax.broadcasted_iota(jnp.int32, (8, rows), 0)

    def stretch(b, carry):
        base = order[0, b] * CH
        for i in range(CH // 8):
            at = sub + (base + i * 8)
            bias[pl.ds(pl.multiple_of(b * CH + i * 8, 8), 8), :] = jnp.where(
                (at >= low) & (at < high), 0.0, -1e30
            )
        return carry

    lax.fori_loop(0, bias.shape[0] // CH, stretch, 0)


def attention_kernel(lens, prefix, order, q, g, k, v, out, dq, dk, dv, bias, dk_sum, dv_sum, k_t, v_t):
    ctx = lax.axis_index("ctx")

    @pl.when(pl.program_id(0) == 0)
    def _():
        fill_bias(lens, prefix, order, ctx, bias)

    scale = HEAD_DIM**-0.5
    k_t[...] = k[...].T
    v_t[...] = v[...].T
    for c in range(GROUP // 2):
        cols = [slice((2 * c + i) * HEAD_DIM, (2 * c + i + 1) * HEAD_DIM) for i in range(2)]
        q2 = jnp.concatenate([q[:, s] for s in cols], 0)
        g2 = jnp.concatenate([g[:, s] for s in cols], 0)
        b = bias[...]
        t = dot(k[...], q2, NT) * (scale * math.log2(math.e)) + jnp.concatenate([b, b], 1)
        p = jnp.exp2(t - jnp.max(t, axis=0, keepdims=True))
        probs = (p * (1.0 / jnp.sum(p, axis=0, keepdims=True))).astype(jnp.bfloat16)
        out_t = dot(v_t[...], probs, NN)
        dots = dot(v[...], g2, NT)
        wide = probs.astype(jnp.float32)
        delta = jnp.sum(wide * dots, axis=0, keepdims=True)
        slopes = (wide * (dots - delta)).astype(jnp.bfloat16)
        dq_t = dot(k_t[...], slopes, NN) * scale
        dv_c = dot(probs, g2, NN)
        dk_c = dot(slopes, q2, NN)
        if c == 0:
            dv_sum[...] = dv_c
            dk_sum[...] = dk_c
        else:
            dv_sum[...] += dv_c
            dk_sum[...] += dk_c
        o2 = out_t.T.astype(jnp.bfloat16)
        d2 = dq_t.T.astype(jnp.bfloat16)
        for i, s in enumerate(cols):
            out[:, s] = o2[i * HEAD_DIM : (i + 1) * HEAD_DIM]
            dq[:, s] = d2[i * HEAD_DIM : (i + 1) * HEAD_DIM]
    dk[...] = (dk_sum[...] * scale).astype(jnp.bfloat16)
    dv[...] = dv_sum[...].astype(jnp.bfloat16)


def attention(q, g, both, lens, prefix, order):
    rows, total, kv_width = q.shape[0], both.shape[0], both.shape[1] // 2

    def block(r, c):
        return pl.BlockSpec((r, c), lambda h: (0, h))

    scalars = pl.BlockSpec(memory_space=pltpu.SMEM)
    wide, narrow = block(rows, GROUP * HEAD_DIM), block(total, HEAD_DIM)
    values = pl.BlockSpec((total, HEAD_DIM), lambda h: (0, h + KV_HEADS))
    shape = jax.ShapeDtypeStruct
    return pl.pallas_call(
        attention_kernel,
        grid=(KV_HEADS,),
        in_specs=[scalars] * 3 + [wide, wide, narrow, values],
        out_specs=[wide, wide, narrow, narrow],
        out_shape=[shape(q.shape, jnp.bfloat16)] * 2 + [shape((total, kv_width), jnp.bfloat16)] * 2,
        scratch_shapes=[
            pltpu.VMEM((total, rows), jnp.float32),
            pltpu.VMEM((total, HEAD_DIM), jnp.float32),
            pltpu.VMEM((total, HEAD_DIM), jnp.float32),
            pltpu.VMEM((HEAD_DIM, total), jnp.bfloat16),
            pltpu.VMEM((HEAD_DIM, total), jnp.bfloat16),
        ],
        compiler_params=pltpu.CompilerParams(vmem_limit_bytes=40 * 1024 * 1024),
        cost_estimate=pl.CostEstimate(
            flops=12 * HEADS * rows * total * HEAD_DIM, bytes_accessed=8 << 20, transcendentals=HEADS * rows * total
        ),
    )(lens, prefix, order, q, g, both, both)


def on_device(layer_input, query, key, value, grad_out, doc_lengths, prefix_lengths, stretch_order):
    both = lax.all_gather(jnp.concatenate([key[0], value[0]], 1), "ctx", axis=0, tiled=True)
    columns = lax.all_to_all(layer_input[0], "dp", split_axis=1, concat_axis=0, tiled=True)
    columns, stretch_order = lax.optimization_barrier((columns, stretch_order))
    out, dq, dk, dv = attention(query[0], grad_out[0], both, doc_lengths, prefix_lengths, stretch_order)
    dv_mine = lax.psum_scatter(dv, "ctx", scatter_dimension=0, tiled=True)
    dv_mine, dk = lax.optimization_barrier((dv_mine, dk))
    dv_batch = lax.all_gather(dv_mine, "dp", axis=0, tiled=True)
    parts = lax.all_to_all(dk, "ctx", split_axis=0, concat_axis=0, tiled=True)
    parts = parts.reshape(-1, dv_mine.shape[0], dk.shape[1]).astype(jnp.float32)
    grad_key = jnp.sum(parts, axis=0).astype(jnp.bfloat16)
    columns, grad_key = lax.optimization_barrier((columns, grad_key))
    part = dot(columns, dv_batch, TN).astype(jnp.bfloat16)
    weight = lax.psum_scatter(part, "ctx", scatter_dimension=0, tiled=True).astype(jnp.float32)
    return (out[None], dq[None], grad_key[None], weight)


def solution(mesh):
    rows = P("dp", "ctx", None)
    scalars = P("dp", None)
    return jax.shard_map(
        on_device,
        mesh=mesh,
        in_specs=(rows,) * 5 + (scalars,) * 3,
        out_specs=(rows, rows, rows, P(("dp", "ctx"), None)),
        check_vma=False,
    )
```

time: 625 us -> 226 us (0.36)
  waiting for transfers between devices: 279 us -> 100 us
  matrix products: 140 us -> 4.79 us
  local copies, waits for them, and re-layouts: 114 us -> 9.05 us
  blocking collectives: 0 us -> 63.2 us
  loops' own time: 46.6 us -> 0 us
  Pallas kernels: 0 us -> 31 us
  other arithmetic: 27.2 us -> 3.9 us
    dot_general x57 -> x1, matrix products: 140 us -> 4.79 us  [dot(): return lax.dot_general(a, b, dims, preferred_element_type=jnp.float32)]
    unnamed x8 -> x4, waiting for transfers between devices: 71.3 us -> 0.07 us
    reduce_scatter x2, waiting for transfers between devices: 138 us -> 74 us  [the longest x1 37.3 us: on_device(): dv_mine = lax.psum_scatter(dv, 'ctx', scatter_dimension=0, tiled=True)]
    all_to_all x0 -> x2, blocking collectives: none -> 63.2 us  [the longest x1 34.9 us: on_device(): lax.all_to_all(layer_input[0], 'dp', split_axis=1, concat_axis=0, tiled=T...]
    dynamic_slice x74 -> x0, local copies, waits for them, and re-layouts: 56.3 us -> none  [the longest x48 55.6 us: run_blocks(): carry, unused = lax.scan(advance, carry, shaped + (firsts,))]
    another operation x3 -> x0, loops' own time: 46.6 us -> none  [run_blocks(): carry, unused = lax.scan(advance, carry, shaped + (firsts,))]
    all_gather x2, waiting for transfers between devices: 69.9 us -> 26.1 us  [the longest x1 22.9 us: on_device(): dv_batch = lax.all_gather(dv_mine, 'dp', axis=0, tiled=True)]
    dynamic_update_slice x32 -> x0, local copies, waits for them, and re-layouts: 31.7 us -> none  [the longest x16 16.1 us: back_step(): grad_k = lax.dynamic_update_slice_in_dim(grad_k, key_part, first, 0)]
  transfers between devices with their start and end apart: 6 -> 4, of which waited for: 6 -> 4; matrix products, arithmetic and copies ran while one was open for 3% -> 4% of each run, Pallas kernels for 0% -> 0%
where the time goes in v1:
time: 226 us
  waiting for transfers between devices  100 us (44%)
  blocking collectives  63.2 us (28%)
  Pallas kernels  31 us (14%)
  between operations  13.8 us (6%)
  local copies, waits for them, and re-layouts  9.05 us (4%)
  matrix products  4.79 us (2%)
  other arithmetic  3.9 us (2%)
    reduce_scatter x1, waiting for transfers between devices, on_device(): dv_mine = lax.psum_scatter(dv, 'ctx', scatter_dimension=0, tiled=True)  37.3 us
    reduce_scatter x1, waiting for transfers between devices, on_device(): lax.psum_scatter(part, 'ctx', scatter_dimension=0, tiled=True)  36.6 us
    all_to_all x1, blocking collectives, on_device(): lax.all_to_all(layer_input[0], 'dp', split_axis=1, concat_axis=0, tiled=T...  34.9 us
    pallas_call x1, Pallas kernels, attention(): pl.pallas_call(attention_kernel, grid=(KV_HEADS,), in_specs=[scalars] * 3...  31 us
    all_to_all x1, blocking collectives, on_device(): parts = lax.all_to_all(dk, 'ctx', split_axis=0, concat_axis=0, tiled=True)  28.3 us
    all_gather x1, waiting for transfers between devices, on_device(): dv_batch = lax.all_gather(dv_mine, 'dp', axis=0, tiled=True)  22.9 us
    unnamed x13, local copies, waits for them, and re-layouts  4.83 us
    dot_general x1, matrix products, dot(): return lax.dot_general(a, b, dims, preferred_element_type=jnp.float32)  4.79 us
  transfers between devices with their start and end apart: 4, of which 4 were waited for; matrix products, arithmetic and copies ran while one was open for 4% of the time, Pallas kernels for 0%

profile of v1, /device:TPU:2, one launch (start us, length us, event | category | flops | bytes accessed | tf_op | source)
XLA Modules:
  0.0 226.0 jit_solution(16196720796065845464)
XLA Ops:
  7.2 0.0 all-gather.3.cloned.1.call-start
  7.2 1.7 pad_maximum_fusion
  8.9 0.0 all-gather.3.cloned.1.call-update
  8.9 0.0 reduce-scatter.3.cloned.1.call-start
  9.0 3.2 %copy.12 = bf16[1,128,8192]{1,2,0:T(8,128)(2,1)S(1)} copy(bf16[1,128,8192]{2,1,0:T(8,128)(2,1)} %param.8) | data formatting | bytes 4194304 | tf_op args[0]
  12.2 34.9 %all_to_all.28 = bf16[128,32,256]{0,2,1:T(8,128)(2,1)} all-to-all(bf16[128,32,256]{0,2,1:T(8,128)(2,1)S(1)} %bitcast.17), channel_id=1, replica_groups=mesh['ctx'=8,'dp'=32] {'dp'}, dimensions={1} | all-to-all | bytes 4194304 | tf_op jit(solution)/shard_map/all_to_all | solution.py:130
  47.1 0.0 copy-start.1
  47.1 0.0 copy-start.2
  47.1 0.0 copy-start.3
  47.1 0.0 copy-start.5
  47.1 4.2 %copy.13 = bf16[32,128,256]{2,1,0:T(8,128)(2,1)} copy(bf16[32,128,256]{1,2,0:T(8,128)(2,1)} %bitcast.16) | data formatting | bytes 4194304 | tf_op jit(solution)/shard_map/all_to_all | solution.py:130
  51.3 3.2 %all-gather.3.cloned.1.call-done.k.v = bf16[1024,1024]{1,0:T(8,128)(2,1)} async-done(((bf16[128,1024]{1,0:T(8,128)(2,1)}), bf16[1024,1024]{1,0:T(8,128)(2,1)}) %all-gather.3.cloned.1.call-update) | async-done | bytes 2097168 | tf_op jit(solution)/shard_map/all_gather | solution.py:129
  54.6 0.0 copy-done.1
  54.6 0.0 copy-done.2
  54.6 0.0 copy-done.3
  54.6 0.0 copy-done.4
  54.6 0.0 copy-done.5
  54.6 0.0 copy-start
  54.6 1.6 copy-done
  56.2 31.0 %shard_map.111 = (bf16[128,4096]{1,0:T(8,128)(2,1)}, bf16[128,4096]{1,0:T(8,128)(2,1)}, bf16[1024,512]{1,0:T(8,128)(2,1)S(1)}, bf16[1024,512]{1,0:T(8,128)(2,1)}) custom-call(s32[1,8]{1,0:T(1,128)S(1)} %copy-done.3, s32[1,8]{1,0:T(1,128)S(1)} %copy-done.4, s32[1,16]{1,0:T(1,128)S(1)} %copy-done.5, bf16[128,4096]{1,0:T(8,128)(2,1)S(1)} %bitcast.14, ...), custom_call_target="tpu_custom_call" | custom-call | flops 6442450944 | bytes 8388608 | tf_op jit(solution)/shard_map/pallas_call | solution.py:108
  87.2 0.0 reduce-scatter.3.cloned.1.call-update
  87.2 0.0 all-gather.5.cloned.1.call-start
  87.2 37.3 %reduce-scatter.3.cloned.1.call-done = bf16[128,512]{1,0:T(8,128)(2,1)} async-done(((bf16[1024,512]{1,0:T(8,128)(2,1)}), bf16[128,512]{1,0:T(8,128)(2,1)}) %reduce-scatter.3.cloned.1.call-update) | async-done | bytes 131088 | tf_op jit(solution)/shard_map/reduce_scatter | solution.py:133
  124.6 0.0 all-gather.5.cloned.1.call-update
  124.6 0.0 reduce-scatter.5.cloned.1.call-start
  124.7 28.3 %all_to_all.29 = bf16[8,128,512]{2,1,0:T(8,128)(2,1)S(1)} all-to-all(bf16[8,128,512]{2,1,0:T(8,128)(2,1)S(1)} %bitcast.13), channel_id=1, replica_groups=mesh['ctx'=8,'dp'=32] {'ctx'}, dimensions={0} | all-to-all | bytes 2097152 | tf_op jit(solution)/shard_map/all_to_all | solution.py:136
  153.0 0.8 reduce_sum.12
  153.8 22.9 %all-gather.5.cloned.1.call-done = bf16[4096,512]{1,0:T(8,128)(2,1)} async-done(((bf16[128,512]{1,0:T(8,128)(2,1)}), bf16[4096,512]{1,0:T(8,128)(2,1)}) %all-gather.5.cloned.1.call-update) | async-done | bytes 4194320 | tf_op jit(solution)/shard_map/all_gather | solution.py:135
  176.7 4.8 %convolution_convert_fusion = bf16[256,512]{1,0:T(8,128)(2,1)} fusion(bf16[4096,256]{1,0:T(8,128)(2,1)} %bitcast.18, bf16[4096,512]{1,0:T(8,128)(2,1)} %all-gather.5.cloned.1.call-done), kind=kOutput, calls=%fused_computation | convolution fusion | flops 1073872896 | bytes 6553600 | tf_op jit(solution)/shard_map/dot_general | solution.py:24
  181.5 0.0 reduce-scatter.5.cloned.1.call-update
  181.5 36.6 %reduce-scatter.5.cloned.1.call-done = bf16[32,512]{1,0:T(8,128)(2,1)} async-done(((bf16[256,512]{1,0:T(8,128)(2,1)}), bf16[32,512]{1,0:T(8,128)(2,1)}) %reduce-scatter.5.cloned.1.call-update) | async-done | bytes 32784 | tf_op jit(solution)/shard_map/reduce_scatter | solution.py:141
  218.1 1.4 convert_element_type.9
  (1 shorter events, 0.0 us)
Async XLA Ops:
  7.2 47.4 %all-gather.3.cloned.1.call-start = ((), (), s32[]{:S(2)}) async-start(), calls=%async_computation.4 | async-start | bytes 2359296 | tf_op jit(solution)/shard_map/all_gather | solution.py:129
  8.9 115.7 %reduce-scatter.3.cloned.1.call-start = ((), (), s32[]{:S(2)}) async-start(), calls=%async_computation.5 | async-start | bytes 1179648 | tf_op jit(solution)/shard_map/reduce_scatter | solution.py:133
  47.1 7.5 %copy-start.1 = (bf16[1,128,4096]{2,1,0:T(8,128)(2,1)S(1)}, bf16[1,128,4096]{2,1,0:T(8,128)(2,1)}, u32[]{:S(2)}) copy-start(bf16[1,128,4096]{2,1,0:T(8,128)(2,1)} %param.9) | copy-start | bytes 3145732
  47.1 7.5 %copy-start.2 = (bf16[1,128,4096]{2,1,0:T(8,128)(2,1)S(1)}, bf16[1,128,4096]{2,1,0:T(8,128)(2,1)}, u32[]{:S(2)}) copy-start(bf16[1,128,4096]{2,1,0:T(8,128)(2,1)} %param.12) | copy-start | bytes 3145732
  47.1 7.5 %copy-start.3 = (s32[1,8]{1,0:T(1,128)S(1)}, s32[1,8]{1,0:T(1,128)}, u32[]{:S(2)}) copy-start(s32[1,8]{1,0:T(1,128)} %lens.1) | copy-start | bytes 100
  47.1 7.5 %copy-start.4 = (s32[1,8]{1,0:T(1,128)S(1)}, s32[1,8]{1,0:T(1,128)}, u32[]{:S(2)}) copy-start(s32[1,8]{1,0:T(1,128)} %prefix.1) | copy-start | bytes 100
  47.1 7.5 %copy-start.5 = (s32[1,16]{1,0:T(1,128)S(1)}, s32[1,16]{1,0:T(1,128)}, u32[]{:S(2)}) copy-start(s32[1,16]{1,0:T(1,128)} %order) | copy-start | bytes 196
  54.6 1.6 copy-start
  87.2 89.5 %all-gather.5.cloned.1.call-start = ((), (), s32[]{:S(2)}) async-start(), calls=%async_computation.6 | async-start | bytes 4325376 | tf_op jit(solution)/shard_map/all_gather | solution.py:135
  124.6 93.5 %reduce-scatter.5.cloned.1.call-start = ((), (), s32[]{:S(2)}) async-start(), calls=%async_computation.7 | async-start | bytes 294912 | tf_op jit(solution)/shard_map/reduce_scatter | solution.py:141
Sparse Core Ops, SparseCore 0:
  10.4 44.1 all-gather.2
  87.3 37.2 reduce-scatter.2
  127.1 49.4 all-gather.4
  181.6 36.4 reduce-scatter.4

commit v2 on v1

v2 whole, which is shorter than its diff:
```python
import functools
import math

import jax
import jax.numpy as jnp
from jax import lax
from jax.experimental import pallas as pl
from jax.experimental.pallas import tpu as pltpu
from jax.sharding import PartitionSpec as P

HEADS = 32
KV_HEADS = 4
HEAD_DIM = 128
GROUP = 8
CH = 64
NDOC = 8
N_X = 4
N_Y = 4
VMEM = 56 * 1024 * 1024
DISTANCES = (0, -1, 1, -2, 2, -3, 3, 4)

NT = (((1,), (1,)), ((), ()))
NN = (((1,), (0,)), ((), ()))
TN = (((0,), (0,)), ((), ()))


def dot(a, b, dims):
    return lax.dot_general(a, b, dims, preferred_element_type=jnp.float32)


def fill_bias(lens, prefix, order, ctx, bias):
    rows = bias.shape[1]
    per = rows // CH
    n_ctx = bias.shape[0] // rows
    lane = lax.broadcasted_iota(jnp.int32, (8, rows), 1)
    place = lane
    for s in range(per):
        moved = order[0, ctx * per + s] * CH - s * CH
        place = jnp.where(lane >= s * CH, lane + moved, place)
    low = jnp.zeros((8, rows), jnp.int32)
    open_end = jnp.zeros((8, rows), jnp.int32)
    start = jnp.int32(0)
    for d in range(NDOC):
        hit = place >= start
        low = jnp.where(hit, start, low)
        open_end = jnp.where(hit, start + jnp.minimum(prefix[0, d], lens[0, d]), open_end)
        start = start + lens[0, d]
    high = jnp.maximum(place + 1, open_end)
    sub = lax.broadcasted_iota(jnp.int32, (8, rows), 0)
    for n, far in enumerate(DISTANCES):
        owner = lax.rem(ctx + far + n_ctx, n_ctx)
        for s in range(per):
            base = order[0, owner * per + s] * CH
            for i in range(CH // 8):
                at = sub + (base + i * 8)
                row = n * rows + s * CH + i * 8
                bias[row : row + 8, :] = jnp.where((at >= low) & (at < high), 0.0, -1e30)


def pair(c):
    return [slice((2 * c + i) * HEAD_DIM, (2 * c + i + 1) * HEAD_DIM) for i in range(2)]


def owners_of(n_ctx):
    ctx = lax.axis_index("ctx")
    return [lax.rem(ctx + far + n_ctx, n_ctx) for far in DISTANCES]


def probs_kernel(lens, prefix, order, q, g, *refs):
    n_ctx = len(DISTANCES)
    k_blocks = refs[:n_ctx]
    probs, dv, bias, k, total = refs[n_ctx:]
    rows = q.shape[0]

    @pl.when(pl.program_id(0) == 0)
    def _():
        fill_bias(lens, prefix, order, lax.axis_index("ctx"), bias)

    scale = HEAD_DIM**-0.5
    for n in range(n_ctx):
        k[n * rows : (n + 1) * rows] = k_blocks[n][...]
    for c in range(GROUP // 2):
        q2 = jnp.concatenate([q[:, s] for s in pair(c)], 0)
        g2 = jnp.concatenate([g[:, s] for s in pair(c)], 0)
        b = bias[...]
        t = dot(k[...], q2, NT) * (scale * math.log2(math.e)) + jnp.concatenate([b, b], 1)
        p = jnp.exp2(t - jnp.max(t, axis=0, keepdims=True))
        p = (p * (1.0 / jnp.sum(p, axis=0, keepdims=True))).astype(jnp.bfloat16)
        probs[0, :, 2 * c * HEAD_DIM : (2 * c + 2) * HEAD_DIM] = p
        dv_c = dot(p, g2, NN)
        if c == 0:
            total[...] = dv_c
        else:
            total[...] += dv_c
    for n, owner in enumerate(owners_of(n_ctx)):
        dv[owner] = total[n * rows : (n + 1) * rows].astype(jnp.bfloat16)


def grads_kernel(q, g, probs, *refs):
    n_ctx = len(DISTANCES)
    k_blocks, v_blocks = refs[:n_ctx], refs[n_ctx : 2 * n_ctx]
    out, dq, dk, v, k_t, v_t, total = refs[2 * n_ctx :]
    rows = q.shape[0]
    scale = HEAD_DIM**-0.5
    for n in range(n_ctx):
        at = slice(n * rows, (n + 1) * rows)
        v[at] = v_blocks[n][...]
        k_t[:, at] = k_blocks[n][...].T
        v_t[:, at] = v_blocks[n][...].T
    for c in range(GROUP // 2):
        q2 = jnp.concatenate([q[:, s] for s in pair(c)], 0)
        g2 = jnp.concatenate([g[:, s] for s in pair(c)], 0)
        p = probs[0, :, 2 * c * HEAD_DIM : (2 * c + 2) * HEAD_DIM]
        out_t = dot(v_t[...], p, NN)
        dots = dot(v[...], g2, NT)
        wide = p.astype(jnp.float32)
        delta = jnp.sum(wide * dots, axis=0, keepdims=True)
        slopes = (wide * (dots - delta)).astype(jnp.bfloat16)
        dq_t = dot(k_t[...], slopes, NN) * scale
        dk_c = dot(slopes, q2, NN)
        if c == 0:
            total[...] = dk_c
        else:
            total[...] += dk_c
        o2 = out_t.T.astype(jnp.bfloat16)
        d2 = dq_t.T.astype(jnp.bfloat16)
        for i, s in enumerate(pair(c)):
            out[:, s] = o2[i * HEAD_DIM : (i + 1) * HEAD_DIM]
            dq[:, s] = d2[i * HEAD_DIM : (i + 1) * HEAD_DIM]
    for n, owner in enumerate(owners_of(n_ctx)):
        dk[owner] = (total[n * rows : (n + 1) * rows] * scale).astype(jnp.bfloat16)


def specs_of(rows, n_ctx):
    wide = pl.BlockSpec((rows, GROUP * HEAD_DIM), lambda h: (0, h))
    first = pl.BlockSpec((rows, HEAD_DIM), lambda h: (0, h))
    second = pl.BlockSpec((rows, HEAD_DIM), lambda h: (0, h + KV_HEADS))
    keys, values = [first] * n_ctx, [second] * (n_ctx - 1) + [first]
    parts = pl.BlockSpec((n_ctx, rows, HEAD_DIM), lambda h: (0, 0, h))
    square = pl.BlockSpec((1, n_ctx * rows, GROUP * rows), lambda h: (h, 0, 0))
    return wide, keys, values, parts, square


def probs_and_dv(q, g, k_blocks, lens, prefix, order):
    rows, n_ctx = q.shape[0], len(k_blocks)
    kv_width, total = k_blocks[-1].shape[1], rows * n_ctx
    wide, keys, values, parts, square = specs_of(rows, n_ctx)
    shape = jax.ShapeDtypeStruct
    return pl.pallas_call(
        probs_kernel,
        grid=(KV_HEADS,),
        in_specs=[pl.BlockSpec(memory_space=pltpu.SMEM)] * 3 + [wide, wide] + keys,
        out_specs=[square, parts],
        out_shape=[
            shape((KV_HEADS, total, GROUP * rows), jnp.bfloat16),
            shape((n_ctx, rows, kv_width), jnp.bfloat16),
        ],
        scratch_shapes=[
            pltpu.VMEM((total, rows), jnp.float32),
            pltpu.VMEM((total, HEAD_DIM), jnp.bfloat16),
            pltpu.VMEM((total, HEAD_DIM), jnp.float32),
        ],
        compiler_params=pltpu.CompilerParams(vmem_limit_bytes=VMEM),
        cost_estimate=pl.CostEstimate(
            flops=4 * HEADS * rows * total * HEAD_DIM, bytes_accessed=12 << 20, transcendentals=HEADS * rows * total
        ),
    )(lens, prefix, order, q, g, *k_blocks)


def out_and_grads(q, g, probs, k_blocks, v_blocks):
    rows, n_ctx = q.shape[0], len(k_blocks)
    kv_width, total = k_blocks[-1].shape[1], rows * n_ctx
    wide, keys, values, parts, square = specs_of(rows, n_ctx)
    shape = jax.ShapeDtypeStruct
    return pl.pallas_call(
        grads_kernel,
        grid=(KV_HEADS,),
        in_specs=[wide, wide, square] + keys + values,
        out_specs=[wide, wide, parts],
        out_shape=[shape(q.shape, jnp.bfloat16)] * 2 + [shape((n_ctx, rows, kv_width), jnp.bfloat16)],
        scratch_shapes=[
            pltpu.VMEM((total, HEAD_DIM), jnp.bfloat16),
            pltpu.VMEM((HEAD_DIM, total), jnp.bfloat16),
            pltpu.VMEM((HEAD_DIM, total), jnp.bfloat16),
            pltpu.VMEM((total, HEAD_DIM), jnp.float32),
        ],
        compiler_params=pltpu.CompilerParams(vmem_limit_bytes=VMEM),
        cost_estimate=pl.CostEstimate(
            flops=8 * HEADS * rows * total * HEAD_DIM, bytes_accessed=14 << 20, transcendentals=0
        ),
    )(q, g, probs, *k_blocks, *v_blocks)


def along_ctx(a, far):
    n = lax.axis_size("ctx")
    return lax.ppermute(a, "ctx", [(i, (i + far) % n) for i in range(n)])


def place_of(i):
    return i >> 3, (i >> 1) & 3, i & 1


def index_of(y, x, core):
    return ((y % N_Y) * N_X + x % N_X) * 2 + core


def along_dp(a, dy, dx, other_core):
    pairs = []
    for i in range(lax.axis_size("dp")):
        y, x, core = place_of(i)
        pairs.append((i, index_of(y + dy, x + dx, core ^ other_core)))
    return lax.ppermute(a, "dp", pairs)


def over_x(pieces):
    return [pieces[0]] + [along_dp(pieces[d], 0, d if d < 3 else -1, 0) for d in range(1, N_X)]


def pick_kernel(where, *refs):
    half = len(refs) // 2
    for source, target in zip(refs[:half], refs[half:]):
        target[...] = source[...]


def columns_for_x(layer, y, x):
    rows, model = layer.shape
    width = model // (N_X * N_Y)

    def source(d):
        return pl.BlockSpec((rows, width), lambda j, at: (0, lax.rem(at[0] + j, N_Y) * N_X + lax.rem(at[1] + d, N_X)))

    return pl.pallas_call(
        pick_kernel,
        grid_spec=pltpu.PrefetchScalarGridSpec(
            num_scalar_prefetch=1,
            grid=(N_Y,),
            in_specs=[source(d) for d in range(N_X)],
            out_specs=[pl.BlockSpec((rows, width), lambda j, at: (0, j))] * N_X,
        ),
        out_shape=[jax.ShapeDtypeStruct((rows, model // N_X), layer.dtype)] * N_X,
        cost_estimate=pl.CostEstimate(flops=0, bytes_accessed=4 * layer.size, transcendentals=0),
    )(jnp.stack([y, x]).astype(jnp.int32), *[layer] * N_X)


def turn_kernel(where, *refs):
    mine, others = refs[2 * N_X :]
    rows = refs[0].shape[0]
    for d in range(N_X):
        at = slice(d * rows, (d + 1) * rows)
        mine[:, at] = refs[d][...].T
        others[:, at] = refs[N_X + d][...].T


def split_cores(pieces, core):
    rows, width = pieces[0].shape
    narrow = width // (2 * N_Y)
    own = pl.BlockSpec((rows, narrow), lambda j, at: (0, 2 * j + at[0]))
    other = pl.BlockSpec((rows, narrow), lambda j, at: (0, 2 * j + 1 - at[0]))
    return pl.pallas_call(
        turn_kernel,
        grid_spec=pltpu.PrefetchScalarGridSpec(
            num_scalar_prefetch=1,
            grid=(N_Y,),
            in_specs=[own] * N_X + [other] * N_X,
            out_specs=[pl.BlockSpec((narrow, N_X * rows), lambda j, at: (j, 0))] * 2,
        ),
        out_shape=[jax.ShapeDtypeStruct((width // 2, N_X * rows), pieces[0].dtype)] * 2,
        cost_estimate=pl.CostEstimate(flops=0, bytes_accessed=16 * pieces[0].size, transcendentals=0),
    )(core[None].astype(jnp.int32), *pieces, *pieces)


def on_device(layer_input, query, key, value, grad_out, doc_lengths, prefix_lengths, stretch_order):
    n_ctx = lax.axis_size("ctx")
    y, x, core = place_of(lax.axis_index("dp"))
    here = jnp.concatenate([key[0], value[0]], 1)
    half = n_ctx // 2
    width = key.shape[2]
    up, down = [here], [here]
    columns = columns_for_x(layer_input[0], y, x)
    moved = over_x(columns)
    for step in range(half - 1):
        if step == 1:
            up[1], down[1], picked = lax.optimization_barrier((up[1], down[1], columns[0]))
        up.append(along_ctx(up[-1], 1))
        down.append(along_ctx(down[-1], -1))
    far_key = along_ctx(up[-1][:, :width], 1)
    far_value = along_ctx(down[-1][:, width:], -1)
    far_key, far_value, moved[1], moved[3] = lax.optimization_barrier((far_key, far_value, moved[1], moved[3]))
    blocks = [down[far] if far > 0 else up[-far] for far in DISTANCES[:-1]]
    keys, values = blocks + [far_key], blocks + [far_value]

    q, g = query[0], grad_out[0]
    probs, dv = probs_and_dv(q, g, keys, doc_lengths, prefix_lengths, stretch_order)
    got = lax.all_to_all(dv, "ctx", split_axis=0, concat_axis=0, tiled=True)
    out, dq, dk = out_and_grads(q, g, probs, keys, values)
    moved, dk = lax.optimization_barrier(([picked] + moved[1:], dk))
    mine_t, others_t = split_cores(moved, core)
    got, mine_t, others_t = lax.optimization_barrier((got, mine_t, others_t))
    grad_value = jnp.sum(got.astype(jnp.float32), axis=0).astype(jnp.bfloat16)
    others_t = along_dp(others_t, 0, 0, 1)
    got_k = lax.all_to_all(dk, "ctx", split_axis=0, concat_axis=0, tiled=True)

    near = jnp.concatenate(over_x([grad_value] * N_X), 0)
    far = along_dp(near, 0, 0, 1)
    part = (dot(mine_t, near, NN) + dot(others_t, far, NN)).reshape(N_Y, -1, near.shape[1])
    sent = part.astype(jnp.bfloat16)
    sent, got_k = lax.optimization_barrier((sent, got_k))
    total = part[0]
    for d in range(1, N_Y):
        total = total + along_dp(sent[d], d if d < 3 else -1, 0, 0).astype(jnp.float32)
    total = total.astype(jnp.bfloat16).reshape(n_ctx, -1, near.shape[1])

    grad_key = jnp.sum(got_k.astype(jnp.float32), axis=0).astype(jnp.bfloat16)
    last = lax.all_to_all(total, "ctx", split_axis=0, concat_axis=0, tiled=True)
    weight = jnp.sum(last.astype(jnp.float32), axis=0)
    return (out[None], dq[None], grad_key[None], weight)


def solution(mesh):
    rows = P("dp", "ctx", None)
    scalars = P("dp", None)
    return jax.shard_map(
        on_device,
        mesh=mesh,
        in_specs=(rows,) * 5 + (scalars,) * 3,
        out_specs=(rows, rows, rows, P(("dp", "ctx"), None)),
        check_vma=False,
    )
```

time: 226 us -> 142 us (0.63); the launches traced: 226 us -> 139 us
  blocking collectives: 63.2 us -> 0 us
  waiting for transfers between devices: 100 us -> 50.6 us
  starting transfers between devices: 0.16 us -> 43.9 us
  between operations: 13.8 us -> 0.9 us
  local copies, waits for them, and re-layouts: 9.05 us -> 1.83 us
  Pallas kernels: 31 us -> 35.7 us
  matrix products: 4.79 us -> 2.38 us
    reduce_scatter x2 -> x0, waiting for transfers between devices: 74 us -> none  [the longest x1 37.3 us: on_device(): dv_mine = lax.psum_scatter(dv, 'ctx', scatter_dimension=0, tiled=True)]
    all_to_all x2 -> x0, blocking collectives: 63.2 us -> none  [the longest x1 34.9 us: on_device(): lax.all_to_all(layer_input[0], 'dp', split_axis=1, concat_axis=0, tiled=T...]
    ppermute x0 -> x19, starting transfers between devices: none -> 30.7 us  [the longest x8 15.8 us: along_ctx(): return lax.ppermute(a, 'ctx', [(i, (i + far) % n) for i in range(n)])]
    ppermute x0 -> x19, waiting for transfers between devices: none -> 28.4 us  [the longest x11 14.5 us: along_dp(): return lax.ppermute(a, 'dp', pairs)]
    all_gather x2 -> x0, waiting for transfers between devices: 26.1 us -> none  [the longest x1 22.9 us: on_device(): dv_batch = lax.all_gather(dv_mine, 'dp', axis=0, tiled=True)]
    all_to_all x0 -> x3, waiting for transfers between devices: none -> 22.2 us  [the longest x1 10.1 us: on_device(): last = lax.all_to_all(total, 'ctx', split_axis=0, concat_axis=0, tiled=True)]
    all_to_all x0 -> x3, starting transfers between devices: none -> 13.1 us  [the longest x1 5.4 us: on_device(): last = lax.all_to_all(total, 'ctx', split_axis=0, concat_axis=0, tiled=True)]
    pallas_call x1 -> x4, Pallas kernels: 31 us -> 35.7 us  [the longest x1 15.2 us: out_and_grads(): pl.pallas_call(grads_kernel, grid=(KV_HEADS,), in_specs=[wide, wide, squa...]
  transfers between devices with their start and end apart: 4 -> 22, of which waited for: 4 -> 15; matrix products, arithmetic and copies ran while one was open for 4% -> 3% of each run, Pallas kernels for 0% -> 17%
where the time goes in v2:
time: 142 us; the launch traced here: 139 us
  waiting for transfers between devices  50.6 us (36%)
  starting transfers between devices  43.9 us (31%)
  Pallas kernels  35.7 us (25%)
  other arithmetic  4.04 us (3%)
  matrix products  2.38 us (2%)
  local copies, waits for them, and re-layouts  1.83 us (1%)
    ppermute x8, starting transfers between devices, along_ctx(): return lax.ppermute(a, 'ctx', [(i, (i + far) % n) for i in range(n)])  15.8 us
    pallas_call x1, Pallas kernels, out_and_grads(): pl.pallas_call(grads_kernel, grid=(KV_HEADS,), in_specs=[wide, wide, squa...  15.2 us
    ppermute x11, starting transfers between devices, along_dp(): return lax.ppermute(a, 'dp', pairs)  15 us
    ppermute x11, waiting for transfers between devices, along_dp(): return lax.ppermute(a, 'dp', pairs)  14.5 us
    ppermute x8, waiting for transfers between devices, along_ctx(): return lax.ppermute(a, 'ctx', [(i, (i + far) % n) for i in range(n)])  13.9 us
    pallas_call x1, Pallas kernels, probs_and_dv(): pl.pallas_call(probs_kernel, grid=(KV_HEADS,), in_specs=[pl.BlockSpec(mem...  11.9 us
    all_to_all x1, waiting for transfers between devices, on_device(): last = lax.all_to_all(total, 'ctx', split_axis=0, concat_axis=0, tiled=True)  10.1 us
    all_to_all x1, waiting for transfers between devices, on_device(): got = lax.all_to_all(dv, 'ctx', split_axis=0, concat_axis=0, tiled=True)  6.45 us
  transfers between devices with their start and end apart: 22, of which 15 were waited for; matrix products, arithmetic and copies ran while one was open for 3% of the time, Pallas kernels for 17%

profile of v2, /device:TPU:2, one launch (start us, length us, event | category | flops | bytes accessed | tf_op | source)
XLA Modules:
  0.0 139.4 jit_solution(16149944360684664524)
XLA Ops:
  1.6 5.9 %collective-permute-start.1 = (bf16[128,1024]{1,0:T(8,128)(2,1)S(1)}, bf16[128,1024]{1,0:T(8,128)(2,1)S(1)}, u32[]{:S(2)}, u32[]{:S(2)}) collective-permute-start(bf16[128,1024]{1,0:T(8,128)(2,1)S(1)} %pad_maximum_fusion.1.refs_0_.refs_8_), channel_id=1, source_target_pairs={{0,224},{32,0},{64,32},{96,64},{128,96},{160,128},{192,160},{224,1... | collective-permute-start | bytes 786440 | tf_op jit(solution)/shard_map/ppermute | solution.py:196
  8.1 4.5 %shard_map.111 = (bf16[128,2048]{1,0:T(8,128)(2,1)}, bf16[128,2048]{1,0:T(8,128)(2,1)}, bf16[128,2048]{1,0:T(8,128)(2,1)}, bf16[128,2048]{1,0:T(8,128)(2,1)}) custom-call(s32[2]{0:T(128)} %pad_add_fusion.where, bf16[128,8192]{1,0:T(8,128)(2,1)} %bitcast.22, bf16[128,8192]{1,0:T(8,128)(2,1)} %bitcast.23, bf16[128,8192]{1,0:T(8,128)(2,1)} %bitcast.24, ...), custom_call_target="tpu_custom_call" | custom-call | bytes 4194304 | tf_op jit(solution)/shard_map/pallas_call | solution.py:232
  13.1 3.4 %collective-permute-done.refs_1_.refs_9_ = bf16[128,1024]{1,0:T(8,128)(2,1)S(1)} collective-permute-done((bf16[128,1024]{1,0:T(8,128)(2,1)S(1)}, bf16[128,1024]{1,0:T(8,128)(2,1)S(1)}, u32[]{:S(2)}, u32[]{:S(2)}) %collective-permute-start) | collective-permute-done | bytes 262176 | tf_op jit(solution)/shard_map/ppermute | solution.py:196
  16.6 3.2 %collective-permute-start.3 = (bf16[128,1024]{1,0:T(8,128)(2,1)S(1)}, bf16[128,1024]{1,0:T(8,128)(2,1)S(1)}, u32[]{:S(2)}, u32[]{:S(2)}) collective-permute-start(bf16[128,1024]{1,0:T(8,128)(2,1)S(1)} %collective-permute-done.1.refs_2_.refs_10_), channel_id=1, source_target_pairs={{0,224},{32,0},{64,32},{96,64},{128,96},{160,128},{192,160},{224,1... | collective-permute-start | bytes 786440 | tf_op jit(solution)/shard_map/ppermute | solution.py:196
  19.8 1.5 %collective-permute-start.8 = (bf16[128,2048]{1,0:T(8,128)(2,1)}, bf16[128,2048]{1,0:T(8,128)(2,1)S(1)}, u32[]{:S(2)}, u32[]{:S(2)}) collective-permute-start(bf16[128,2048]{1,0:T(8,128)(2,1)} %get-tuple-element.35), channel_id=1, source_target_pairs={{0,2},{1,3},{2,4},{3,5},{4,6},{5,7},{6,0},{7,1},{8,10},{9,11},{10,... | collective-permute-start | bytes 1572872 | tf_op jit(solution)/shard_map/ppermute | solution.py:212
  21.8 2.8 %collective-permute-done.2.refs_3_.refs_11_ = bf16[128,1024]{1,0:T(8,128)(2,1)S(1)} collective-permute-done((bf16[128,1024]{1,0:T(8,128)(2,1)S(1)}, bf16[128,1024]{1,0:T(8,128)(2,1)S(1)}, u32[]{:S(2)}, u32[]{:S(2)}) %collective-permute-start.2) | collective-permute-done | bytes 262176 | tf_op jit(solution)/shard_map/ppermute | solution.py:196
  24.6 3.2 %collective-permute-start.5 = (bf16[128,1024]{1,0:T(8,128)(2,1)S(1)}, bf16[128,1024]{1,0:T(8,128)(2,1)S(1)}, u32[]{:S(2)}, u32[]{:S(2)}) collective-permute-start(bf16[128,1024]{1,0:T(8,128)(2,1)S(1)} %collective-permute-done.3.refs_4_.refs_12_), channel_id=1, source_target_pairs={{0,224},{32,0},{64,32},{96,64},{128,96},{160,128},{192,160},{224,1... | collective-permute-start | bytes 786440 | tf_op jit(solution)/shard_map/ppermute | solution.py:196
  27.9 4.3 %collective-permute-done.4.refs_5_.refs_13_ = bf16[128,1024]{1,0:T(8,128)(2,1)S(1)} collective-permute-done((bf16[128,1024]{1,0:T(8,128)(2,1)S(1)}, bf16[128,1024]{1,0:T(8,128)(2,1)S(1)}, u32[]{:S(2)}, u32[]{:S(2)}) %collective-permute-start.4) | collective-permute-done | bytes 262176 | tf_op jit(solution)/shard_map/ppermute | solution.py:196
  32.3 3.3 %collective-permute-start.7 = (bf16[128,512]{1,0:T(8,128)(2,1)S(1)}, bf16[128,512]{1,0:T(8,128)(2,1)S(1)}, u32[]{:S(2)}, u32[]{:S(2)}) collective-permute-start(bf16[128,512]{1,0:T(8,128)(2,1)S(1)} %slice.26), channel_id=1, source_target_pairs={{0,224},{32,0},{64,32},{96,64},{128,96},{160,128},{192,160},{224,1... | collective-permute-start | bytes 393224 | tf_op jit(solution)/shard_map/ppermute | solution.py:196
  35.6 2.8 %collective-permute-done.6.refs_7_ = bf16[128,512]{1,0:T(8,128)(2,1)S(1)} collective-permute-done((bf16[128,512]{1,0:T(8,128)(2,1)S(1)}, bf16[128,512]{1,0:T(8,128)(2,1)S(1)}, u32[]{:S(2)}, u32[]{:S(2)}) %collective-permute-start.6) | collective-permute-done | bytes 131104 | tf_op jit(solution)/shard_map/ppermute | solution.py:196
  39.1 11.9 %shard_map.112 = (bf16[4,1024,1024]{2,1,0:T(8,128)(2,1)}, bf16[8,128,512]{2,1,0:T(8,128)(2,1)}) custom-call(s32[1,8]{1,0:T(1,128)} %lens.1, s32[1,8]{1,0:T(1,128)} %prefix.1, s32[1,16]{1,0:T(1,128)} %order.1, bf16[128,4096]{1,0:T(8,128)(2,1)} %bitcast.30, bf16[128,4096]{1,0:T(8,128)(2,1)} %bitcast.32, bf16[128,1024]{1,0:T(8,128)(2,1)} %copy-done.4, ...), custom_call_target="tpu_custom_call" | custom-call | flops 2147483648 | bytes 12582912 | tf_op jit(solution)/shard_map/pallas_call | solution.py:149
  51.0 4.2 %all-to-all-start = ((bf16[8,128,512]{2,1,0:T(8,128)(2,1)}), bf16[8,128,512]{2,1,0:T(8,128)(2,1)S(1)}, u32[]{:S(2)}, u32[]{:S(2)}) async-start(bf16[8,128,512]{2,1,0:T(8,128)(2,1)} %get-tuple-element.42), calls=%async_computation | async-start | bytes 2097152 | tf_op jit(solution)/shard_map/all_to_all | solution.py:294
  55.2 2.4 %collective-permute-start.10 = (bf16[128,2048]{1,0:T(8,128)(2,1)S(1)}, bf16[128,2048]{1,0:T(8,128)(2,1)S(1)}, u32[]{:S(2)}, u32[]{:S(2)}) collective-permute-start(bf16[128,2048]{1,0:T(8,128)(2,1)S(1)} %copy-done.7), channel_id=1, source_target_pairs={{0,4},{1,5},{2,6},{3,7},{4,0},{5,1},{6,2},{7,3},{8,12},{9,13},{10,... | collective-permute-start | bytes 1572872 | tf_op jit(solution)/shard_map/ppermute | solution.py:212
  57.6 15.2 %shard_map.113 = (bf16[128,4096]{1,0:T(8,128)(2,1)}, bf16[128,4096]{1,0:T(8,128)(2,1)}, bf16[8,128,512]{2,1,0:T(8,128)(2,1)}) custom-call(bf16[128,4096]{1,0:T(8,128)(2,1)} %bitcast.31, bf16[128,4096]{1,0:T(8,128)(2,1)} %bitcast.33, bf16[4,1024,1024]{2,1,0:T(8,128)(2,1)} %get-tuple-element.38.probs, bf16[128,1024]{1,0:T(8,128)(2,1)} %copy-done.4, ...), custom_call_target="tpu_custom_call" | custom-call | flops 4294967296 | bytes 14680064 | tf_op jit(solution)/shard_map/pallas_call | solution.py:175
  72.9 6.4 %all-to-all-done = bf16[8,128,512]{2,1,0:T(8,128)(2,1)S(1)} async-done(((bf16[8,128,512]{2,1,0:T(8,128)(2,1)}), bf16[8,128,512]{2,1,0:T(8,128)(2,1)S(1)}, u32[]{:S(2)}, u32[]{:S(2)}) %all-to-all-start) | async-done | bytes 1048608 | tf_op jit(solution)/shard_map/all_to_all | solution.py:294
  79.3 3.6 %all-to-all-start.1 = ((bf16[8,128,512]{2,1,0:T(8,128)(2,1)}), bf16[8,128,512]{2,1,0:T(8,128)(2,1)S(1)}, u32[]{:S(2)}, u32[]{:S(2)}) async-start(bf16[8,128,512]{2,1,0:T(8,128)(2,1)} %get-tuple-element.57), calls=%async_computation.1 | async-start | bytes 2097152 | tf_op jit(solution)/shard_map/all_to_all | solution.py:301
  82.9 4.1 %shard_map.114 = (bf16[1024,512]{1,0:T(8,128)(2,1)}, bf16[1024,512]{1,0:T(8,128)(2,1)}) custom-call(s32[1]{0:T(128)} %bitcast.9.where, bf16[128,2048]{1,0:T(8,128)(2,1)} %get-tuple-element.48.refs_0_.refs_4_, bf16[128,2048]{1,0:T(8,128)(2,1)} %copy-done, bf16[128,2048]{1,0:T(8,128)(2,1)} %copy-done.2, bf16[128,2048]{1,0:T(8,128)(2,1)} %copy-done.1, ...), custom_call_target="tpu_custom_call" | custom-call | bytes 4194304 | tf_op jit(solution)/shard_map/pallas_call | solution.py:259
  88.1 2.1 %collective-permute-start.12 = (bf16[128,512]{1,0:T(8,128)(2,1)S(1)}, bf16[128,512]{1,0:T(8,128)(2,1)S(1)}, u32[]{:S(2)}, u32[]{:S(2)}) collective-permute-start(bf16[128,512]{1,0:T(8,128)(2,1)S(1)} %reduce_sum.33), channel_id=1, source_target_pairs={{0,4},{1,5},{2,6},{3,7},{4,0},{5,1},{6,2},{7,3},{8,12},{9,13},{10,... | collective-permute-start | bytes 393224 | tf_op jit(solution)/shard_map/ppermute | solution.py:212
  90.2 2.1 %collective-permute-start.11 = (bf16[128,512]{1,0:T(8,128)(2,1)S(1)}, bf16[128,512]{1,0:T(8,128)(2,1)S(1)}, u32[]{:S(2)}, u32[]{:S(2)}) collective-permute-start(bf16[128,512]{1,0:T(8,128)(2,1)S(1)} %reduce_sum.33), channel_id=1, source_target_pairs={{0,2},{1,3},{2,4},{3,5},{4,6},{5,7},{6,0},{7,1},{8,10},{9,11},{10,... | collective-permute-start | bytes 393224 | tf_op jit(solution)/shard_map/ppermute | solution.py:212
  93.2 3.7 %collective-permute-done.12 = bf16[128,512]{1,0:T(8,128)(2,1)S(1)} collective-permute-done((bf16[128,512]{1,0:T(8,128)(2,1)S(1)}, bf16[128,512]{1,0:T(8,128)(2,1)S(1)}, u32[]{:S(2)}, u32[]{:S(2)}) %collective-permute-start.12) | collective-permute-done | bytes 131104 | tf_op jit(solution)/shard_map/ppermute | solution.py:212
  97.9 1.9 %collective-permute-done.15 = bf16[512,512]{1,0:T(8,128)(2,1)S(1)} collective-permute-done((bf16[512,512]{1,0:T(8,128)(2,1)S(1)}, bf16[512,512]{1,0:T(8,128)(2,1)S(1)}, u32[]{:S(2)}, u32[]{:S(2)}) %collective-permute-start.15) | collective-permute-done | bytes 524320 | tf_op jit(solution)/shard_map/ppermute | solution.py:212
  100.5 1.7 %fusion.3 = (bf16[1024,512]{1,0:T(8,128)(2,1)}, f32[1024,512]{1,0:T(8,128)S(1)}) fusion(f32[1024,512]{1,0:T(8,128)S(1)} %fusion.4, bf16[1024,512]{1,0:T(8,128)(2,1)S(1)} %copy-done.3, bf16[128,512]{1,0:T(8,128)(2,1)S(1)} %collective-permute-done.13, bf16[128,512]{1,0:T(8,128)(2,1)S(1)} %collective-permute-done.12, ...), kind=kOutput, calls=%fused_computation.12 | convolution fusion | flops 540016640 | bytes 6815744 | tf_op jit(solution)/shard_map/dot_general | solution.py:28
  102.2 5.7 %all-to-all-done.1 = bf16[8,128,512]{2,1,0:T(8,128)(2,1)S(1)} async-done(((bf16[8,128,512]{2,1,0:T(8,128)(2,1)}), bf16[8,128,512]{2,1,0:T(8,128)(2,1)S(1)}, u32[]{:S(2)}, u32[]{:S(2)}) %all-to-all-start.1) | async-done | bytes 1048608 | tf_op jit(solution)/shard_map/all_to_all | solution.py:301
  107.9 1.2 slice_bitcast_fusion.2
  109.1 1.7 %collective-permute-start.16 = (bf16[256,512]{1,0:T(8,128)(2,1)S(1)}, bf16[256,512]{1,0:T(8,128)(2,1)S(1)}, u32[]{:S(2)}, u32[]{:S(2)}) collective-permute-start(bf16[256,512]{1,0:T(8,128)(2,1)S(1)} %get-tuple-element.60), channel_id=1, source_target_pairs={{0,8},{1,9},{2,10},{3,11},{4,12},{5,13},{6,14},{7,15},{8,16},{9,17... | collective-permute-start | bytes 786440 | tf_op jit(solution)/shard_map/ppermute | solution.py:212
  110.7 1.7 %collective-permute-start.18 = (bf16[256,512]{1,0:T(8,128)(2,1)S(1)}, bf16[256,512]{1,0:T(8,128)(2,1)S(1)}, u32[]{:S(2)}, u32[]{:S(2)}) collective-permute-start(bf16[256,512]{1,0:T(8,128)(2,1)S(1)} %get-tuple-element.61), channel_id=1, source_target_pairs={{0,24},{1,25},{2,26},{3,27},{4,28},{5,29},{6,30},{7,31},{8,0},{9,1... | collective-permute-start | bytes 786440 | tf_op jit(solution)/shard_map/ppermute | solution.py:212
  112.4 2.0 %collective-permute-start.17 = (bf16[256,512]{1,0:T(8,128)(2,1)S(1)}, bf16[256,512]{1,0:T(8,128)(2,1)S(1)}, u32[]{:S(2)}, u32[]{:S(2)}) collective-permute-start(bf16[256,512]{1,0:T(8,128)(2,1)S(1)} %get-tuple-element.62), channel_id=1, source_target_pairs={{0,16},{1,17},{2,18},{3,19},{4,20},{5,21},{6,22},{7,23},{8,24},{9,... | collective-permute-start | bytes 786440 | tf_op jit(solution)/shard_map/ppermute | solution.py:212
  114.4 4.4 %collective-permute-done.16 = bf16[256,512]{1,0:T(8,128)(2,1)S(1)} collective-permute-done((bf16[256,512]{1,0:T(8,128)(2,1)S(1)}, bf16[256,512]{1,0:T(8,128)(2,1)S(1)}, u32[]{:S(2)}, u32[]{:S(2)}) %collective-permute-start.16) | collective-permute-done | bytes 262176 | tf_op jit(solution)/shard_map/ppermute | solution.py:212
  118.8 1.0 collective-permute-done.18
  119.8 1.8 %collective-permute-done.17 = bf16[256,512]{1,0:T(8,128)(2,1)S(1)} collective-permute-done((bf16[256,512]{1,0:T(8,128)(2,1)S(1)}, bf16[256,512]{1,0:T(8,128)(2,1)S(1)}, u32[]{:S(2)}, u32[]{:S(2)}) %collective-permute-start.17) | collective-permute-done | bytes 262176 | tf_op jit(solution)/shard_map/ppermute | solution.py:212
  122.4 5.4 %all-to-all-start.2 = ((bf16[8,32,512]{2,1,0:T(8,128)(2,1)}), bf16[8,32,512]{2,1,0:T(8,128)(2,1)S(1)}, u32[]{:S(2)}, u32[]{:S(2)}) async-start(bf16[8,32,512]{2,1,0:T(8,128)(2,1)} %bitcast.15), calls=%async_computation.2 | async-start | bytes 524288 | tf_op jit(solution)/shard_map/all_to_all | solution.py:314
  128.6 10.1 %all-to-all-done.2 = bf16[8,32,512]{2,1,0:T(8,128)(2,1)S(1)} async-done(((bf16[8,32,512]{2,1,0:T(8,128)(2,1)}), bf16[8,32,512]{2,1,0:T(8,128)(2,1)S(1)}, u32[]{:S(2)}, u32[]{:S(2)}) %all-to-all-start.2) | async-done | bytes 262176 | tf_op jit(solution)/shard_map/all_to_all | solution.py:314
  (56 shorter events, 9.3 us)
Async XLA Ops:
  1.6 11.0 %copy-start.4 = (bf16[128,1024]{1,0:T(8,128)(2,1)}, bf16[128,1024]{1,0:T(8,128)(2,1)S(1)}, u32[]{:S(2)}) copy-start(bf16[128,1024]{1,0:T(8,128)(2,1)S(1)} %pad_maximum_fusion.1.refs_0_.refs_8_) | copy-start | bytes 786436
  1.6 11.5 %collective-permute-start.1 = (bf16[128,1024]{1,0:T(8,128)(2,1)S(1)}, bf16[128,1024]{1,0:T(8,128)(2,1)S(1)}, u32[]{:S(2)}, u32[]{:S(2)}) collective-permute-start(bf16[128,1024]{1,0:T(8,128)(2,1)S(1)} %pad_maximum_fusion.1.refs_0_.refs_8_), channel_id=1, source_target_pairs={{0,224},{32,0},{64,32},{96,64},{128,96},{160,128},{192,160},{224,1... | collective-permute-start | bytes 786440 | tf_op jit(solution)/shard_map/ppermute | solution.py:196
  7.6 9.0 %collective-permute-start = (bf16[128,1024]{1,0:T(8,128)(2,1)S(1)}, bf16[128,1024]{1,0:T(8,128)(2,1)S(1)}, u32[]{:S(2)}, u32[]{:S(2)}) collective-permute-start(bf16[128,1024]{1,0:T(8,128)(2,1)S(1)} %pad_maximum_fusion.1.refs_0_.refs_8_), channel_id=1, source_target_pairs={{0,32},{32,64},{64,96},{96,128},{128,160},{160,192},{192,224},{224... | collective-permute-start | bytes 786440 | tf_op jit(solution)/shard_map/ppermute | solution.py:196
  13.1 25.3 %copy-start.8 = (bf16[128,1024]{1,0:T(8,128)(2,1)}, bf16[128,1024]{1,0:T(8,128)(2,1)S(1)}, u32[]{:S(2)}) copy-start(bf16[128,1024]{1,0:T(8,128)(2,1)S(1)} %collective-permute-done.1.refs_2_.refs_10_) | copy-start | bytes 786436
  16.5 21.9 %copy-start.9 = (bf16[128,1024]{1,0:T(8,128)(2,1)}, bf16[128,1024]{1,0:T(8,128)(2,1)S(1)}, u32[]{:S(2)}) copy-start(bf16[128,1024]{1,0:T(8,128)(2,1)S(1)} %collective-permute-done.refs_1_.refs_9_) | copy-start | bytes 786436
  16.5 8.1 %collective-permute-start.2 = (bf16[128,1024]{1,0:T(8,128)(2,1)S(1)}, bf16[128,1024]{1,0:T(8,128)(2,1)S(1)}, u32[]{:S(2)}, u32[]{:S(2)}) collective-permute-start(bf16[128,1024]{1,0:T(8,128)(2,1)S(1)} %collective-permute-done.refs_1_.refs_9_), channel_id=1, source_target_pairs={{0,32},{32,64},{64,96},{96,128},{128,160},{160,192},{192,224},{224... | collective-permute-start | bytes 786440 | tf_op jit(solution)/shard_map/ppermute | solution.py:196
  16.6 8.1 %collective-permute-start.3 = (bf16[128,1024]{1,0:T(8,128)(2,1)S(1)}, bf16[128,1024]{1,0:T(8,128)(2,1)S(1)}, u32[]{:S(2)}, u32[]{:S(2)}) collective-permute-start(bf16[128,1024]{1,0:T(8,128)(2,1)S(1)} %collective-permute-done.1.refs_2_.refs_10_), channel_id=1, source_target_pairs={{0,224},{32,0},{64,32},{96,64},{128,96},{160,128},{192,160},{224,1... | collective-permute-start | bytes 786440 | tf_op jit(solution)/shard_map/ppermute | solution.py:196
  19.8 15.8 %collective-permute-start.8 = (bf16[128,2048]{1,0:T(8,128)(2,1)}, bf16[128,2048]{1,0:T(8,128)(2,1)S(1)}, u32[]{:S(2)}, u32[]{:S(2)}) collective-permute-start(bf16[128,2048]{1,0:T(8,128)(2,1)} %get-tuple-element.35), channel_id=1, source_target_pairs={{0,2},{1,3},{2,4},{3,5},{4,6},{5,7},{6,0},{7,1},{8,10},{9,11},{10,... | collective-permute-start | bytes 1572872 | tf_op jit(solution)/shard_map/ppermute | solution.py:212
  21.3 14.4 %collective-permute-start.9 = (bf16[128,2048]{1,0:T(8,128)(2,1)}, bf16[128,2048]{1,0:T(8,128)(2,1)S(1)}, u32[]{:S(2)}, u32[]{:S(2)}) collective-permute-start(bf16[128,2048]{1,0:T(8,128)(2,1)} %get-tuple-element.36), channel_id=1, source_target_pairs={{0,6},{1,7},{2,0},{3,1},{4,2},{5,3},{6,4},{7,5},{8,14},{9,15},{10,... | collective-permute-start | bytes 1572872 | tf_op jit(solution)/shard_map/ppermute | solution.py:212
  24.6 13.9 %copy-start.10 = (bf16[128,1024]{1,0:T(8,128)(2,1)}, bf16[128,1024]{1,0:T(8,128)(2,1)S(1)}, u32[]{:S(2)}) copy-start(bf16[128,1024]{1,0:T(8,128)(2,1)S(1)} %collective-permute-done.2.refs_3_.refs_11_) | copy-start | bytes 786436
  24.6 7.6 %collective-permute-start.4 = (bf16[128,1024]{1,0:T(8,128)(2,1)S(1)}, bf16[128,1024]{1,0:T(8,128)(2,1)S(1)}, u32[]{:S(2)}, u32[]{:S(2)}) collective-permute-start(bf16[128,1024]{1,0:T(8,128)(2,1)S(1)} %collective-permute-done.2.refs_3_.refs_11_), channel_id=1, source_target_pairs={{0,32},{32,64},{64,96},{96,128},{128,160},{160,192},{192,224},{224... | collective-permute-start | bytes 786440 | tf_op jit(solution)/shard_map/ppermute | solution.py:196
  24.6 13.9 %copy-start.11 = (bf16[128,1024]{1,0:T(8,128)(2,1)}, bf16[128,1024]{1,0:T(8,128)(2,1)S(1)}, u32[]{:S(2)}) copy-start(bf16[128,1024]{1,0:T(8,128)(2,1)S(1)} %collective-permute-done.3.refs_4_.refs_12_) | copy-start | bytes 786436
  24.6 7.7 %collective-permute-start.5 = (bf16[128,1024]{1,0:T(8,128)(2,1)S(1)}, bf16[128,1024]{1,0:T(8,128)(2,1)S(1)}, u32[]{:S(2)}, u32[]{:S(2)}) collective-permute-start(bf16[128,1024]{1,0:T(8,128)(2,1)S(1)} %collective-permute-done.3.refs_4_.refs_12_), channel_id=1, source_target_pairs={{0,224},{32,0},{64,32},{96,64},{128,96},{160,128},{192,160},{224,1... | collective-permute-start | bytes 786440 | tf_op jit(solution)/shard_map/ppermute | solution.py:196
  32.2 6.3 %copy-start.5 = (bf16[128,1024]{1,0:T(8,128)(2,1)}, bf16[128,1024]{1,0:T(8,128)(2,1)S(1)}, u32[]{:S(2)}) copy-start(bf16[128,1024]{1,0:T(8,128)(2,1)S(1)} %collective-permute-done.4.refs_5_.refs_13_) | copy-start | bytes 786436
  32.2 6.3 %collective-permute-start.6 = (bf16[128,512]{1,0:T(8,128)(2,1)S(1)}, bf16[128,512]{1,0:T(8,128)(2,1)S(1)}, u32[]{:S(2)}, u32[]{:S(2)}) collective-permute-start(bf16[128,512]{1,0:T(8,128)(2,1)S(1)} %slice.25), channel_id=1, source_target_pairs={{0,32},{32,64},{64,96},{96,128},{128,160},{160,192},{192,224},{224... | collective-permute-start | bytes 393224 | tf_op jit(solution)/shard_map/ppermute | solution.py:196
  32.3 6.1 %collective-permute-start.7 = (bf16[128,512]{1,0:T(8,128)(2,1)S(1)}, bf16[128,512]{1,0:T(8,128)(2,1)S(1)}, u32[]{:S(2)}, u32[]{:S(2)}) collective-permute-start(bf16[128,512]{1,0:T(8,128)(2,1)S(1)} %slice.26), channel_id=1, source_target_pairs={{0,224},{32,0},{64,32},{96,64},{128,96},{160,128},{192,160},{224,1... | collective-permute-start | bytes 393224 | tf_op jit(solution)/shard_map/ppermute | solution.py:196
  35.6 15.4 %copy-start = (bf16[128,2048]{1,0:T(8,128)(2,1)}, bf16[128,2048]{1,0:T(8,128)(2,1)S(1)}, u32[]{:S(2)}) copy-start(bf16[128,2048]{1,0:T(8,128)(2,1)S(1)} %collective-permute-done.8.refs_1_.refs_5_) | copy-start | bytes 1572868
  35.6 15.4 %copy-start.1 = (bf16[128,2048]{1,0:T(8,128)(2,1)}, bf16[128,2048]{1,0:T(8,128)(2,1)S(1)}, u32[]{:S(2)}) copy-start(bf16[128,2048]{1,0:T(8,128)(2,1)S(1)} %collective-permute-done.9.refs_3_.refs_7_) | copy-start | bytes 1572868
  38.5 12.6 %copy-start.13 = (bf16[128,512]{1,0:T(8,128)(2,1)}, bf16[128,512]{1,0:T(8,128)(2,1)S(1)}, u32[]{:S(2)}) copy-start(bf16[128,512]{1,0:T(8,128)(2,1)S(1)} %collective-permute-done.7.refs_15_) | copy-start | bytes 393220
  51.0 28.3 %all-to-all-start = ((bf16[8,128,512]{2,1,0:T(8,128)(2,1)}), bf16[8,128,512]{2,1,0:T(8,128)(2,1)S(1)}, u32[]{:S(2)}, u32[]{:S(2)}) async-start(bf16[8,128,512]{2,1,0:T(8,128)(2,1)} %get-tuple-element.42), calls=%async_computation | async-start | bytes 2097152 | tf_op jit(solution)/shard_map/all_to_all | solution.py:294
  55.2 17.6 %collective-permute-start.10 = (bf16[128,2048]{1,0:T(8,128)(2,1)S(1)}, bf16[128,2048]{1,0:T(8,128)(2,1)S(1)}, u32[]{:S(2)}, u32[]{:S(2)}) collective-permute-start(bf16[128,2048]{1,0:T(8,128)(2,1)S(1)} %copy-done.7), channel_id=1, source_target_pairs={{0,4},{1,5},{2,6},{3,7},{4,0},{5,1},{6,2},{7,3},{8,12},{9,13},{10,... | collective-permute-start | bytes 1572872 | tf_op jit(solution)/shard_map/ppermute | solution.py:212
  72.9 10.0 %copy-start.2 = (bf16[128,2048]{1,0:T(8,128)(2,1)}, bf16[128,2048]{1,0:T(8,128)(2,1)S(1)}, u32[]{:S(2)}) copy-start(bf16[128,2048]{1,0:T(8,128)(2,1)S(1)} %collective-permute-done.10.refs_2_.refs_6_) | copy-start | bytes 1572868
  79.3 28.6 %all-to-all-start.1 = ((bf16[8,128,512]{2,1,0:T(8,128)(2,1)}), bf16[8,128,512]{2,1,0:T(8,128)(2,1)S(1)}, u32[]{:S(2)}, u32[]{:S(2)}) async-start(bf16[8,128,512]{2,1,0:T(8,128)(2,1)} %get-tuple-element.57), calls=%async_computation.1 | async-start | bytes 2097152 | tf_op jit(solution)/shard_map/all_to_all | solution.py:301
  87.0 12.8 %collective-permute-start.14 = (bf16[1024,512]{1,0:T(8,128)(2,1)}, bf16[1024,512]{1,0:T(8,128)(2,1)S(1)}, u32[]{:S(2)}, u32[]{:S(2)}) collective-permute-start(bf16[1024,512]{1,0:T(8,128)(2,1)} %get-tuple-element.56), channel_id=1, source_target_pairs={{0,1},{1,0},{2,3},{3,2},{4,5},{5,4},{6,7},{7,6},{8,9},{9,8},{10,11... | collective-permute-start | bytes 3145736 | tf_op jit(solution)/shard_map/ppermute | solution.py:212
  87.2 6.0 %collective-permute-start.13 = (bf16[128,512]{1,0:T(8,128)(2,1)S(1)}, bf16[128,512]{1,0:T(8,128)(2,1)S(1)}, u32[]{:S(2)}, u32[]{:S(2)}) collective-permute-start(bf16[128,512]{1,0:T(8,128)(2,1)S(1)} %reduce_sum.33), channel_id=1, source_target_pairs={{0,6},{1,7},{2,0},{3,1},{4,2},{5,3},{6,4},{7,5},{8,14},{9,15},{10,... | collective-permute-start | bytes 393224 | tf_op jit(solution)/shard_map/ppermute | solution.py:212
  88.1 8.8 %collective-permute-start.12 = (bf16[128,512]{1,0:T(8,128)(2,1)S(1)}, bf16[128,512]{1,0:T(8,128)(2,1)S(1)}, u32[]{:S(2)}, u32[]{:S(2)}) collective-permute-start(bf16[128,512]{1,0:T(8,128)(2,1)S(1)} %reduce_sum.33), channel_id=1, source_target_pairs={{0,4},{1,5},{2,6},{3,7},{4,0},{5,1},{6,2},{7,3},{8,12},{9,13},{10,... | collective-permute-start | bytes 393224 | tf_op jit(solution)/shard_map/ppermute | solution.py:212
  90.2 7.5 %collective-permute-start.11 = (bf16[128,512]{1,0:T(8,128)(2,1)S(1)}, bf16[128,512]{1,0:T(8,128)(2,1)S(1)}, u32[]{:S(2)}, u32[]{:S(2)}) collective-permute-start(bf16[128,512]{1,0:T(8,128)(2,1)S(1)} %reduce_sum.33), channel_id=1, source_target_pairs={{0,2},{1,3},{2,4},{3,5},{4,6},{5,7},{6,0},{7,1},{8,10},{9,11},{10,... | collective-permute-start | bytes 393224 | tf_op jit(solution)/shard_map/ppermute | solution.py:212
  97.8 2.0 %collective-permute-start.15 = (bf16[512,512]{1,0:T(8,128)(2,1)S(1)}, bf16[512,512]{1,0:T(8,128)(2,1)S(1)}, u32[]{:S(2)}, u32[]{:S(2)}) collective-permute-start(bf16[512,512]{1,0:T(8,128)(2,1)S(1)} %pad_maximum_fusion), channel_id=1, source_target_pairs={{0,1},{1,0},{2,3},{3,2},{4,5},{5,4},{6,7},{7,6},{8,9},{9,8},{10,11... | collective-permute-start | bytes 1572872 | tf_op jit(solution)/shard_map/ppermute | solution.py:212
  109.1 9.7 %collective-permute-start.16 = (bf16[256,512]{1,0:T(8,128)(2,1)S(1)}, bf16[256,512]{1,0:T(8,128)(2,1)S(1)}, u32[]{:S(2)}, u32[]{:S(2)}) collective-permute-start(bf16[256,512]{1,0:T(8,128)(2,1)S(1)} %get-tuple-element.60), channel_id=1, source_target_pairs={{0,8},{1,9},{2,10},{3,11},{4,12},{5,13},{6,14},{7,15},{8,16},{9,17... | collective-permute-start | bytes 786440 | tf_op jit(solution)/shard_map/ppermute | solution.py:212
  110.7 9.0 %collective-permute-start.18 = (bf16[256,512]{1,0:T(8,128)(2,1)S(1)}, bf16[256,512]{1,0:T(8,128)(2,1)S(1)}, u32[]{:S(2)}, u32[]{:S(2)}) collective-permute-start(bf16[256,512]{1,0:T(8,128)(2,1)S(1)} %get-tuple-element.61), channel_id=1, source_target_pairs={{0,24},{1,25},{2,26},{3,27},{4,28},{5,29},{6,30},{7,31},{8,0},{9,1... | collective-permute-start | bytes 786440 | tf_op jit(solution)/shard_map/ppermute | solution.py:212
  112.4 9.2 %collective-permute-start.17 = (bf16[256,512]{1,0:T(8,128)(2,1)S(1)}, bf16[256,512]{1,0:T(8,128)(2,1)S(1)}, u32[]{:S(2)}, u32[]{:S(2)}) collective-permute-start(bf16[256,512]{1,0:T(8,128)(2,1)S(1)} %get-tuple-element.62), channel_id=1, source_target_pairs={{0,16},{1,17},{2,18},{3,19},{4,20},{5,21},{6,22},{7,23},{8,24},{9,... | collective-permute-start | bytes 786440 | tf_op jit(solution)/shard_map/ppermute | solution.py:212
  122.4 16.3 %all-to-all-start.2 = ((bf16[8,32,512]{2,1,0:T(8,128)(2,1)}), bf16[8,32,512]{2,1,0:T(8,128)(2,1)S(1)}, u32[]{:S(2)}, u32[]{:S(2)}) async-start(bf16[8,32,512]{2,1,0:T(8,128)(2,1)} %bitcast.15), calls=%async_computation.2 | async-start | bytes 524288 | tf_op jit(solution)/shard_map/all_to_all | solution.py:314
  (4 other events, 13.8 us)

commit v3 on v2

--- a/solution.py
+++ b/solution.py
@@ -99,7 +99,8 @@
 def grads_kernel(q, g, probs, *refs):
     n_ctx = len(DISTANCES)
     k_blocks, v_blocks = refs[:n_ctx], refs[n_ctx : 2 * n_ctx]
-    out, dq, dk, v, k_t, v_t, total = refs[2 * n_ctx :]
+    out, dq = refs[2 * n_ctx : 2 * n_ctx + 2]
+    dk, (v, k_t, v_t, total) = refs[2 * n_ctx + 2 : 3 * n_ctx + 2], refs[3 * n_ctx + 2 :]
     rows = q.shape[0]
     scale = HEAD_DIM**-0.5
     for n in range(n_ctx):
@@ -127,8 +128,8 @@
         for i, s in enumerate(pair(c)):
             out[:, s] = o2[i * HEAD_DIM : (i + 1) * HEAD_DIM]
             dq[:, s] = d2[i * HEAD_DIM : (i + 1) * HEAD_DIM]
-    for n, owner in enumerate(owners_of(n_ctx)):
-        dk[owner] = (total[n * rows : (n + 1) * rows] * scale).astype(jnp.bfloat16)
+    for n in range(n_ctx):
+        dk[n][...] = (total[n * rows : (n + 1) * rows] * scale).astype(jnp.bfloat16)
 
 
 def specs_of(rows, n_ctx):
@@ -176,8 +177,8 @@
         grads_kernel,
         grid=(KV_HEADS,),
         in_specs=[wide, wide, square] + keys + values,
-        out_specs=[wide, wide, parts],
-        out_shape=[shape(q.shape, jnp.bfloat16)] * 2 + [shape((n_ctx, rows, kv_width), jnp.bfloat16)],
+        out_specs=[wide, wide] + [keys[0]] * n_ctx,
+        out_shape=[shape(q.shape, jnp.bfloat16)] * 2 + [shape((rows, kv_width), jnp.bfloat16)] * n_ctx,
         scratch_shapes=[
             pltpu.VMEM((total, HEAD_DIM), jnp.bfloat16),
             pltpu.VMEM((HEAD_DIM, total), jnp.bfloat16),
@@ -196,6 +197,10 @@
     return lax.ppermute(a, "ctx", [(i, (i + far) % n) for i in range(n)])
 
 
+def plus(a, b):
+    return (a.astype(jnp.float32) + b.astype(jnp.float32)).astype(jnp.bfloat16)
+
+
 def place_of(i):
     return i >> 3, (i >> 1) & 3, i & 1
 
@@ -216,57 +221,73 @@
     return [pieces[0]] + [along_dp(pieces[d], 0, d if d < 3 else -1, 0) for d in range(1, N_X)]
 
 
-def pick_kernel(where, *refs):
-    half = len(refs) // 2
-    for source, target in zip(refs[:half], refs[half:]):
-        target[...] = source[...]
-
-
-def columns_for_x(layer, y, x):
+def turn_kernel(where, *refs):
+    targets = refs[2 * N_X :]
+    for d in range(N_X):
+        targets[d][0] = refs[d][...].T
+        targets[d][1] = refs[N_X + d][...].T
+
+
+def columns_for_x(layer, y, x, core):
     rows, model = layer.shape
-    width = model // (N_X * N_Y)
-
-    def source(d):
-        return pl.BlockSpec((rows, width), lambda j, at: (0, lax.rem(at[0] + j, N_Y) * N_X + lax.rem(at[1] + d, N_X)))
-
-    return pl.pallas_call(
-        pick_kernel,
-        grid_spec=pltpu.PrefetchScalarGridSpec(
-            num_scalar_prefetch=1,
-            grid=(N_Y,),
-            in_specs=[source(d) for d in range(N_X)],
-            out_specs=[pl.BlockSpec((rows, width), lambda j, at: (0, j))] * N_X,
-        ),
-        out_shape=[jax.ShapeDtypeStruct((rows, model // N_X), layer.dtype)] * N_X,
-        cost_estimate=pl.CostEstimate(flops=0, bytes_accessed=4 * layer.size, transcendentals=0),
-    )(jnp.stack([y, x]).astype(jnp.int32), *[layer] * N_X)
-
-
-def turn_kernel(where, *refs):
-    mine, others = refs[2 * N_X :]
-    rows = refs[0].shape[0]
-    for d in range(N_X):
-        at = slice(d * rows, (d + 1) * rows)
-        mine[:, at] = refs[d][...].T
-        others[:, at] = refs[N_X + d][...].T
-
-
-def split_cores(pieces, core):
-    rows, width = pieces[0].shape
-    narrow = width // (2 * N_Y)
-    own = pl.BlockSpec((rows, narrow), lambda j, at: (0, 2 * j + at[0]))
-    other = pl.BlockSpec((rows, narrow), lambda j, at: (0, 2 * j + 1 - at[0]))
+    width = model // (N_X * N_Y * 2)
+
+    def place(j, at, d):
+        return (lax.rem(at[0] + j, N_Y) * N_X + lax.rem(at[1] + d, N_X)) * 2
+
+    def mine(d):
+        return pl.BlockSpec((rows, width), lambda j, at: (0, place(j, at, d) + at[2]))
+
+    def other(d):
+        return pl.BlockSpec((rows, width), lambda j, at: (0, place(j, at, d) + 1 - at[2]))
+
     return pl.pallas_call(
         turn_kernel,
         grid_spec=pltpu.PrefetchScalarGridSpec(
             num_scalar_prefetch=1,
             grid=(N_Y,),
-            in_specs=[own] * N_X + [other] * N_X,
-            out_specs=[pl.BlockSpec((narrow, N_X * rows), lambda j, at: (j, 0))] * 2,
+            in_specs=[mine(d) for d in range(N_X)] + [other(d) for d in range(N_X)],
+            out_specs=[pl.BlockSpec((2, width, rows), lambda j, at: (0, j, 0))] * N_X,
         ),
-        out_shape=[jax.ShapeDtypeStruct((width // 2, N_X * rows), pieces[0].dtype)] * 2,
-        cost_estimate=pl.CostEstimate(flops=0, bytes_accessed=16 * pieces[0].size, transcendentals=0),
-    )(core[None].astype(jnp.int32), *pieces, *pieces)
+        out_shape=[jax.ShapeDtypeStruct((2, N_Y * width, rows), layer.dtype)] * N_X,
+        cost_estimate=pl.CostEstimate(flops=0, bytes_accessed=4 * layer.size, transcendentals=0),
+    )(jnp.stack([y, x, core]).astype(jnp.int32), *[layer] * (2 * N_X))
+
+
+def weight_kernel(*refs):
+    columns, (others, last_others, near, far, own), sent = refs[:N_X], refs[N_X : N_X + 5], refs[N_X + 5 :]
+    rows = own.shape[0]
+    tokens = near.shape[0] // N_X
+    both = [
+        jnp.concatenate([near[d * tokens : (d + 1) * tokens], far[d * tokens : (d + 1) * tokens]], 0) for d in range(N_X)
+    ]
+    for j in range(N_Y):
+        at = slice(j * rows, (j + 1) * rows)
+        away = [others[0, at], others[1, at], last_others[at], others[2, at]]
+        pairs = [jnp.concatenate([columns[d][0, at], away[d]], 1) for d in range(N_X)]
+        term = sum(dot(pairs[d], both[d], NN) for d in range(N_X))
+        if j == 0:
+            own[...] = term
+        else:
+            sent[j - 1][...] = term.astype(jnp.bfloat16)
+
+
+def weight_terms(columns, others, last_others, near, far):
+    rows, width = columns[0].shape[1] // N_Y, near.shape[1]
+    shape = jax.ShapeDtypeStruct
+    halves = pl.BlockSpec((1,) + columns[0].shape[1:], lambda i: (0, 0, 0))
+    whole = [pl.BlockSpec(a.shape, lambda i, n=a.ndim: (0,) * n) for a in (others, last_others, near, far)]
+    part = pl.BlockSpec((rows, width), lambda i: (0, 0))
+    own, *sent = pl.pallas_call(
+        weight_kernel,
+        grid=(1,),
+        in_specs=[halves] * N_X + whole,
+        out_specs=[part] * N_Y,
+        out_shape=[shape((rows, width), jnp.float32)] + [shape((rows, width), jnp.bfloat16)] * (N_Y - 1),
+        compiler_params=pltpu.CompilerParams(vmem_limit_bytes=VMEM // 4),
+        cost_estimate=pl.CostEstimate(flops=0, bytes_accessed=1 << 16, transcendentals=0),
+    )(*columns, others, last_others, near, far)
+    return own, sent
 
 
 def on_device(layer_input, query, key, value, grad_out, doc_lengths, prefix_lengths, stretch_order):
@@ -276,7 +297,7 @@
     half = n_ctx // 2
     width = key.shape[2]
     up, down = [here], [here]
-    columns = columns_for_x(layer_input[0], y, x)
+    columns = columns_for_x(layer_input[0], y, x, core)
     moved = over_x(columns)
     for step in range(half - 1):
         if step == 1:
@@ -292,25 +313,35 @@
     q, g = query[0], grad_out[0]
     probs, dv = probs_and_dv(q, g, keys, doc_lengths, prefix_lengths, stretch_order)
     got = lax.all_to_all(dv, "ctx", split_axis=0, concat_axis=0, tiled=True)
-    out, dq, dk = out_and_grads(q, g, probs, keys, values)
-    moved, dk = lax.optimization_barrier(([picked] + moved[1:], dk))
-    mine_t, others_t = split_cores(moved, core)
-    got, mine_t, others_t = lax.optimization_barrier((got, mine_t, others_t))
+    moved[0] = picked
+    early = jnp.stack([moved[d][1] for d in (0, 1, 3)])
+    probs, early = lax.optimization_barrier((probs, early))
+    others = along_dp(early, 0, 0, 1)
+    out, dq, *parts = out_and_grads(q, g, probs, keys, values)
+    parts = dict(zip(DISTANCES, parts))
+    moved[2], parts[half] = lax.optimization_barrier((moved[2], parts[half]))
+    last_others = along_dp(moved[2][1], 0, 0, 1)
+
+    rising, falling = along_ctx(parts[half], 1), along_ctx(parts[1 - half], -1)
+    got, rising, falling = lax.optimization_barrier((got, rising, falling))
     grad_value = jnp.sum(got.astype(jnp.float32), axis=0).astype(jnp.bfloat16)
-    others_t = along_dp(others_t, 0, 0, 1)
-    got_k = lax.all_to_all(dk, "ctx", split_axis=0, concat_axis=0, tiled=True)
+    rising, falling = plus(rising, parts[half - 1]), plus(falling, parts[2 - half])
+    rising, falling = along_ctx(rising, 1), along_ctx(falling, -1)
 
     near = jnp.concatenate(over_x([grad_value] * N_X), 0)
+    near, rising, falling = lax.optimization_barrier((near, rising, falling))
     far = along_dp(near, 0, 0, 1)
-    part = (dot(mine_t, near, NN) + dot(others_t, far, NN)).reshape(N_Y, -1, near.shape[1])
-    sent = part.astype(jnp.bfloat16)
-    sent, got_k = lax.optimization_barrier((sent, got_k))
-    total = part[0]
+    rising, falling = plus(rising, parts[half - 2]), plus(falling, parts[3 - half])
+    rising, falling = along_ctx(rising, 1), along_ctx(falling, -1)
+    own, sent = weight_terms(moved, others, last_others, near, far)
+    total = own
     for d in range(1, N_Y):
-        total = total + along_dp(sent[d], d if d < 3 else -1, 0, 0).astype(jnp.float32)
+        total = total + along_dp(sent[d - 1], d if d < 3 else -1, 0, 0).astype(jnp.float32)
     total = total.astype(jnp.bfloat16).reshape(n_ctx, -1, near.shape[1])
-
-    grad_key = jnp.sum(got_k.astype(jnp.float32), axis=0).astype(jnp.bfloat16)
+    total, rising, falling = lax.optimization_barrier((total, rising, falling))
+    rising = along_ctx(plus(rising, parts[half - 3]), 1)
+
+    grad_key = plus(plus(rising, falling), parts[0])
     last = lax.all_to_all(total, "ctx", split_axis=0, concat_axis=0, tiled=True)
     weight = jnp.sum(last.astype(jnp.float32), axis=0)
     return (out[None], dq[None], grad_key[None], weight)

time: 142 us -> 136 us (0.958); the launches traced: 139 us -> 135 us
  waiting for transfers between devices: 50.6 us -> 36.6 us
  starting transfers between devices: 43.9 us -> 54.1 us
  other arithmetic: 4.04 us -> 9.99 us
  Pallas kernels: 35.7 us -> 33.1 us
  matrix products: 2.38 us -> 0 us
    ppermute x8 -> x15, waiting for transfers between devices: 13.9 us -> 29.2 us  [along_ctx(): return lax.ppermute(a, 'ctx', [(i, (i + far) % n) for i in range(n)])]
    ppermute x8 -> x15, starting transfers between devices: 15.8 us -> 28.4 us  [along_ctx(): return lax.ppermute(a, 'ctx', [(i, (i + far) % n) for i in range(n)])]
    all_to_all x1, waiting for transfers between devices: 10.1 us -> 0.48 us  [on_device(): last = lax.all_to_all(total, 'ctx', split_axis=0, concat_axis=0, tiled=True)]
    ppermute x11 -> x12, waiting for transfers between devices: 14.5 us -> 6.57 us  [along_dp(): return lax.ppermute(a, 'dp', pairs)]
    all_to_all x1, waiting for transfers between devices: 6.45 us -> 0.28 us  [on_device(): got = lax.all_to_all(dv, 'ctx', split_axis=0, concat_axis=0, tiled=True)]
    all_to_all x1 -> x0, waiting for transfers between devices: 5.71 us -> none  [on_device(): got_k = lax.all_to_all(dk, 'ctx', split_axis=0, concat_axis=0, tiled=True)]
    convert_element_type x0 -> x5, other arithmetic: none -> 3.78 us  [plus(): return (a.astype(jnp.float32) + b.astype(jnp.float32)).astype(jnp.bfloat16)]
    all_to_all x1 -> x0, starting transfers between devices: 3.56 us -> none  [on_device(): got_k = lax.all_to_all(dk, 'ctx', split_axis=0, concat_axis=0, tiled=True)]
  transfers between devices with their start and end apart: 22 -> 29, of which waited for: 15 -> 14; matrix products, arithmetic and copies ran while one was open for 3% -> 6% of each run, Pallas kernels for 17% -> 15%
where the time goes in v3:
time: 136 us; the launch traced here: 135 us
  starting transfers between devices  54.1 us (40%)
  waiting for transfers between devices  36.6 us (27%)
  Pallas kernels  33.1 us (24%)
  other arithmetic  9.99 us (7%)
    ppermute x15, waiting for transfers between devices, along_ctx(): return lax.ppermute(a, 'ctx', [(i, (i + far) % n) for i in range(n)])  29.2 us
    ppermute x15, starting transfers between devices, along_ctx(): return lax.ppermute(a, 'ctx', [(i, (i + far) % n) for i in range(n)])  28.4 us
    ppermute x12, starting transfers between devices, along_dp(): return lax.ppermute(a, 'dp', pairs)  16 us
    pallas_call x1, Pallas kernels, out_and_grads(): pl.pallas_call(grads_kernel, grid=(KV_HEADS,), in_specs=[wide, wide, squa...  15.2 us
    pallas_call x1, Pallas kernels, probs_and_dv(): pl.pallas_call(probs_kernel, grid=(KV_HEADS,), in_specs=[pl.BlockSpec(mem...  11.8 us
    ppermute x12, waiting for transfers between devices, along_dp(): return lax.ppermute(a, 'dp', pairs)  6.57 us
    all_to_all x1, starting transfers between devices, on_device(): last = lax.all_to_all(total, 'ctx', split_axis=0, concat_axis=0, tiled=True)  5.39 us
    pallas_call x1, Pallas kernels, columns_for_x(): pl.pallas_call(turn_kernel, grid_spec=pltpu.PrefetchScalarGridSpec(num_sc...  4.82 us
  transfers between devices with their start and end apart: 29, of which 14 were waited for; matrix products, arithmetic and copies ran while one was open for 6% of the time, Pallas kernels for 15%

profile of v3, /device:TPU:2, one launch (start us, length us, event | category | flops | bytes accessed | tf_op | source)
XLA Modules:
  0.0 135.4 jit_solution(5993801104592934339)
XLA Ops:
  1.6 5.9 %collective-permute-start.1 = (bf16[128,1024]{1,0:T(8,128)(2,1)S(1)}, bf16[128,1024]{1,0:T(8,128)(2,1)S(1)}, u32[]{:S(2)}, u32[]{:S(2)}) collective-permute-start(bf16[128,1024]{1,0:T(8,128)(2,1)S(1)} %pad_maximum_fusion.2.refs_0_.refs_8_), channel_id=1, source_target_pairs={{0,224},{32,0},{64,32},{96,64},{128,96},{160,128},{192,160},{224,1... | collective-permute-start | bytes 786440 | tf_op jit(solution)/shard_map/ppermute | solution.py:197
  8.2 4.8 %shard_map.111 = (bf16[2,1024,128]{2,1,0:T(8,128)(2,1)}, bf16[2,1024,128]{2,1,0:T(8,128)(2,1)}, bf16[2,1024,128]{2,1,0:T(8,128)(2,1)}, bf16[2,1024,128]{2,1,0:T(8,128)(2,1)}) custom-call(s32[3]{0:T(128)} %pad_add_fusion.where, bf16[128,8192]{1,0:T(8,128)(2,1)} %bitcast.15, bf16[128,8192]{1,0:T(8,128)(2,1)} %bitcast.16, bf16[128,8192]{1,0:T(8,128)(2,1)} %bitcast.17, ...), custom_call_target="tpu_custom_call" | custom-call | bytes 4194304 | tf_op jit(solution)/shard_map/pallas_call | solution.py:244
  13.1 3.4 %collective-permute-done.refs_1_.refs_9_ = bf16[128,1024]{1,0:T(8,128)(2,1)S(1)} collective-permute-done((bf16[128,1024]{1,0:T(8,128)(2,1)S(1)}, bf16[128,1024]{1,0:T(8,128)(2,1)S(1)}, u32[]{:S(2)}, u32[]{:S(2)}) %collective-permute-start) | collective-permute-done | bytes 262176 | tf_op jit(solution)/shard_map/ppermute | solution.py:197
  16.6 3.2 %collective-permute-start.3 = (bf16[128,1024]{1,0:T(8,128)(2,1)S(1)}, bf16[128,1024]{1,0:T(8,128)(2,1)S(1)}, u32[]{:S(2)}, u32[]{:S(2)}) collective-permute-start(bf16[128,1024]{1,0:T(8,128)(2,1)S(1)} %collective-permute-done.1.refs_2_.refs_10_), channel_id=1, source_target_pairs={{0,224},{32,0},{64,32},{96,64},{128,96},{160,128},{192,160},{224,1... | collective-permute-start | bytes 786440 | tf_op jit(solution)/shard_map/ppermute | solution.py:197
  19.8 1.5 %collective-permute-start.8 = (bf16[2,1024,128]{2,1,0:T(8,128)(2,1)}, bf16[2,1024,128]{2,1,0:T(8,128)(2,1)S(1)}, u32[]{:S(2)}, u32[]{:S(2)}) collective-permute-start(bf16[2,1024,128]{2,1,0:T(8,128)(2,1)} %get-tuple-element.47), channel_id=1, source_target_pairs={{0,2},{1,3},{2,4},{3,5},{4,6},{5,7},{6,0},{7,1},{8,10},{9,11},{10,... | collective-permute-start | bytes 1572872 | tf_op jit(solution)/shard_map/ppermute | solution.py:217
  21.8 2.8 %collective-permute-done.2.refs_3_.refs_11_ = bf16[128,1024]{1,0:T(8,128)(2,1)S(1)} collective-permute-done((bf16[128,1024]{1,0:T(8,128)(2,1)S(1)}, bf16[128,1024]{1,0:T(8,128)(2,1)S(1)}, u32[]{:S(2)}, u32[]{:S(2)}) %collective-permute-start.2) | collective-permute-done | bytes 262176 | tf_op jit(solution)/shard_map/ppermute | solution.py:197
  24.6 3.2 %collective-permute-start.5 = (bf16[128,1024]{1,0:T(8,128)(2,1)S(1)}, bf16[128,1024]{1,0:T(8,128)(2,1)S(1)}, u32[]{:S(2)}, u32[]{:S(2)}) collective-permute-start(bf16[128,1024]{1,0:T(8,128)(2,1)S(1)} %collective-permute-done.3.refs_4_.refs_12_), channel_id=1, source_target_pairs={{0,224},{32,0},{64,32},{96,64},{128,96},{160,128},{192,160},{224,1... | collective-permute-start | bytes 786440 | tf_op jit(solution)/shard_map/ppermute | solution.py:197
  27.9 4.3 %collective-permute-done.4.refs_5_.refs_13_ = bf16[128,1024]{1,0:T(8,128)(2,1)S(1)} collective-permute-done((bf16[128,1024]{1,0:T(8,128)(2,1)S(1)}, bf16[128,1024]{1,0:T(8,128)(2,1)S(1)}, u32[]{:S(2)}, u32[]{:S(2)}) %collective-permute-start.4) | collective-permute-done | bytes 262176 | tf_op jit(solution)/shard_map/ppermute | solution.py:197
  32.3 3.3 %collective-permute-start.7 = (bf16[128,512]{1,0:T(8,128)(2,1)S(1)}, bf16[128,512]{1,0:T(8,128)(2,1)S(1)}, u32[]{:S(2)}, u32[]{:S(2)}) collective-permute-start(bf16[128,512]{1,0:T(8,128)(2,1)S(1)} %slice.25), channel_id=1, source_target_pairs={{0,224},{32,0},{64,32},{96,64},{128,96},{160,128},{192,160},{224,1... | collective-permute-start | bytes 393224 | tf_op jit(solution)/shard_map/ppermute | solution.py:197
  35.6 2.8 %collective-permute-done.6.refs_7_ = bf16[128,512]{1,0:T(8,128)(2,1)S(1)} collective-permute-done((bf16[128,512]{1,0:T(8,128)(2,1)S(1)}, bf16[128,512]{1,0:T(8,128)(2,1)S(1)}, u32[]{:S(2)}, u32[]{:S(2)}) %collective-permute-start.6) | collective-permute-done | bytes 131104 | tf_op jit(solution)/shard_map/ppermute | solution.py:197
  39.1 11.8 %shard_map.112 = (bf16[4,1024,1024]{2,1,0:T(8,128)(2,1)}, bf16[8,128,512]{2,1,0:T(8,128)(2,1)}) custom-call(s32[1,8]{1,0:T(1,128)} %lens.1, s32[1,8]{1,0:T(1,128)} %prefix.1, s32[1,16]{1,0:T(1,128)} %order.1, bf16[128,4096]{1,0:T(8,128)(2,1)} %bitcast.25, bf16[128,4096]{1,0:T(8,128)(2,1)} %bitcast.27, bf16[128,1024]{1,0:T(8,128)(2,1)} %copy-done.1, ...), custom_call_target="tpu_custom_call" | custom-call | flops 2147483648 | bytes 12582912 | tf_op jit(solution)/shard_map/pallas_call | solution.py:150
  51.0 4.3 %all-to-all-start = ((bf16[8,128,512]{2,1,0:T(8,128)(2,1)}), bf16[8,128,512]{2,1,0:T(8,128)(2,1)}, u32[]{:S(2)}, u32[]{:S(2)}) async-start(bf16[8,128,512]{2,1,0:T(8,128)(2,1)} %get-tuple-element.62), calls=%async_computation | async-start | bytes 2097152 | tf_op jit(solution)/shard_map/all_to_all | solution.py:315
  55.3 2.4 %collective-permute-start.10 = (bf16[2,1024,128]{2,1,0:T(8,128)(2,1)}, bf16[2,1024,128]{2,1,0:T(8,128)(2,1)S(1)}, u32[]{:S(2)}, u32[]{:S(2)}) collective-permute-start(bf16[2,1024,128]{2,1,0:T(8,128)(2,1)} %get-tuple-element.58), channel_id=1, source_target_pairs={{0,4},{1,5},{2,6},{3,7},{4,0},{5,1},{6,2},{7,3},{8,12},{9,13},{10,... | collective-permute-start | bytes 1572872 | tf_op jit(solution)/shard_map/ppermute | solution.py:217
  58.7 15.2 %shard_map.113 = (bf16[128,4096]{1,0:T(8,128)(2,1)}, bf16[128,4096]{1,0:T(8,128)(2,1)}, bf16[128,512]{1,0:T(8,128)(2,1)}, bf16[128,512]{1,0:T(8,128)(2,1)}, bf16...) custom-call(bf16[128,4096]{1,0:T(8,128)(2,1)} %bitcast.26, ...), custom_call_target="tpu_custom_call" | custom-call | flops 4294967296 | bytes 14680064 | tf_op jit(solution)/shard_map/pallas_call | solution.py:176
  73.9 1.7 %collective-permute-start.13 = (bf16[128,512]{1,0:T(8,128)(2,1)}, bf16[128,512]{1,0:T(8,128)(2,1)S(1)}, u32[]{:S(2)}, u32[]{:S(2)}) collective-permute-start(bf16[128,512]{1,0:T(8,128)(2,1)} %get-tuple-element.63), channel_id=1, source_target_pairs={{0,32},{32,64},{64,96},{96,128},{128,160},{160,192},{192,224},{224... | collective-permute-start | bytes 393224 | tf_op jit(solution)/shard_map/ppermute | solution.py:197
  75.6 1.6 %collective-permute-start.14 = (bf16[128,512]{1,0:T(8,128)(2,1)}, bf16[128,512]{1,0:T(8,128)(2,1)S(1)}, u32[]{:S(2)}, u32[]{:S(2)}) collective-permute-start(bf16[128,512]{1,0:T(8,128)(2,1)} %get-tuple-element.64), channel_id=1, source_target_pairs={{0,224},{32,0},{64,32},{96,64},{128,96},{160,128},{192,160},{224,1... | collective-permute-start | bytes 393224 | tf_op jit(solution)/shard_map/ppermute | solution.py:197
  77.2 3.9 %collective-permute-done.13 = bf16[128,512]{1,0:T(8,128)(2,1)S(1)} collective-permute-done((bf16[128,512]{1,0:T(8,128)(2,1)}, bf16[128,512]{1,0:T(8,128)(2,1)S(1)}, u32[]{:S(2)}, u32[]{:S(2)}) %collective-permute-start.13) | collective-permute-done | bytes 131104 | tf_op jit(solution)/shard_map/ppermute | solution.py:197
  81.4 1.4 %reduce_sum.21 = bf16[128,512]{1,0:T(8,128)(2,1)S(1)} reduce(bf16[8,128,512]{2,1,0:T(8,128)(2,1)} %all-to-all-done, bf16[]{:T(256)} %constant.10.clone.1), dimensions={0}, to_apply=%region_0.0 | reduce | flops 458752 | bytes 1179650 | tf_op jit(solution)/shard_map/reduce_sum | solution.py:327
  83.9 1.9 %collective-permute-start.16 = (bf16[128,512]{1,0:T(8,128)(2,1)S(1)}, bf16[128,512]{1,0:T(8,128)(2,1)S(1)}, u32[]{:S(2)}, u32[]{:S(2)}) collective-permute-start(bf16[128,512]{1,0:T(8,128)(2,1)S(1)} %reduce_sum.21), channel_id=1, source_target_pairs={{0,4},{1,5},{2,6},{3,7},{4,0},{5,1},{6,2},{7,3},{8,12},{9,13},{10,... | collective-permute-start | bytes 393224 | tf_op jit(solution)/shard_map/ppermute | solution.py:217
  85.8 2.1 %collective-permute-start.15 = (bf16[128,512]{1,0:T(8,128)(2,1)S(1)}, bf16[128,512]{1,0:T(8,128)(2,1)S(1)}, u32[]{:S(2)}, u32[]{:S(2)}) collective-permute-start(bf16[128,512]{1,0:T(8,128)(2,1)S(1)} %reduce_sum.21), channel_id=1, source_target_pairs={{0,2},{1,3},{2,4},{3,5},{4,6},{5,7},{6,0},{7,1},{8,10},{9,11},{10,... | collective-permute-start | bytes 393224 | tf_op jit(solution)/shard_map/ppermute | solution.py:217
  90.3 2.9 %collective-permute-start.19 = (bf16[128,512]{1,0:T(8,128)(2,1)S(1)}, bf16[128,512]{1,0:T(8,128)(2,1)S(1)}, u32[]{:S(2)}, u32[]{:S(2)}) collective-permute-start(bf16[128,512]{1,0:T(8,128)(2,1)S(1)} %add_convert_fusion.6), channel_id=1, source_target_pairs={{0,224},{32,0},{64,32},{96,64},{128,96},{160,128},{192,160},{224,1... | collective-permute-start | bytes 393224 | tf_op jit(solution)/shard_map/ppermute | solution.py:197
  93.2 1.9 %collective-permute-done.18 = bf16[128,512]{1,0:T(8,128)(2,1)S(1)} collective-permute-done((bf16[128,512]{1,0:T(8,128)(2,1)S(1)}, bf16[128,512]{1,0:T(8,128)(2,1)S(1)}, u32[]{:S(2)}, u32[]{:S(2)}) %collective-permute-start.18) | collective-permute-done | bytes 131104 | tf_op jit(solution)/shard_map/ppermute | solution.py:197
  96.3 1.7 %collective-permute-done.12.refs_5_ = bf16[1024,128]{1,0:T(8,128)(2,1)S(1)} collective-permute-done((bf16[1024,128]{1,0:T(8,128)(2,1)S(1)}, bf16[1024,128]{1,0:T(8,128)(2,1)S(1)}, u32[]{:S(2)}, u32[]{:S(2)}) %collective-permute-start.12) | collective-permute-done | bytes 262176 | tf_op jit(solution)/shard_map/ppermute | solution.py:217
  98.0 1.2 shard_map.114
  99.2 1.7 %collective-permute-start.21 = (bf16[256,512]{1,0:T(8,128)(2,1)S(1)}, bf16[256,512]{1,0:T(8,128)(2,1)S(1)}, u32[]{:S(2)}, u32[]{:S(2)}) collective-permute-start(bf16[256,512]{1,0:T(8,128)(2,1)S(1)} %get-tuple-element.72), channel_id=1, source_target_pairs={{0,8},{1,9},{2,10},{3,11},{4,12},{5,13},{6,14},{7,15},{8,16},{9,17... | collective-permute-start | bytes 786440 | tf_op jit(solution)/shard_map/ppermute | solution.py:217
  100.9 2.9 %collective-permute-start.22 = (bf16[256,512]{1,0:T(8,128)(2,1)S(1)}, bf16[256,512]{1,0:T(8,128)(2,1)S(1)}, u32[]{:S(2)}, u32[]{:S(2)}) collective-permute-start(bf16[256,512]{1,0:T(8,128)(2,1)S(1)} %get-tuple-element.73), channel_id=1, source_target_pairs={{0,16},{1,17},{2,18},{3,19},{4,20},{5,21},{6,22},{7,23},{8,24},{9,... | collective-permute-start | bytes 786440 | tf_op jit(solution)/shard_map/ppermute | solution.py:217
  103.8 1.3 collective-permute-start.23
  106.1 3.7 %collective-permute-start.25 = (bf16[128,512]{1,0:T(8,128)(2,1)S(1)}, bf16[128,512]{1,0:T(8,128)(2,1)S(1)}, u32[]{:S(2)}, u32[]{:S(2)}) collective-permute-start(bf16[128,512]{1,0:T(8,128)(2,1)S(1)} %add_convert_fusion.4), channel_id=1, source_target_pairs={{0,224},{32,0},{64,32},{96,64},{128,96},{160,128},{192,160},{224,1... | collective-permute-start | bytes 393224 | tf_op jit(solution)/shard_map/ppermute | solution.py:197
  110.9 4.9 %collective-permute-done.22 = bf16[256,512]{1,0:T(8,128)(2,1)S(1)} collective-permute-done((bf16[256,512]{1,0:T(8,128)(2,1)S(1)}, bf16[256,512]{1,0:T(8,128)(2,1)S(1)}, u32[]{:S(2)}, u32[]{:S(2)}) %collective-permute-start.22) | collective-permute-done | bytes 262176 | tf_op jit(solution)/shard_map/ppermute | solution.py:217
  117.0 5.4 %all-to-all-start.1 = ((bf16[8,32,512]{2,1,0:T(8,128)(2,1)}), bf16[8,32,512]{2,1,0:T(8,128)(2,1)S(1)}, u32[]{:S(2)}, u32[]{:S(2)}) async-start(bf16[8,32,512]{2,1,0:T(8,128)(2,1)} %bitcast.11), calls=%async_computation.1 | async-start | bytes 524288 | tf_op jit(solution)/shard_map/all_to_all | solution.py:345
  122.5 2.1 %collective-permute-start.26 = (bf16[128,512]{1,0:T(8,128)(2,1)S(1)}, bf16[128,512]{1,0:T(8,128)(2,1)S(1)}, u32[]{:S(2)}, u32[]{:S(2)}) collective-permute-start(bf16[128,512]{1,0:T(8,128)(2,1)S(1)} %add_convert_fusion.3), channel_id=1, source_target_pairs={{0,32},{32,64},{64,96},{96,128},{128,160},{160,192},{192,224},{224... | collective-permute-start | bytes 393224 | tf_op jit(solution)/shard_map/ppermute | solution.py:197
  124.5 9.0 %collective-permute-done.26 = bf16[128,512]{1,0:T(8,128)(2,1)S(1)} collective-permute-done((bf16[128,512]{1,0:T(8,128)(2,1)S(1)}, bf16[128,512]{1,0:T(8,128)(2,1)S(1)}, u32[]{:S(2)}, u32[]{:S(2)}) %collective-permute-start.26) | collective-permute-done | bytes 131104 | tf_op jit(solution)/shard_map/ppermute | solution.py:197
  (73 shorter events, 14.3 us)
Async XLA Ops:
  1.6 11.5 %collective-permute-start.1 = (bf16[128,1024]{1,0:T(8,128)(2,1)S(1)}, bf16[128,1024]{1,0:T(8,128)(2,1)S(1)}, u32[]{:S(2)}, u32[]{:S(2)}) collective-permute-start(bf16[128,1024]{1,0:T(8,128)(2,1)S(1)} %pad_maximum_fusion.2.refs_0_.refs_8_), channel_id=1, source_target_pairs={{0,224},{32,0},{64,32},{96,64},{128,96},{160,128},{192,160},{224,1... | collective-permute-start | bytes 786440 | tf_op jit(solution)/shard_map/ppermute | solution.py:197
  7.6 9.0 %collective-permute-start = (bf16[128,1024]{1,0:T(8,128)(2,1)S(1)}, bf16[128,1024]{1,0:T(8,128)(2,1)S(1)}, u32[]{:S(2)}, u32[]{:S(2)}) collective-permute-start(bf16[128,1024]{1,0:T(8,128)(2,1)S(1)} %pad_maximum_fusion.2.refs_0_.refs_8_), channel_id=1, source_target_pairs={{0,32},{32,64},{64,96},{96,128},{128,160},{160,192},{192,224},{224... | collective-permute-start | bytes 786440 | tf_op jit(solution)/shard_map/ppermute | solution.py:197
  13.0 44.6 %copy-start = (bf16[2,1024,128]{2,1,0:T(8,128)(2,1)S(1)}, bf16[2,1024,128]{2,1,0:T(8,128)(2,1)}, u32[]{:S(2)}) copy-start(bf16[2,1024,128]{2,1,0:T(8,128)(2,1)} %get-tuple-element.51.refs_0_) | copy-start | bytes 1572868
  16.5 8.1 %collective-permute-start.2 = (bf16[128,1024]{1,0:T(8,128)(2,1)S(1)}, bf16[128,1024]{1,0:T(8,128)(2,1)S(1)}, u32[]{:S(2)}, u32[]{:S(2)}) collective-permute-start(bf16[128,1024]{1,0:T(8,128)(2,1)S(1)} %collective-permute-done.refs_1_.refs_9_), channel_id=1, source_target_pairs={{0,32},{32,64},{64,96},{96,128},{128,160},{160,192},{192,224},{224... | collective-permute-start | bytes 786440 | tf_op jit(solution)/shard_map/ppermute | solution.py:197
  16.6 8.1 %collective-permute-start.3 = (bf16[128,1024]{1,0:T(8,128)(2,1)S(1)}, bf16[128,1024]{1,0:T(8,128)(2,1)S(1)}, u32[]{:S(2)}, u32[]{:S(2)}) collective-permute-start(bf16[128,1024]{1,0:T(8,128)(2,1)S(1)} %collective-permute-done.1.refs_2_.refs_10_), channel_id=1, source_target_pairs={{0,224},{32,0},{64,32},{96,64},{128,96},{160,128},{192,160},{224,1... | collective-permute-start | bytes 786440 | tf_op jit(solution)/shard_map/ppermute | solution.py:197
  19.8 15.8 %collective-permute-start.8 = (bf16[2,1024,128]{2,1,0:T(8,128)(2,1)}, bf16[2,1024,128]{2,1,0:T(8,128)(2,1)S(1)}, u32[]{:S(2)}, u32[]{:S(2)}) collective-permute-start(bf16[2,1024,128]{2,1,0:T(8,128)(2,1)} %get-tuple-element.47), channel_id=1, source_target_pairs={{0,2},{1,3},{2,4},{3,5},{4,6},{5,7},{6,0},{7,1},{8,10},{9,11},{10,... | collective-permute-start | bytes 1572872 | tf_op jit(solution)/shard_map/ppermute | solution.py:217
  21.3 14.4 %collective-permute-start.9 = (bf16[2,1024,128]{2,1,0:T(8,128)(2,1)}, bf16[2,1024,128]{2,1,0:T(8,128)(2,1)S(1)}, u32[]{:S(2)}, u32[]{:S(2)}) collective-permute-start(bf16[2,1024,128]{2,1,0:T(8,128)(2,1)} %get-tuple-element.48), channel_id=1, source_target_pairs={{0,6},{1,7},{2,0},{3,1},{4,2},{5,3},{6,4},{7,5},{8,14},{9,15},{10,... | collective-permute-start | bytes 1572872 | tf_op jit(solution)/shard_map/ppermute | solution.py:217
  24.6 7.6 %collective-permute-start.4 = (bf16[128,1024]{1,0:T(8,128)(2,1)S(1)}, bf16[128,1024]{1,0:T(8,128)(2,1)S(1)}, u32[]{:S(2)}, u32[]{:S(2)}) collective-permute-start(bf16[128,1024]{1,0:T(8,128)(2,1)S(1)} %collective-permute-done.2.refs_3_.refs_11_), channel_id=1, source_target_pairs={{0,32},{32,64},{64,96},{96,128},{128,160},{160,192},{192,224},{224... | collective-permute-start | bytes 786440 | tf_op jit(solution)/shard_map/ppermute | solution.py:197
  24.6 7.7 %collective-permute-start.5 = (bf16[128,1024]{1,0:T(8,128)(2,1)S(1)}, bf16[128,1024]{1,0:T(8,128)(2,1)S(1)}, u32[]{:S(2)}, u32[]{:S(2)}) collective-permute-start(bf16[128,1024]{1,0:T(8,128)(2,1)S(1)} %collective-permute-done.3.refs_4_.refs_12_), channel_id=1, source_target_pairs={{0,224},{32,0},{64,32},{96,64},{128,96},{160,128},{192,160},{224,1... | collective-permute-start | bytes 786440 | tf_op jit(solution)/shard_map/ppermute | solution.py:197
  32.2 6.3 %collective-permute-start.6 = (bf16[128,512]{1,0:T(8,128)(2,1)S(1)}, bf16[128,512]{1,0:T(8,128)(2,1)S(1)}, u32[]{:S(2)}, u32[]{:S(2)}) collective-permute-start(bf16[128,512]{1,0:T(8,128)(2,1)S(1)} %slice.24), channel_id=1, source_target_pairs={{0,32},{32,64},{64,96},{96,128},{128,160},{160,192},{192,224},{224... | collective-permute-start | bytes 393224 | tf_op jit(solution)/shard_map/ppermute | solution.py:197
  32.3 6.1 %collective-permute-start.7 = (bf16[128,512]{1,0:T(8,128)(2,1)S(1)}, bf16[128,512]{1,0:T(8,128)(2,1)S(1)}, u32[]{:S(2)}, u32[]{:S(2)}) collective-permute-start(bf16[128,512]{1,0:T(8,128)(2,1)S(1)} %slice.25), channel_id=1, source_target_pairs={{0,224},{32,0},{64,32},{96,64},{128,96},{160,128},{192,160},{224,1... | collective-permute-start | bytes 393224 | tf_op jit(solution)/shard_map/ppermute | solution.py:197
  51.0 30.4 %all-to-all-start = ((bf16[8,128,512]{2,1,0:T(8,128)(2,1)}), bf16[8,128,512]{2,1,0:T(8,128)(2,1)}, u32[]{:S(2)}, u32[]{:S(2)}) async-start(bf16[8,128,512]{2,1,0:T(8,128)(2,1)} %get-tuple-element.62), calls=%async_computation | async-start | bytes 2097152 | tf_op jit(solution)/shard_map/all_to_all | solution.py:315
  55.3 18.7 %collective-permute-start.10 = (bf16[2,1024,128]{2,1,0:T(8,128)(2,1)}, bf16[2,1024,128]{2,1,0:T(8,128)(2,1)S(1)}, u32[]{:S(2)}, u32[]{:S(2)}) collective-permute-start(bf16[2,1024,128]{2,1,0:T(8,128)(2,1)} %get-tuple-element.58), channel_id=1, source_target_pairs={{0,4},{1,5},{2,6},{3,7},{4,0},{5,1},{6,2},{7,3},{8,12},{9,13},{10,... | collective-permute-start | bytes 1572872 | tf_op jit(solution)/shard_map/ppermute | solution.py:217
  73.9 48.5 %copy-start.2 = (bf16[128,512]{1,0:T(8,128)(2,1)S(1)}, bf16[128,512]{1,0:T(8,128)(2,1)}, u32[]{:S(2)}) copy-start(bf16[128,512]{1,0:T(8,128)(2,1)} %get-tuple-element.80) | copy-start | bytes 393220
  73.9 59.6 %copy-start.3 = (bf16[128,512]{1,0:T(8,128)(2,1)S(1)}, bf16[128,512]{1,0:T(8,128)(2,1)}, u32[]{:S(2)}) copy-start(bf16[128,512]{1,0:T(8,128)(2,1)} %get-tuple-element.82) | copy-start | bytes 393220
  73.9 7.2 %collective-permute-start.13 = (bf16[128,512]{1,0:T(8,128)(2,1)}, bf16[128,512]{1,0:T(8,128)(2,1)S(1)}, u32[]{:S(2)}, u32[]{:S(2)}) collective-permute-start(bf16[128,512]{1,0:T(8,128)(2,1)} %get-tuple-element.63), channel_id=1, source_target_pairs={{0,32},{32,64},{64,96},{96,128},{128,160},{160,192},{192,224},{224... | collective-permute-start | bytes 393224 | tf_op jit(solution)/shard_map/ppermute | solution.py:197
  75.6 5.5 %collective-permute-start.14 = (bf16[128,512]{1,0:T(8,128)(2,1)}, bf16[128,512]{1,0:T(8,128)(2,1)S(1)}, u32[]{:S(2)}, u32[]{:S(2)}) collective-permute-start(bf16[128,512]{1,0:T(8,128)(2,1)} %get-tuple-element.64), channel_id=1, source_target_pairs={{0,224},{32,0},{64,32},{96,64},{128,96},{160,128},{192,160},{224,1... | collective-permute-start | bytes 393224 | tf_op jit(solution)/shard_map/ppermute | solution.py:197
  77.2 20.7 %collective-permute-start.11 = (bf16[3,1024,128]{2,1,0:T(8,128)(2,1)}, bf16[3,1024,128]{2,1,0:T(8,128)(2,1)S(1)}, u32[]{:S(2)}, u32[]{:S(2)}) collective-permute-start(bf16[3,1024,128]{2,1,0:T(8,128)(2,1)} %pad_maximum_fusion), channel_id=1, source_target_pairs={{0,1},{1,0},{2,3},{3,2},{4,5},{5,4},{6,7},{7,6},{8,9},{9,8},{10,11... | collective-permute-start | bytes 2359304 | tf_op jit(solution)/shard_map/ppermute | solution.py:217
  82.8 7.5 %collective-permute-start.17 = (bf16[128,512]{1,0:T(8,128)(2,1)S(1)}, bf16[128,512]{1,0:T(8,128)(2,1)S(1)}, u32[]{:S(2)}, u32[]{:S(2)}) collective-permute-start(bf16[128,512]{1,0:T(8,128)(2,1)S(1)} %reduce_sum.21), channel_id=1, source_target_pairs={{0,6},{1,7},{2,0},{3,1},{4,2},{5,3},{6,4},{7,5},{8,14},{9,15},{10,... | collective-permute-start | bytes 393224 | tf_op jit(solution)/shard_map/ppermute | solution.py:217
  83.9 9.3 %collective-permute-start.16 = (bf16[128,512]{1,0:T(8,128)(2,1)S(1)}, bf16[128,512]{1,0:T(8,128)(2,1)S(1)}, u32[]{:S(2)}, u32[]{:S(2)}) collective-permute-start(bf16[128,512]{1,0:T(8,128)(2,1)S(1)} %reduce_sum.21), channel_id=1, source_target_pairs={{0,4},{1,5},{2,6},{3,7},{4,0},{5,1},{6,2},{7,3},{8,12},{9,13},{10,... | collective-permute-start | bytes 393224 | tf_op jit(solution)/shard_map/ppermute | solution.py:217
  85.8 7.4 %collective-permute-start.15 = (bf16[128,512]{1,0:T(8,128)(2,1)S(1)}, bf16[128,512]{1,0:T(8,128)(2,1)S(1)}, u32[]{:S(2)}, u32[]{:S(2)}) collective-permute-start(bf16[128,512]{1,0:T(8,128)(2,1)S(1)} %reduce_sum.21), channel_id=1, source_target_pairs={{0,2},{1,3},{2,4},{3,5},{4,6},{5,7},{6,0},{7,1},{8,10},{9,11},{10,... | collective-permute-start | bytes 393224 | tf_op jit(solution)/shard_map/ppermute | solution.py:217
  88.8 6.3 %collective-permute-start.18 = (bf16[128,512]{1,0:T(8,128)(2,1)S(1)}, bf16[128,512]{1,0:T(8,128)(2,1)S(1)}, u32[]{:S(2)}, u32[]{:S(2)}) collective-permute-start(bf16[128,512]{1,0:T(8,128)(2,1)S(1)} %add_convert_fusion.7), channel_id=1, source_target_pairs={{0,32},{32,64},{64,96},{96,128},{128,160},{160,192},{192,224},{224... | collective-permute-start | bytes 393224 | tf_op jit(solution)/shard_map/ppermute | solution.py:197
  90.3 5.4 %collective-permute-start.19 = (bf16[128,512]{1,0:T(8,128)(2,1)S(1)}, bf16[128,512]{1,0:T(8,128)(2,1)S(1)}, u32[]{:S(2)}, u32[]{:S(2)}) collective-permute-start(bf16[128,512]{1,0:T(8,128)(2,1)S(1)} %add_convert_fusion.6), channel_id=1, source_target_pairs={{0,224},{32,0},{64,32},{96,64},{128,96},{160,128},{192,160},{224,1... | collective-permute-start | bytes 393224 | tf_op jit(solution)/shard_map/ppermute | solution.py:197
  95.7 2.3 %collective-permute-start.20 = (bf16[512,512]{1,0:T(8,128)(2,1)S(1)}, bf16[512,512]{1,0:T(8,128)(2,1)S(1)}, u32[]{:S(2)}, u32[]{:S(2)}) collective-permute-start(bf16[512,512]{1,0:T(8,128)(2,1)S(1)} %pad_maximum_fusion.1.refs_6_), channel_id=1, source_target_pairs={{0,1},{1,0},{2,3},{3,2},{4,5},{5,4},{6,7},{7,6},{8,9},{9,8},{10,11... | collective-permute-start | bytes 1572872 | tf_op jit(solution)/shard_map/ppermute | solution.py:217
  95.7 2.3 %collective-permute-start.12 = (bf16[1024,128]{1,0:T(8,128)(2,1)S(1)}, bf16[1024,128]{1,0:T(8,128)(2,1)S(1)}, u32[]{:S(2)}, u32[]{:S(2)}) collective-permute-start(bf16[1024,128]{1,0:T(8,128)(2,1)S(1)} %slice_bitcast_fusion), channel_id=1, source_target_pairs={{0,1},{1,0},{2,3},{3,2},{4,5},{5,4},{6,7},{7,6},{8,9},{9,8},{10,11... | collective-permute-start | bytes 786440 | tf_op jit(solution)/shard_map/ppermute | solution.py:217
  99.2 11.6 %collective-permute-start.21 = (bf16[256,512]{1,0:T(8,128)(2,1)S(1)}, bf16[256,512]{1,0:T(8,128)(2,1)S(1)}, u32[]{:S(2)}, u32[]{:S(2)}) collective-permute-start(bf16[256,512]{1,0:T(8,128)(2,1)S(1)} %get-tuple-element.72), channel_id=1, source_target_pairs={{0,8},{1,9},{2,10},{3,11},{4,12},{5,13},{6,14},{7,15},{8,16},{9,17... | collective-permute-start | bytes 786440 | tf_op jit(solution)/shard_map/ppermute | solution.py:217
  100.9 14.8 %collective-permute-start.22 = (bf16[256,512]{1,0:T(8,128)(2,1)S(1)}, bf16[256,512]{1,0:T(8,128)(2,1)S(1)}, u32[]{:S(2)}, u32[]{:S(2)}) collective-permute-start(bf16[256,512]{1,0:T(8,128)(2,1)S(1)} %get-tuple-element.73), channel_id=1, source_target_pairs={{0,16},{1,17},{2,18},{3,19},{4,20},{5,21},{6,22},{7,23},{8,24},{9,... | collective-permute-start | bytes 786440 | tf_op jit(solution)/shard_map/ppermute | solution.py:217
  103.8 11.9 %collective-permute-start.23 = (bf16[256,512]{1,0:T(8,128)(2,1)S(1)}, bf16[256,512]{1,0:T(8,128)(2,1)S(1)}, u32[]{:S(2)}, u32[]{:S(2)}) collective-permute-start(bf16[256,512]{1,0:T(8,128)(2,1)S(1)} %get-tuple-element.74), channel_id=1, source_target_pairs={{0,24},{1,25},{2,26},{3,27},{4,28},{5,29},{6,30},{7,31},{8,0},{9,1... | collective-permute-start | bytes 786440 | tf_op jit(solution)/shard_map/ppermute | solution.py:217
  106.1 10.5 %collective-permute-start.25 = (bf16[128,512]{1,0:T(8,128)(2,1)S(1)}, bf16[128,512]{1,0:T(8,128)(2,1)S(1)}, u32[]{:S(2)}, u32[]{:S(2)}) collective-permute-start(bf16[128,512]{1,0:T(8,128)(2,1)S(1)} %add_convert_fusion.4), channel_id=1, source_target_pairs={{0,224},{32,0},{64,32},{96,64},{128,96},{160,128},{192,160},{224,1... | collective-permute-start | bytes 393224 | tf_op jit(solution)/shard_map/ppermute | solution.py:197
  110.8 6.3 %collective-permute-start.24 = (bf16[128,512]{1,0:T(8,128)(2,1)S(1)}, bf16[128,512]{1,0:T(8,128)(2,1)S(1)}, u32[]{:S(2)}, u32[]{:S(2)}) collective-permute-start(bf16[128,512]{1,0:T(8,128)(2,1)S(1)} %add_convert_fusion.5), channel_id=1, source_target_pairs={{0,32},{32,64},{64,96},{96,128},{128,160},{160,192},{192,224},{224... | collective-permute-start | bytes 393224 | tf_op jit(solution)/shard_map/ppermute | solution.py:197
  117.0 17.7 %all-to-all-start.1 = ((bf16[8,32,512]{2,1,0:T(8,128)(2,1)}), bf16[8,32,512]{2,1,0:T(8,128)(2,1)S(1)}, u32[]{:S(2)}, u32[]{:S(2)}) async-start(bf16[8,32,512]{2,1,0:T(8,128)(2,1)} %bitcast.11), calls=%async_computation.1 | async-start | bytes 524288 | tf_op jit(solution)/shard_map/all_to_all | solution.py:345
  122.5 11.1 %collective-permute-start.26 = (bf16[128,512]{1,0:T(8,128)(2,1)S(1)}, bf16[128,512]{1,0:T(8,128)(2,1)S(1)}, u32[]{:S(2)}, u32[]{:S(2)}) collective-permute-start(bf16[128,512]{1,0:T(8,128)(2,1)S(1)} %add_convert_fusion.3), channel_id=1, source_target_pairs={{0,32},{32,64},{64,96},{96,128},{128,160},{160,192},{192,224},{224... | collective-permute-start | bytes 393224 | tf_op jit(solution)/shard_map/ppermute | solution.py:197
  (9 other events, 116.4 us)

commit v4 on v3

--- a/solution.py
+++ b/solution.py
@@ -113,10 +113,10 @@
         g2 = jnp.concatenate([g[:, s] for s in pair(c)], 0)
         p = probs[0, :, 2 * c * HEAD_DIM : (2 * c + 2) * HEAD_DIM]
         out_t = dot(v_t[...], p, NN)
-        dots = dot(v[...], g2, NT)
-        wide = p.astype(jnp.float32)
-        delta = jnp.sum(wide * dots, axis=0, keepdims=True)
-        slopes = (wide * (dots - delta)).astype(jnp.bfloat16)
+        g_t = g2.T
+        delta = jnp.sum(g_t.astype(jnp.float32) * out_t, axis=0, keepdims=True)
+        dots = dot(v[...], g_t, NN)
+        slopes = (p.astype(jnp.float32) * (dots - delta)).astype(jnp.bfloat16)
         dq_t = dot(k_t[...], slopes, NN) * scale
         dk_c = dot(slopes, q2, NN)
         if c == 0:

time: 136 us -> 135 us (level)
  Pallas kernels: 33.1 us -> 30.5 us
  waiting for transfers between devices: 36.6 us -> 39.1 us
    pallas_call x1, Pallas kernels: 15.2 us -> 12.6 us  [out_and_grads(): pl.pallas_call(grads_kernel, grid=(KV_HEADS,), in_specs=[wide, wide, squa...]
    ppermute x15, waiting for transfers between devices: 29.2 us -> 30.8 us  [along_ctx(): return lax.ppermute(a, 'ctx', [(i, (i + far) % n) for i in range(n)])]
  transfers between devices with their start and end apart: 29 -> 29, of which waited for: 14 -> 14; matrix products, arithmetic and copies ran while one was open for 6% -> 6% of each run, Pallas kernels for 15% -> 13%
where the time goes in v4:
time: 135 us; the launch traced here: 134 us
  starting transfers between devices  53.2 us (39%)
  waiting for transfers between devices  39.1 us (29%)
  Pallas kernels  30.5 us (23%)
  other arithmetic  9.99 us (7%)
    ppermute x15, waiting for transfers between devices, along_ctx(): return lax.ppermute(a, 'ctx', [(i, (i + far) % n) for i in range(n)])  30.8 us
    ppermute x15, starting transfers between devices, along_ctx(): return lax.ppermute(a, 'ctx', [(i, (i + far) % n) for i in range(n)])  28.4 us
    ppermute x12, starting transfers between devices, along_dp(): return lax.ppermute(a, 'dp', pairs)  16 us
    pallas_call x1, Pallas kernels, out_and_grads(): pl.pallas_call(grads_kernel, grid=(KV_HEADS,), in_specs=[wide, wide, squa...  12.6 us
    pallas_call x1, Pallas kernels, probs_and_dv(): pl.pallas_call(probs_kernel, grid=(KV_HEADS,), in_specs=[pl.BlockSpec(mem...  11.8 us
    ppermute x12, waiting for transfers between devices, along_dp(): return lax.ppermute(a, 'dp', pairs)  6.57 us
    pallas_call x1, Pallas kernels, columns_for_x(): pl.pallas_call(turn_kernel, grid_spec=pltpu.PrefetchScalarGridSpec(num_sc...  4.82 us
    all_to_all x1, starting transfers between devices, on_device(): last = lax.all_to_all(total, 'ctx', split_axis=0, concat_axis=0, tiled=True)  4.51 us
  transfers between devices with their start and end apart: 29, of which 14 were waited for; matrix products, arithmetic and copies ran while one was open for 6% of the time, Pallas kernels for 13%

profile of v4, /device:TPU:2, one launch (start us, length us, event | category | flops | bytes accessed | tf_op | source)
XLA Modules:
  0.0 134.4 jit_solution(17159850018345153138)
XLA Ops:
  1.6 5.9 %collective-permute-start.1 = (bf16[128,1024]{1,0:T(8,128)(2,1)S(1)}, bf16[128,1024]{1,0:T(8,128)(2,1)S(1)}, u32[]{:S(2)}, u32[]{:S(2)}) collective-permute-start(bf16[128,1024]{1,0:T(8,128)(2,1)S(1)} %pad_maximum_fusion.2.refs_0_.refs_8_), channel_id=1, source_target_pairs={{0,224},{32,0},{64,32},{96,64},{128,96},{160,128},{192,160},{224,1... | collective-permute-start | bytes 786440 | tf_op jit(solution)/shard_map/ppermute | solution.py:197
  8.2 4.8 %shard_map.111 = (bf16[2,1024,128]{2,1,0:T(8,128)(2,1)}, bf16[2,1024,128]{2,1,0:T(8,128)(2,1)}, bf16[2,1024,128]{2,1,0:T(8,128)(2,1)}, bf16[2,1024,128]{2,1,0:T(8,128)(2,1)}) custom-call(s32[3]{0:T(128)} %pad_add_fusion.where, bf16[128,8192]{1,0:T(8,128)(2,1)} %bitcast.15, bf16[128,8192]{1,0:T(8,128)(2,1)} %bitcast.16, bf16[128,8192]{1,0:T(8,128)(2,1)} %bitcast.17, ...), custom_call_target="tpu_custom_call" | custom-call | bytes 4194304 | tf_op jit(solution)/shard_map/pallas_call | solution.py:244
  13.1 3.4 %collective-permute-done.refs_1_.refs_9_ = bf16[128,1024]{1,0:T(8,128)(2,1)S(1)} collective-permute-done((bf16[128,1024]{1,0:T(8,128)(2,1)S(1)}, bf16[128,1024]{1,0:T(8,128)(2,1)S(1)}, u32[]{:S(2)}, u32[]{:S(2)}) %collective-permute-start) | collective-permute-done | bytes 262176 | tf_op jit(solution)/shard_map/ppermute | solution.py:197
  16.6 3.2 %collective-permute-start.3 = (bf16[128,1024]{1,0:T(8,128)(2,1)S(1)}, bf16[128,1024]{1,0:T(8,128)(2,1)S(1)}, u32[]{:S(2)}, u32[]{:S(2)}) collective-permute-start(bf16[128,1024]{1,0:T(8,128)(2,1)S(1)} %collective-permute-done.1.refs_2_.refs_10_), channel_id=1, source_target_pairs={{0,224},{32,0},{64,32},{96,64},{128,96},{160,128},{192,160},{224,1... | collective-permute-start | bytes 786440 | tf_op jit(solution)/shard_map/ppermute | solution.py:197
  19.8 1.5 %collective-permute-start.8 = (bf16[2,1024,128]{2,1,0:T(8,128)(2,1)}, bf16[2,1024,128]{2,1,0:T(8,128)(2,1)S(1)}, u32[]{:S(2)}, u32[]{:S(2)}) collective-permute-start(bf16[2,1024,128]{2,1,0:T(8,128)(2,1)} %get-tuple-element.47), channel_id=1, source_target_pairs={{0,2},{1,3},{2,4},{3,5},{4,6},{5,7},{6,0},{7,1},{8,10},{9,11},{10,... | collective-permute-start | bytes 1572872 | tf_op jit(solution)/shard_map/ppermute | solution.py:217
  21.8 2.8 %collective-permute-done.2.refs_3_.refs_11_ = bf16[128,1024]{1,0:T(8,128)(2,1)S(1)} collective-permute-done((bf16[128,1024]{1,0:T(8,128)(2,1)S(1)}, bf16[128,1024]{1,0:T(8,128)(2,1)S(1)}, u32[]{:S(2)}, u32[]{:S(2)}) %collective-permute-start.2) | collective-permute-done | bytes 262176 | tf_op jit(solution)/shard_map/ppermute | solution.py:197
  24.6 3.2 %collective-permute-start.5 = (bf16[128,1024]{1,0:T(8,128)(2,1)S(1)}, bf16[128,1024]{1,0:T(8,128)(2,1)S(1)}, u32[]{:S(2)}, u32[]{:S(2)}) collective-permute-start(bf16[128,1024]{1,0:T(8,128)(2,1)S(1)} %collective-permute-done.3.refs_4_.refs_12_), channel_id=1, source_target_pairs={{0,224},{32,0},{64,32},{96,64},{128,96},{160,128},{192,160},{224,1... | collective-permute-start | bytes 786440 | tf_op jit(solution)/shard_map/ppermute | solution.py:197
  27.9 4.3 %collective-permute-done.4.refs_5_.refs_13_ = bf16[128,1024]{1,0:T(8,128)(2,1)S(1)} collective-permute-done((bf16[128,1024]{1,0:T(8,128)(2,1)S(1)}, bf16[128,1024]{1,0:T(8,128)(2,1)S(1)}, u32[]{:S(2)}, u32[]{:S(2)}) %collective-permute-start.4) | collective-permute-done | bytes 262176 | tf_op jit(solution)/shard_map/ppermute | solution.py:197
  32.3 3.3 %collective-permute-start.7 = (bf16[128,512]{1,0:T(8,128)(2,1)S(1)}, bf16[128,512]{1,0:T(8,128)(2,1)S(1)}, u32[]{:S(2)}, u32[]{:S(2)}) collective-permute-start(bf16[128,512]{1,0:T(8,128)(2,1)S(1)} %slice.25), channel_id=1, source_target_pairs={{0,224},{32,0},{64,32},{96,64},{128,96},{160,128},{192,160},{224,1... | collective-permute-start | bytes 393224 | tf_op jit(solution)/shard_map/ppermute | solution.py:197
  35.6 2.8 %collective-permute-done.6.refs_7_ = bf16[128,512]{1,0:T(8,128)(2,1)S(1)} collective-permute-done((bf16[128,512]{1,0:T(8,128)(2,1)S(1)}, bf16[128,512]{1,0:T(8,128)(2,1)S(1)}, u32[]{:S(2)}, u32[]{:S(2)}) %collective-permute-start.6) | collective-permute-done | bytes 131104 | tf_op jit(solution)/shard_map/ppermute | solution.py:197
  39.1 11.8 %shard_map.112 = (bf16[4,1024,1024]{2,1,0:T(8,128)(2,1)}, bf16[8,128,512]{2,1,0:T(8,128)(2,1)}) custom-call(s32[1,8]{1,0:T(1,128)} %lens.1, s32[1,8]{1,0:T(1,128)} %prefix.1, s32[1,16]{1,0:T(1,128)} %order.1, bf16[128,4096]{1,0:T(8,128)(2,1)} %bitcast.25, bf16[128,4096]{1,0:T(8,128)(2,1)} %bitcast.27, bf16[128,1024]{1,0:T(8,128)(2,1)} %copy-done.1, ...), custom_call_target="tpu_custom_call" | custom-call | flops 2147483648 | bytes 12582912 | tf_op jit(solution)/shard_map/pallas_call | solution.py:150
  51.0 4.3 %all-to-all-start = ((bf16[8,128,512]{2,1,0:T(8,128)(2,1)}), bf16[8,128,512]{2,1,0:T(8,128)(2,1)}, u32[]{:S(2)}, u32[]{:S(2)}) async-start(bf16[8,128,512]{2,1,0:T(8,128)(2,1)} %get-tuple-element.62), calls=%async_computation | async-start | bytes 2097152 | tf_op jit(solution)/shard_map/all_to_all | solution.py:315
  55.3 2.4 %collective-permute-start.10 = (bf16[2,1024,128]{2,1,0:T(8,128)(2,1)}, bf16[2,1024,128]{2,1,0:T(8,128)(2,1)S(1)}, u32[]{:S(2)}, u32[]{:S(2)}) collective-permute-start(bf16[2,1024,128]{2,1,0:T(8,128)(2,1)} %get-tuple-element.58), channel_id=1, source_target_pairs={{0,4},{1,5},{2,6},{3,7},{4,0},{5,1},{6,2},{7,3},{8,12},{9,13},{10,... | collective-permute-start | bytes 1572872 | tf_op jit(solution)/shard_map/ppermute | solution.py:217
  58.7 12.6 %shard_map.113 = (bf16[128,4096]{1,0:T(8,128)(2,1)}, bf16[128,4096]{1,0:T(8,128)(2,1)}, bf16[128,512]{1,0:T(8,128)(2,1)}, bf16[128,512]{1,0:T(8,128)(2,1)}, bf16...) custom-call(bf16[128,4096]{1,0:T(8,128)(2,1)} %bitcast.26, ...), custom_call_target="tpu_custom_call" | custom-call | flops 4294967296 | bytes 14680064 | tf_op jit(solution)/shard_map/pallas_call | solution.py:176
  71.4 1.7 %collective-permute-start.13 = (bf16[128,512]{1,0:T(8,128)(2,1)}, bf16[128,512]{1,0:T(8,128)(2,1)S(1)}, u32[]{:S(2)}, u32[]{:S(2)}) collective-permute-start(bf16[128,512]{1,0:T(8,128)(2,1)} %get-tuple-element.63), channel_id=1, source_target_pairs={{0,32},{32,64},{64,96},{96,128},{128,160},{160,192},{192,224},{224... | collective-permute-start | bytes 393224 | tf_op jit(solution)/shard_map/ppermute | solution.py:197
  73.0 1.6 %collective-permute-start.14 = (bf16[128,512]{1,0:T(8,128)(2,1)}, bf16[128,512]{1,0:T(8,128)(2,1)S(1)}, u32[]{:S(2)}, u32[]{:S(2)}) collective-permute-start(bf16[128,512]{1,0:T(8,128)(2,1)} %get-tuple-element.64), channel_id=1, source_target_pairs={{0,224},{32,0},{64,32},{96,64},{128,96},{160,128},{192,160},{224,1... | collective-permute-start | bytes 393224 | tf_op jit(solution)/shard_map/ppermute | solution.py:197
  74.7 5.5 %collective-permute-done.13 = bf16[128,512]{1,0:T(8,128)(2,1)S(1)} collective-permute-done((bf16[128,512]{1,0:T(8,128)(2,1)}, bf16[128,512]{1,0:T(8,128)(2,1)S(1)}, u32[]{:S(2)}, u32[]{:S(2)}) %collective-permute-start.13) | collective-permute-done | bytes 131104 | tf_op jit(solution)/shard_map/ppermute | solution.py:197
  81.3 1.4 %reduce_sum.21 = bf16[128,512]{1,0:T(8,128)(2,1)S(1)} reduce(bf16[8,128,512]{2,1,0:T(8,128)(2,1)} %all-to-all-done, bf16[]{:T(256)} %constant.10.clone.1), dimensions={0}, to_apply=%region_0.0 | reduce | flops 458752 | bytes 1179650 | tf_op jit(solution)/shard_map/reduce_sum | solution.py:327
  83.7 2.1 %collective-permute-start.16 = (bf16[128,512]{1,0:T(8,128)(2,1)S(1)}, bf16[128,512]{1,0:T(8,128)(2,1)S(1)}, u32[]{:S(2)}, u32[]{:S(2)}) collective-permute-start(bf16[128,512]{1,0:T(8,128)(2,1)S(1)} %reduce_sum.21), channel_id=1, source_target_pairs={{0,4},{1,5},{2,6},{3,7},{4,0},{5,1},{6,2},{7,3},{8,12},{9,13},{10,... | collective-permute-start | bytes 393224 | tf_op jit(solution)/shard_map/ppermute | solution.py:217
  85.7 2.1 %collective-permute-start.15 = (bf16[128,512]{1,0:T(8,128)(2,1)S(1)}, bf16[128,512]{1,0:T(8,128)(2,1)S(1)}, u32[]{:S(2)}, u32[]{:S(2)}) collective-permute-start(bf16[128,512]{1,0:T(8,128)(2,1)S(1)} %reduce_sum.21), channel_id=1, source_target_pairs={{0,2},{1,3},{2,4},{3,5},{4,6},{5,7},{6,0},{7,1},{8,10},{9,11},{10,... | collective-permute-start | bytes 393224 | tf_op jit(solution)/shard_map/ppermute | solution.py:217
  90.3 2.8 %collective-permute-start.19 = (bf16[128,512]{1,0:T(8,128)(2,1)S(1)}, bf16[128,512]{1,0:T(8,128)(2,1)S(1)}, u32[]{:S(2)}, u32[]{:S(2)}) collective-permute-start(bf16[128,512]{1,0:T(8,128)(2,1)S(1)} %add_convert_fusion.6), channel_id=1, source_target_pairs={{0,224},{32,0},{64,32},{96,64},{128,96},{160,128},{192,160},{224,1... | collective-permute-start | bytes 393224 | tf_op jit(solution)/shard_map/ppermute | solution.py:197
  93.2 1.9 %collective-permute-done.18 = bf16[128,512]{1,0:T(8,128)(2,1)S(1)} collective-permute-done((bf16[128,512]{1,0:T(8,128)(2,1)S(1)}, bf16[128,512]{1,0:T(8,128)(2,1)S(1)}, u32[]{:S(2)}, u32[]{:S(2)}) %collective-permute-start.18) | collective-permute-done | bytes 131104 | tf_op jit(solution)/shard_map/ppermute | solution.py:197
  96.3 1.7 %collective-permute-done.12.refs_5_ = bf16[1024,128]{1,0:T(8,128)(2,1)S(1)} collective-permute-done((bf16[1024,128]{1,0:T(8,128)(2,1)S(1)}, bf16[1024,128]{1,0:T(8,128)(2,1)S(1)}, u32[]{:S(2)}, u32[]{:S(2)}) %collective-permute-start.12) | collective-permute-done | bytes 262176 | tf_op jit(solution)/shard_map/ppermute | solution.py:217
  97.9 1.2 shard_map.114
  99.2 1.7 %collective-permute-start.21 = (bf16[256,512]{1,0:T(8,128)(2,1)S(1)}, bf16[256,512]{1,0:T(8,128)(2,1)S(1)}, u32[]{:S(2)}, u32[]{:S(2)}) collective-permute-start(bf16[256,512]{1,0:T(8,128)(2,1)S(1)} %get-tuple-element.72), channel_id=1, source_target_pairs={{0,8},{1,9},{2,10},{3,11},{4,12},{5,13},{6,14},{7,15},{8,16},{9,17... | collective-permute-start | bytes 786440 | tf_op jit(solution)/shard_map/ppermute | solution.py:217
  100.8 2.9 %collective-permute-start.22 = (bf16[256,512]{1,0:T(8,128)(2,1)S(1)}, bf16[256,512]{1,0:T(8,128)(2,1)S(1)}, u32[]{:S(2)}, u32[]{:S(2)}) collective-permute-start(bf16[256,512]{1,0:T(8,128)(2,1)S(1)} %get-tuple-element.73), channel_id=1, source_target_pairs={{0,16},{1,17},{2,18},{3,19},{4,20},{5,21},{6,22},{7,23},{8,24},{9,... | collective-permute-start | bytes 786440 | tf_op jit(solution)/shard_map/ppermute | solution.py:217
  103.7 1.3 %collective-permute-start.23 = (bf16[256,512]{1,0:T(8,128)(2,1)S(1)}, bf16[256,512]{1,0:T(8,128)(2,1)S(1)}, u32[]{:S(2)}, u32[]{:S(2)}) collective-permute-start(bf16[256,512]{1,0:T(8,128)(2,1)S(1)} %get-tuple-element.74), channel_id=1, source_target_pairs={{0,24},{1,25},{2,26},{3,27},{4,28},{5,29},{6,30},{7,31},{8,0},{9,1... | collective-permute-start | bytes 786440 | tf_op jit(solution)/shard_map/ppermute | solution.py:217
  106.0 3.7 %collective-permute-start.25 = (bf16[128,512]{1,0:T(8,128)(2,1)S(1)}, bf16[128,512]{1,0:T(8,128)(2,1)S(1)}, u32[]{:S(2)}, u32[]{:S(2)}) collective-permute-start(bf16[128,512]{1,0:T(8,128)(2,1)S(1)} %add_convert_fusion.4), channel_id=1, source_target_pairs={{0,224},{32,0},{64,32},{96,64},{128,96},{160,128},{192,160},{224,1... | collective-permute-start | bytes 393224 | tf_op jit(solution)/shard_map/ppermute | solution.py:197
  110.8 4.9 %collective-permute-done.22 = bf16[256,512]{1,0:T(8,128)(2,1)S(1)} collective-permute-done((bf16[256,512]{1,0:T(8,128)(2,1)S(1)}, bf16[256,512]{1,0:T(8,128)(2,1)S(1)}, u32[]{:S(2)}, u32[]{:S(2)}) %collective-permute-start.22) | collective-permute-done | bytes 262176 | tf_op jit(solution)/shard_map/ppermute | solution.py:217
  117.0 4.5 %all-to-all-start.1 = ((bf16[8,32,512]{2,1,0:T(8,128)(2,1)}), bf16[8,32,512]{2,1,0:T(8,128)(2,1)S(1)}, u32[]{:S(2)}, u32[]{:S(2)}) async-start(bf16[8,32,512]{2,1,0:T(8,128)(2,1)} %bitcast.11), calls=%async_computation.1 | async-start | bytes 524288 | tf_op jit(solution)/shard_map/all_to_all | solution.py:345
  121.5 2.1 %collective-permute-start.26 = (bf16[128,512]{1,0:T(8,128)(2,1)S(1)}, bf16[128,512]{1,0:T(8,128)(2,1)S(1)}, u32[]{:S(2)}, u32[]{:S(2)}) collective-permute-start(bf16[128,512]{1,0:T(8,128)(2,1)S(1)} %add_convert_fusion.3), channel_id=1, source_target_pairs={{0,32},{32,64},{64,96},{96,128},{128,160},{160,192},{192,224},{224... | collective-permute-start | bytes 393224 | tf_op jit(solution)/shard_map/ppermute | solution.py:197
  123.6 9.0 %collective-permute-done.26 = bf16[128,512]{1,0:T(8,128)(2,1)S(1)} collective-permute-done((bf16[128,512]{1,0:T(8,128)(2,1)S(1)}, bf16[128,512]{1,0:T(8,128)(2,1)S(1)}, u32[]{:S(2)}, u32[]{:S(2)}) %collective-permute-start.26) | collective-permute-done | bytes 131104 | tf_op jit(solution)/shard_map/ppermute | solution.py:197
  (73 shorter events, 15.1 us)
Async XLA Ops:
  1.6 11.5 %collective-permute-start.1 = (bf16[128,1024]{1,0:T(8,128)(2,1)S(1)}, bf16[128,1024]{1,0:T(8,128)(2,1)S(1)}, u32[]{:S(2)}, u32[]{:S(2)}) collective-permute-start(bf16[128,1024]{1,0:T(8,128)(2,1)S(1)} %pad_maximum_fusion.2.refs_0_.refs_8_), channel_id=1, source_target_pairs={{0,224},{32,0},{64,32},{96,64},{128,96},{160,128},{192,160},{224,1... | collective-permute-start | bytes 786440 | tf_op jit(solution)/shard_map/ppermute | solution.py:197
  7.6 9.0 %collective-permute-start = (bf16[128,1024]{1,0:T(8,128)(2,1)S(1)}, bf16[128,1024]{1,0:T(8,128)(2,1)S(1)}, u32[]{:S(2)}, u32[]{:S(2)}) collective-permute-start(bf16[128,1024]{1,0:T(8,128)(2,1)S(1)} %pad_maximum_fusion.2.refs_0_.refs_8_), channel_id=1, source_target_pairs={{0,32},{32,64},{64,96},{96,128},{128,160},{160,192},{192,224},{224... | collective-permute-start | bytes 786440 | tf_op jit(solution)/shard_map/ppermute | solution.py:197
  13.0 44.6 %copy-start = (bf16[2,1024,128]{2,1,0:T(8,128)(2,1)S(1)}, bf16[2,1024,128]{2,1,0:T(8,128)(2,1)}, u32[]{:S(2)}) copy-start(bf16[2,1024,128]{2,1,0:T(8,128)(2,1)} %get-tuple-element.51.refs_0_) | copy-start | bytes 1572868
  16.5 8.1 %collective-permute-start.2 = (bf16[128,1024]{1,0:T(8,128)(2,1)S(1)}, bf16[128,1024]{1,0:T(8,128)(2,1)S(1)}, u32[]{:S(2)}, u32[]{:S(2)}) collective-permute-start(bf16[128,1024]{1,0:T(8,128)(2,1)S(1)} %collective-permute-done.refs_1_.refs_9_), channel_id=1, source_target_pairs={{0,32},{32,64},{64,96},{96,128},{128,160},{160,192},{192,224},{224... | collective-permute-start | bytes 786440 | tf_op jit(solution)/shard_map/ppermute | solution.py:197
  16.6 8.1 %collective-permute-start.3 = (bf16[128,1024]{1,0:T(8,128)(2,1)S(1)}, bf16[128,1024]{1,0:T(8,128)(2,1)S(1)}, u32[]{:S(2)}, u32[]{:S(2)}) collective-permute-start(bf16[128,1024]{1,0:T(8,128)(2,1)S(1)} %collective-permute-done.1.refs_2_.refs_10_), channel_id=1, source_target_pairs={{0,224},{32,0},{64,32},{96,64},{128,96},{160,128},{192,160},{224,1... | collective-permute-start | bytes 786440 | tf_op jit(solution)/shard_map/ppermute | solution.py:197
  19.8 15.8 %collective-permute-start.8 = (bf16[2,1024,128]{2,1,0:T(8,128)(2,1)}, bf16[2,1024,128]{2,1,0:T(8,128)(2,1)S(1)}, u32[]{:S(2)}, u32[]{:S(2)}) collective-permute-start(bf16[2,1024,128]{2,1,0:T(8,128)(2,1)} %get-tuple-element.47), channel_id=1, source_target_pairs={{0,2},{1,3},{2,4},{3,5},{4,6},{5,7},{6,0},{7,1},{8,10},{9,11},{10,... | collective-permute-start | bytes 1572872 | tf_op jit(solution)/shard_map/ppermute | solution.py:217
  21.3 14.4 %collective-permute-start.9 = (bf16[2,1024,128]{2,1,0:T(8,128)(2,1)}, bf16[2,1024,128]{2,1,0:T(8,128)(2,1)S(1)}, u32[]{:S(2)}, u32[]{:S(2)}) collective-permute-start(bf16[2,1024,128]{2,1,0:T(8,128)(2,1)} %get-tuple-element.48), channel_id=1, source_target_pairs={{0,6},{1,7},{2,0},{3,1},{4,2},{5,3},{6,4},{7,5},{8,14},{9,15},{10,... | collective-permute-start | bytes 1572872 | tf_op jit(solution)/shard_map/ppermute | solution.py:217
  24.6 7.6 %collective-permute-start.4 = (bf16[128,1024]{1,0:T(8,128)(2,1)S(1)}, bf16[128,1024]{1,0:T(8,128)(2,1)S(1)}, u32[]{:S(2)}, u32[]{:S(2)}) collective-permute-start(bf16[128,1024]{1,0:T(8,128)(2,1)S(1)} %collective-permute-done.2.refs_3_.refs_11_), channel_id=1, source_target_pairs={{0,32},{32,64},{64,96},{96,128},{128,160},{160,192},{192,224},{224... | collective-permute-start | bytes 786440 | tf_op jit(solution)/shard_map/ppermute | solution.py:197
  24.6 7.7 %collective-permute-start.5 = (bf16[128,1024]{1,0:T(8,128)(2,1)S(1)}, bf16[128,1024]{1,0:T(8,128)(2,1)S(1)}, u32[]{:S(2)}, u32[]{:S(2)}) collective-permute-start(bf16[128,1024]{1,0:T(8,128)(2,1)S(1)} %collective-permute-done.3.refs_4_.refs_12_), channel_id=1, source_target_pairs={{0,224},{32,0},{64,32},{96,64},{128,96},{160,128},{192,160},{224,1... | collective-permute-start | bytes 786440 | tf_op jit(solution)/shard_map/ppermute | solution.py:197
  32.2 6.3 %collective-permute-start.6 = (bf16[128,512]{1,0:T(8,128)(2,1)S(1)}, bf16[128,512]{1,0:T(8,128)(2,1)S(1)}, u32[]{:S(2)}, u32[]{:S(2)}) collective-permute-start(bf16[128,512]{1,0:T(8,128)(2,1)S(1)} %slice.24), channel_id=1, source_target_pairs={{0,32},{32,64},{64,96},{96,128},{128,160},{160,192},{192,224},{224... | collective-permute-start | bytes 393224 | tf_op jit(solution)/shard_map/ppermute | solution.py:197
  32.3 6.1 %collective-permute-start.7 = (bf16[128,512]{1,0:T(8,128)(2,1)S(1)}, bf16[128,512]{1,0:T(8,128)(2,1)S(1)}, u32[]{:S(2)}, u32[]{:S(2)}) collective-permute-start(bf16[128,512]{1,0:T(8,128)(2,1)S(1)} %slice.25), channel_id=1, source_target_pairs={{0,224},{32,0},{64,32},{96,64},{128,96},{160,128},{192,160},{224,1... | collective-permute-start | bytes 393224 | tf_op jit(solution)/shard_map/ppermute | solution.py:197
  51.0 30.4 %all-to-all-start = ((bf16[8,128,512]{2,1,0:T(8,128)(2,1)}), bf16[8,128,512]{2,1,0:T(8,128)(2,1)}, u32[]{:S(2)}, u32[]{:S(2)}) async-start(bf16[8,128,512]{2,1,0:T(8,128)(2,1)} %get-tuple-element.62), calls=%async_computation | async-start | bytes 2097152 | tf_op jit(solution)/shard_map/all_to_all | solution.py:315
  55.3 16.1 %collective-permute-start.10 = (bf16[2,1024,128]{2,1,0:T(8,128)(2,1)}, bf16[2,1024,128]{2,1,0:T(8,128)(2,1)S(1)}, u32[]{:S(2)}, u32[]{:S(2)}) collective-permute-start(bf16[2,1024,128]{2,1,0:T(8,128)(2,1)} %get-tuple-element.58), channel_id=1, source_target_pairs={{0,4},{1,5},{2,6},{3,7},{4,0},{5,1},{6,2},{7,3},{8,12},{9,13},{10,... | collective-permute-start | bytes 1572872 | tf_op jit(solution)/shard_map/ppermute | solution.py:217
  71.3 50.2 %copy-start.2 = (bf16[128,512]{1,0:T(8,128)(2,1)S(1)}, bf16[128,512]{1,0:T(8,128)(2,1)}, u32[]{:S(2)}) copy-start(bf16[128,512]{1,0:T(8,128)(2,1)} %get-tuple-element.80) | copy-start | bytes 393220
  71.3 61.3 %copy-start.3 = (bf16[128,512]{1,0:T(8,128)(2,1)S(1)}, bf16[128,512]{1,0:T(8,128)(2,1)}, u32[]{:S(2)}) copy-start(bf16[128,512]{1,0:T(8,128)(2,1)} %get-tuple-element.82) | copy-start | bytes 393220
  71.4 8.8 %collective-permute-start.13 = (bf16[128,512]{1,0:T(8,128)(2,1)}, bf16[128,512]{1,0:T(8,128)(2,1)S(1)}, u32[]{:S(2)}, u32[]{:S(2)}) collective-permute-start(bf16[128,512]{1,0:T(8,128)(2,1)} %get-tuple-element.63), channel_id=1, source_target_pairs={{0,32},{32,64},{64,96},{96,128},{128,160},{160,192},{192,224},{224... | collective-permute-start | bytes 393224 | tf_op jit(solution)/shard_map/ppermute | solution.py:197
  73.0 7.1 %collective-permute-start.14 = (bf16[128,512]{1,0:T(8,128)(2,1)}, bf16[128,512]{1,0:T(8,128)(2,1)S(1)}, u32[]{:S(2)}, u32[]{:S(2)}) collective-permute-start(bf16[128,512]{1,0:T(8,128)(2,1)} %get-tuple-element.64), channel_id=1, source_target_pairs={{0,224},{32,0},{64,32},{96,64},{128,96},{160,128},{192,160},{224,1... | collective-permute-start | bytes 393224 | tf_op jit(solution)/shard_map/ppermute | solution.py:197
  74.7 23.3 %collective-permute-start.11 = (bf16[3,1024,128]{2,1,0:T(8,128)(2,1)}, bf16[3,1024,128]{2,1,0:T(8,128)(2,1)S(1)}, u32[]{:S(2)}, u32[]{:S(2)}) collective-permute-start(bf16[3,1024,128]{2,1,0:T(8,128)(2,1)} %pad_maximum_fusion), channel_id=1, source_target_pairs={{0,1},{1,0},{2,3},{3,2},{4,5},{5,4},{6,7},{7,6},{8,9},{9,8},{10,11... | collective-permute-start | bytes 2359304 | tf_op jit(solution)/shard_map/ppermute | solution.py:217
  82.7 7.6 %collective-permute-start.17 = (bf16[128,512]{1,0:T(8,128)(2,1)S(1)}, bf16[128,512]{1,0:T(8,128)(2,1)S(1)}, u32[]{:S(2)}, u32[]{:S(2)}) collective-permute-start(bf16[128,512]{1,0:T(8,128)(2,1)S(1)} %reduce_sum.21), channel_id=1, source_target_pairs={{0,6},{1,7},{2,0},{3,1},{4,2},{5,3},{6,4},{7,5},{8,14},{9,15},{10,... | collective-permute-start | bytes 393224 | tf_op jit(solution)/shard_map/ppermute | solution.py:217
  83.7 9.5 %collective-permute-start.16 = (bf16[128,512]{1,0:T(8,128)(2,1)S(1)}, bf16[128,512]{1,0:T(8,128)(2,1)S(1)}, u32[]{:S(2)}, u32[]{:S(2)}) collective-permute-start(bf16[128,512]{1,0:T(8,128)(2,1)S(1)} %reduce_sum.21), channel_id=1, source_target_pairs={{0,4},{1,5},{2,6},{3,7},{4,0},{5,1},{6,2},{7,3},{8,12},{9,13},{10,... | collective-permute-start | bytes 393224 | tf_op jit(solution)/shard_map/ppermute | solution.py:217
  85.7 7.4 %collective-permute-start.15 = (bf16[128,512]{1,0:T(8,128)(2,1)S(1)}, bf16[128,512]{1,0:T(8,128)(2,1)S(1)}, u32[]{:S(2)}, u32[]{:S(2)}) collective-permute-start(bf16[128,512]{1,0:T(8,128)(2,1)S(1)} %reduce_sum.21), channel_id=1, source_target_pairs={{0,2},{1,3},{2,4},{3,5},{4,6},{5,7},{6,0},{7,1},{8,10},{9,11},{10,... | collective-permute-start | bytes 393224 | tf_op jit(solution)/shard_map/ppermute | solution.py:217
  88.8 6.3 %collective-permute-start.18 = (bf16[128,512]{1,0:T(8,128)(2,1)S(1)}, bf16[128,512]{1,0:T(8,128)(2,1)S(1)}, u32[]{:S(2)}, u32[]{:S(2)}) collective-permute-start(bf16[128,512]{1,0:T(8,128)(2,1)S(1)} %add_convert_fusion.7), channel_id=1, source_target_pairs={{0,32},{32,64},{64,96},{96,128},{128,160},{160,192},{192,224},{224... | collective-permute-start | bytes 393224 | tf_op jit(solution)/shard_map/ppermute | solution.py:197
  90.3 5.3 %collective-permute-start.19 = (bf16[128,512]{1,0:T(8,128)(2,1)S(1)}, bf16[128,512]{1,0:T(8,128)(2,1)S(1)}, u32[]{:S(2)}, u32[]{:S(2)}) collective-permute-start(bf16[128,512]{1,0:T(8,128)(2,1)S(1)} %add_convert_fusion.6), channel_id=1, source_target_pairs={{0,224},{32,0},{64,32},{96,64},{128,96},{160,128},{192,160},{224,1... | collective-permute-start | bytes 393224 | tf_op jit(solution)/shard_map/ppermute | solution.py:197
  95.6 2.3 %collective-permute-start.20 = (bf16[512,512]{1,0:T(8,128)(2,1)S(1)}, bf16[512,512]{1,0:T(8,128)(2,1)S(1)}, u32[]{:S(2)}, u32[]{:S(2)}) collective-permute-start(bf16[512,512]{1,0:T(8,128)(2,1)S(1)} %pad_maximum_fusion.1.refs_6_), channel_id=1, source_target_pairs={{0,1},{1,0},{2,3},{3,2},{4,5},{5,4},{6,7},{7,6},{8,9},{9,8},{10,11... | collective-permute-start | bytes 1572872 | tf_op jit(solution)/shard_map/ppermute | solution.py:217
  95.7 2.3 %collective-permute-start.12 = (bf16[1024,128]{1,0:T(8,128)(2,1)S(1)}, bf16[1024,128]{1,0:T(8,128)(2,1)S(1)}, u32[]{:S(2)}, u32[]{:S(2)}) collective-permute-start(bf16[1024,128]{1,0:T(8,128)(2,1)S(1)} %slice_bitcast_fusion), channel_id=1, source_target_pairs={{0,1},{1,0},{2,3},{3,2},{4,5},{5,4},{6,7},{7,6},{8,9},{9,8},{10,11... | collective-permute-start | bytes 786440 | tf_op jit(solution)/shard_map/ppermute | solution.py:217
  99.2 11.6 %collective-permute-start.21 = (bf16[256,512]{1,0:T(8,128)(2,1)S(1)}, bf16[256,512]{1,0:T(8,128)(2,1)S(1)}, u32[]{:S(2)}, u32[]{:S(2)}) collective-permute-start(bf16[256,512]{1,0:T(8,128)(2,1)S(1)} %get-tuple-element.72), channel_id=1, source_target_pairs={{0,8},{1,9},{2,10},{3,11},{4,12},{5,13},{6,14},{7,15},{8,16},{9,17... | collective-permute-start | bytes 786440 | tf_op jit(solution)/shard_map/ppermute | solution.py:217
  100.8 14.8 %collective-permute-start.22 = (bf16[256,512]{1,0:T(8,128)(2,1)S(1)}, bf16[256,512]{1,0:T(8,128)(2,1)S(1)}, u32[]{:S(2)}, u32[]{:S(2)}) collective-permute-start(bf16[256,512]{1,0:T(8,128)(2,1)S(1)} %get-tuple-element.73), channel_id=1, source_target_pairs={{0,16},{1,17},{2,18},{3,19},{4,20},{5,21},{6,22},{7,23},{8,24},{9,... | collective-permute-start | bytes 786440 | tf_op jit(solution)/shard_map/ppermute | solution.py:217
  103.7 11.9 %collective-permute-start.23 = (bf16[256,512]{1,0:T(8,128)(2,1)S(1)}, bf16[256,512]{1,0:T(8,128)(2,1)S(1)}, u32[]{:S(2)}, u32[]{:S(2)}) collective-permute-start(bf16[256,512]{1,0:T(8,128)(2,1)S(1)} %get-tuple-element.74), channel_id=1, source_target_pairs={{0,24},{1,25},{2,26},{3,27},{4,28},{5,29},{6,30},{7,31},{8,0},{9,1... | collective-permute-start | bytes 786440 | tf_op jit(solution)/shard_map/ppermute | solution.py:217
  106.0 10.5 %collective-permute-start.25 = (bf16[128,512]{1,0:T(8,128)(2,1)S(1)}, bf16[128,512]{1,0:T(8,128)(2,1)S(1)}, u32[]{:S(2)}, u32[]{:S(2)}) collective-permute-start(bf16[128,512]{1,0:T(8,128)(2,1)S(1)} %add_convert_fusion.4), channel_id=1, source_target_pairs={{0,224},{32,0},{64,32},{96,64},{128,96},{160,128},{192,160},{224,1... | collective-permute-start | bytes 393224 | tf_op jit(solution)/shard_map/ppermute | solution.py:197
  110.7 6.3 %collective-permute-start.24 = (bf16[128,512]{1,0:T(8,128)(2,1)S(1)}, bf16[128,512]{1,0:T(8,128)(2,1)S(1)}, u32[]{:S(2)}, u32[]{:S(2)}) collective-permute-start(bf16[128,512]{1,0:T(8,128)(2,1)S(1)} %add_convert_fusion.5), channel_id=1, source_target_pairs={{0,32},{32,64},{64,96},{96,128},{128,160},{160,192},{192,224},{224... | collective-permute-start | bytes 393224 | tf_op jit(solution)/shard_map/ppermute | solution.py:197
  117.0 16.8 %all-to-all-start.1 = ((bf16[8,32,512]{2,1,0:T(8,128)(2,1)}), bf16[8,32,512]{2,1,0:T(8,128)(2,1)S(1)}, u32[]{:S(2)}, u32[]{:S(2)}) async-start(bf16[8,32,512]{2,1,0:T(8,128)(2,1)} %bitcast.11), calls=%async_computation.1 | async-start | bytes 524288 | tf_op jit(solution)/shard_map/all_to_all | solution.py:345
  121.5 11.1 %collective-permute-start.26 = (bf16[128,512]{1,0:T(8,128)(2,1)S(1)}, bf16[128,512]{1,0:T(8,128)(2,1)S(1)}, u32[]{:S(2)}, u32[]{:S(2)}) collective-permute-start(bf16[128,512]{1,0:T(8,128)(2,1)S(1)} %add_convert_fusion.3), channel_id=1, source_target_pairs={{0,32},{32,64},{64,96},{96,128},{128,160},{160,192},{192,224},{224... | collective-permute-start | bytes 393224 | tf_op jit(solution)/shard_map/ppermute | solution.py:197
  (9 other events, 116.4 us)

commit v5 on v4

--- a/solution.py
+++ b/solution.py
@@ -322,16 +322,15 @@
     moved[2], parts[half] = lax.optimization_barrier((moved[2], parts[half]))
     last_others = along_dp(moved[2][1], 0, 0, 1)
 
-    rising, falling = along_ctx(parts[half], 1), along_ctx(parts[1 - half], -1)
-    got, rising, falling = lax.optimization_barrier((got, rising, falling))
+    rising = along_ctx(parts[half], 1)
+    got, rising = lax.optimization_barrier((got, rising))
     grad_value = jnp.sum(got.astype(jnp.float32), axis=0).astype(jnp.bfloat16)
-    rising, falling = plus(rising, parts[half - 1]), plus(falling, parts[2 - half])
-    rising, falling = along_ctx(rising, 1), along_ctx(falling, -1)
+    rising, falling = along_ctx(plus(rising, parts[half - 1]), 1), along_ctx(parts[1 - half], -1)
 
     near = jnp.concatenate(over_x([grad_value] * N_X), 0)
     near, rising, falling = lax.optimization_barrier((near, rising, falling))
     far = along_dp(near, 0, 0, 1)
-    rising, falling = plus(rising, parts[half - 2]), plus(falling, parts[3 - half])
+    rising, falling = plus(rising, parts[half - 2]), plus(falling, parts[2 - half])
     rising, falling = along_ctx(rising, 1), along_ctx(falling, -1)
     own, sent = weight_terms(moved, others, last_others, near, far)
     total = own
@@ -339,7 +338,8 @@
         total = total + along_dp(sent[d - 1], d if d < 3 else -1, 0, 0).astype(jnp.float32)
     total = total.astype(jnp.bfloat16).reshape(n_ctx, -1, near.shape[1])
     total, rising, falling = lax.optimization_barrier((total, rising, falling))
-    rising = along_ctx(plus(rising, parts[half - 3]), 1)
+    rising, falling = plus(rising, parts[half - 3]), plus(falling, parts[3 - half])
+    rising, falling = along_ctx(rising, 1), along_ctx(falling, -1)
 
     grad_key = plus(plus(rising, falling), parts[0])
     last = lax.all_to_all(total, "ctx", split_axis=0, concat_axis=0, tiled=True)

time: 135 us -> 135 us (level); the launches traced: 134 us -> 132 us
  starting transfers between devices: 53.2 us -> 49.1 us
  waiting for transfers between devices: 39.1 us -> 42.1 us
    ppermute x12, waiting for transfers between devices: 6.57 us -> 9.86 us  [along_dp(): return lax.ppermute(a, 'dp', pairs)]
    ppermute x15, starting transfers between devices: 28.4 us -> 25.4 us  [along_ctx(): return lax.ppermute(a, 'ctx', [(i, (i + far) % n) for i in range(n)])]
  transfers between devices with their start and end apart: 29 -> 29, of which waited for: 14 -> 15; matrix products, arithmetic and copies ran while one was open for 6% -> 6% of each run, Pallas kernels for 13% -> 13%
where the time goes in v5:
time: 135 us; the launch traced here: 132 us
  starting transfers between devices  49.1 us (36%)
  waiting for transfers between devices  42.1 us (31%)
  Pallas kernels  30.5 us (23%)
  other arithmetic  9.07 us (7%)
    ppermute x15, waiting for transfers between devices, along_ctx(): return lax.ppermute(a, 'ctx', [(i, (i + far) % n) for i in range(n)])  30.7 us
    ppermute x15, starting transfers between devices, along_ctx(): return lax.ppermute(a, 'ctx', [(i, (i + far) % n) for i in range(n)])  25.4 us
    ppermute x12, starting transfers between devices, along_dp(): return lax.ppermute(a, 'dp', pairs)  16 us
    pallas_call x1, Pallas kernels, out_and_grads(): pl.pallas_call(grads_kernel, grid=(KV_HEADS,), in_specs=[wide, wide, squa...  12.6 us
    pallas_call x1, Pallas kernels, probs_and_dv(): pl.pallas_call(probs_kernel, grid=(KV_HEADS,), in_specs=[pl.BlockSpec(mem...  11.8 us
    ppermute x12, waiting for transfers between devices, along_dp(): return lax.ppermute(a, 'dp', pairs)  9.86 us
    pallas_call x1, Pallas kernels, columns_for_x(): pl.pallas_call(turn_kernel, grid_spec=pltpu.PrefetchScalarGridSpec(num_sc...  4.82 us
    all_to_all x1, starting transfers between devices, on_device(): got = lax.all_to_all(dv, 'ctx', split_axis=0, concat_axis=0, tiled=True)  4.26 us
  transfers between devices with their start and end apart: 29, of which 15 were waited for; matrix products, arithmetic and copies ran while one was open for 6% of the time, Pallas kernels for 13%

profile of v5, /device:TPU:2, one launch (start us, length us, event | category | flops | bytes accessed | tf_op | source)
XLA Modules:
  0.0 132.5 jit_solution(5891881426695373687)
XLA Ops:
  1.6 5.9 %collective-permute-start.1 = (bf16[128,1024]{1,0:T(8,128)(2,1)S(1)}, bf16[128,1024]{1,0:T(8,128)(2,1)S(1)}, u32[]{:S(2)}, u32[]{:S(2)}) collective-permute-start(bf16[128,1024]{1,0:T(8,128)(2,1)S(1)} %pad_maximum_fusion.2.refs_0_.refs_8_), channel_id=1, source_target_pairs={{0,224},{32,0},{64,32},{96,64},{128,96},{160,128},{192,160},{224,1... | collective-permute-start | bytes 786440 | tf_op jit(solution)/shard_map/ppermute | solution.py:197
  8.2 4.8 %shard_map.111 = (bf16[2,1024,128]{2,1,0:T(8,128)(2,1)}, bf16[2,1024,128]{2,1,0:T(8,128)(2,1)}, bf16[2,1024,128]{2,1,0:T(8,128)(2,1)}, bf16[2,1024,128]{2,1,0:T(8,128)(2,1)}) custom-call(s32[3]{0:T(128)} %pad_add_fusion.where, bf16[128,8192]{1,0:T(8,128)(2,1)} %bitcast.15, bf16[128,8192]{1,0:T(8,128)(2,1)} %bitcast.16, bf16[128,8192]{1,0:T(8,128)(2,1)} %bitcast.17, ...), custom_call_target="tpu_custom_call" | custom-call | bytes 4194304 | tf_op jit(solution)/shard_map/pallas_call | solution.py:244
  13.1 3.4 %collective-permute-done.refs_1_.refs_9_ = bf16[128,1024]{1,0:T(8,128)(2,1)S(1)} collective-permute-done((bf16[128,1024]{1,0:T(8,128)(2,1)S(1)}, bf16[128,1024]{1,0:T(8,128)(2,1)S(1)}, u32[]{:S(2)}, u32[]{:S(2)}) %collective-permute-start) | collective-permute-done | bytes 262176 | tf_op jit(solution)/shard_map/ppermute | solution.py:197
  16.6 3.2 %collective-permute-start.3 = (bf16[128,1024]{1,0:T(8,128)(2,1)S(1)}, bf16[128,1024]{1,0:T(8,128)(2,1)S(1)}, u32[]{:S(2)}, u32[]{:S(2)}) collective-permute-start(bf16[128,1024]{1,0:T(8,128)(2,1)S(1)} %collective-permute-done.1.refs_2_.refs_10_), channel_id=1, source_target_pairs={{0,224},{32,0},{64,32},{96,64},{128,96},{160,128},{192,160},{224,1... | collective-permute-start | bytes 786440 | tf_op jit(solution)/shard_map/ppermute | solution.py:197
  19.8 1.5 %collective-permute-start.8 = (bf16[2,1024,128]{2,1,0:T(8,128)(2,1)}, bf16[2,1024,128]{2,1,0:T(8,128)(2,1)S(1)}, u32[]{:S(2)}, u32[]{:S(2)}) collective-permute-start(bf16[2,1024,128]{2,1,0:T(8,128)(2,1)} %get-tuple-element.46), channel_id=1, source_target_pairs={{0,2},{1,3},{2,4},{3,5},{4,6},{5,7},{6,0},{7,1},{8,10},{9,11},{10,... | collective-permute-start | bytes 1572872 | tf_op jit(solution)/shard_map/ppermute | solution.py:217
  21.8 2.8 %collective-permute-done.2.refs_3_.refs_11_ = bf16[128,1024]{1,0:T(8,128)(2,1)S(1)} collective-permute-done((bf16[128,1024]{1,0:T(8,128)(2,1)S(1)}, bf16[128,1024]{1,0:T(8,128)(2,1)S(1)}, u32[]{:S(2)}, u32[]{:S(2)}) %collective-permute-start.2) | collective-permute-done | bytes 262176 | tf_op jit(solution)/shard_map/ppermute | solution.py:197
  24.6 3.2 %collective-permute-start.5 = (bf16[128,1024]{1,0:T(8,128)(2,1)S(1)}, bf16[128,1024]{1,0:T(8,128)(2,1)S(1)}, u32[]{:S(2)}, u32[]{:S(2)}) collective-permute-start(bf16[128,1024]{1,0:T(8,128)(2,1)S(1)} %collective-permute-done.3.refs_4_.refs_12_), channel_id=1, source_target_pairs={{0,224},{32,0},{64,32},{96,64},{128,96},{160,128},{192,160},{224,1... | collective-permute-start | bytes 786440 | tf_op jit(solution)/shard_map/ppermute | solution.py:197
  27.9 4.3 %collective-permute-done.4.refs_5_.refs_13_ = bf16[128,1024]{1,0:T(8,128)(2,1)S(1)} collective-permute-done((bf16[128,1024]{1,0:T(8,128)(2,1)S(1)}, bf16[128,1024]{1,0:T(8,128)(2,1)S(1)}, u32[]{:S(2)}, u32[]{:S(2)}) %collective-permute-start.4) | collective-permute-done | bytes 262176 | tf_op jit(solution)/shard_map/ppermute | solution.py:197
  32.3 3.3 %collective-permute-start.7 = (bf16[128,512]{1,0:T(8,128)(2,1)S(1)}, bf16[128,512]{1,0:T(8,128)(2,1)S(1)}, u32[]{:S(2)}, u32[]{:S(2)}) collective-permute-start(bf16[128,512]{1,0:T(8,128)(2,1)S(1)} %slice.25), channel_id=1, source_target_pairs={{0,224},{32,0},{64,32},{96,64},{128,96},{160,128},{192,160},{224,1... | collective-permute-start | bytes 393224 | tf_op jit(solution)/shard_map/ppermute | solution.py:197
  35.6 2.8 %collective-permute-done.6.refs_7_ = bf16[128,512]{1,0:T(8,128)(2,1)S(1)} collective-permute-done((bf16[128,512]{1,0:T(8,128)(2,1)S(1)}, bf16[128,512]{1,0:T(8,128)(2,1)S(1)}, u32[]{:S(2)}, u32[]{:S(2)}) %collective-permute-start.6) | collective-permute-done | bytes 131104 | tf_op jit(solution)/shard_map/ppermute | solution.py:197
  39.1 11.8 %shard_map.112 = (bf16[4,1024,1024]{2,1,0:T(8,128)(2,1)}, bf16[8,128,512]{2,1,0:T(8,128)(2,1)}) custom-call(s32[1,8]{1,0:T(1,128)} %lens.1, s32[1,8]{1,0:T(1,128)} %prefix.1, s32[1,16]{1,0:T(1,128)} %order.1, bf16[128,4096]{1,0:T(8,128)(2,1)} %bitcast.25, bf16[128,4096]{1,0:T(8,128)(2,1)} %bitcast.27, bf16[128,1024]{1,0:T(8,128)(2,1)} %copy-done.1, ...), custom_call_target="tpu_custom_call" | custom-call | flops 2147483648 | bytes 12582912 | tf_op jit(solution)/shard_map/pallas_call | solution.py:150
  51.0 4.3 %all-to-all-start = ((bf16[8,128,512]{2,1,0:T(8,128)(2,1)}), bf16[8,128,512]{2,1,0:T(8,128)(2,1)}, u32[]{:S(2)}, u32[]{:S(2)}) async-start(bf16[8,128,512]{2,1,0:T(8,128)(2,1)} %get-tuple-element.61), calls=%async_computation | async-start | bytes 2097152 | tf_op jit(solution)/shard_map/all_to_all | solution.py:315
  55.2 2.4 %collective-permute-start.10 = (bf16[2,1024,128]{2,1,0:T(8,128)(2,1)}, bf16[2,1024,128]{2,1,0:T(8,128)(2,1)S(1)}, u32[]{:S(2)}, u32[]{:S(2)}) collective-permute-start(bf16[2,1024,128]{2,1,0:T(8,128)(2,1)} %get-tuple-element.57), channel_id=1, source_target_pairs={{0,4},{1,5},{2,6},{3,7},{4,0},{5,1},{6,2},{7,3},{8,12},{9,13},{10,... | collective-permute-start | bytes 1572872 | tf_op jit(solution)/shard_map/ppermute | solution.py:217
  58.7 12.6 %shard_map.113 = (bf16[128,4096]{1,0:T(8,128)(2,1)}, bf16[128,4096]{1,0:T(8,128)(2,1)}, bf16[128,512]{1,0:T(8,128)(2,1)}, bf16[128,512]{1,0:T(8,128)(2,1)}, bf16...) custom-call(bf16[128,4096]{1,0:T(8,128)(2,1)} %bitcast.26, ...), custom_call_target="tpu_custom_call" | custom-call | flops 4294967296 | bytes 14680064 | tf_op jit(solution)/shard_map/pallas_call | solution.py:176
  71.3 1.7 %collective-permute-start.13 = (bf16[128,512]{1,0:T(8,128)(2,1)}, bf16[128,512]{1,0:T(8,128)(2,1)S(1)}, u32[]{:S(2)}, u32[]{:S(2)}) collective-permute-start(bf16[128,512]{1,0:T(8,128)(2,1)} %get-tuple-element.62), channel_id=1, source_target_pairs={{0,32},{32,64},{64,96},{96,128},{128,160},{160,192},{192,224},{224... | collective-permute-start | bytes 393224 | tf_op jit(solution)/shard_map/ppermute | solution.py:197
  73.0 1.6 %collective-permute-start.18 = (bf16[128,512]{1,0:T(8,128)(2,1)}, bf16[128,512]{1,0:T(8,128)(2,1)S(1)}, u32[]{:S(2)}, u32[]{:S(2)}) collective-permute-start(bf16[128,512]{1,0:T(8,128)(2,1)} %get-tuple-element.66), channel_id=1, source_target_pairs={{0,224},{32,0},{64,32},{96,64},{128,96},{160,128},{192,160},{224,1... | collective-permute-start | bytes 393224 | tf_op jit(solution)/shard_map/ppermute | solution.py:197
  74.7 5.5 %collective-permute-done.13 = bf16[128,512]{1,0:T(8,128)(2,1)S(1)} collective-permute-done((bf16[128,512]{1,0:T(8,128)(2,1)}, bf16[128,512]{1,0:T(8,128)(2,1)S(1)}, u32[]{:S(2)}, u32[]{:S(2)}) %collective-permute-start.13) | collective-permute-done | bytes 131104 | tf_op jit(solution)/shard_map/ppermute | solution.py:197
  80.1 1.2 all-to-all-done
  81.3 1.4 %reduce_sum.21 = bf16[128,512]{1,0:T(8,128)(2,1)S(1)} reduce(bf16[8,128,512]{2,1,0:T(8,128)(2,1)} %all-to-all-done, bf16[]{:T(256)} %constant.10.clone.1), dimensions={0}, to_apply=%region_0.0 | reduce | flops 458752 | bytes 1179650 | tf_op jit(solution)/shard_map/reduce_sum | solution.py:327
  83.7 2.1 %collective-permute-start.15 = (bf16[128,512]{1,0:T(8,128)(2,1)S(1)}, bf16[128,512]{1,0:T(8,128)(2,1)S(1)}, u32[]{:S(2)}, u32[]{:S(2)}) collective-permute-start(bf16[128,512]{1,0:T(8,128)(2,1)S(1)} %reduce_sum.21), channel_id=1, source_target_pairs={{0,4},{1,5},{2,6},{3,7},{4,0},{5,1},{6,2},{7,3},{8,12},{9,13},{10,... | collective-permute-start | bytes 393224 | tf_op jit(solution)/shard_map/ppermute | solution.py:217
  85.7 2.1 %collective-permute-start.14 = (bf16[128,512]{1,0:T(8,128)(2,1)S(1)}, bf16[128,512]{1,0:T(8,128)(2,1)S(1)}, u32[]{:S(2)}, u32[]{:S(2)}) collective-permute-start(bf16[128,512]{1,0:T(8,128)(2,1)S(1)} %reduce_sum.21), channel_id=1, source_target_pairs={{0,2},{1,3},{2,4},{3,5},{4,6},{5,7},{6,0},{7,1},{8,10},{9,11},{10,... | collective-permute-start | bytes 393224 | tf_op jit(solution)/shard_map/ppermute | solution.py:217
  91.3 3.8 %collective-permute-done.17 = bf16[128,512]{1,0:T(8,128)(2,1)S(1)} collective-permute-done((bf16[128,512]{1,0:T(8,128)(2,1)S(1)}, bf16[128,512]{1,0:T(8,128)(2,1)S(1)}, u32[]{:S(2)}, u32[]{:S(2)}) %collective-permute-start.17) | collective-permute-done | bytes 131104 | tf_op jit(solution)/shard_map/ppermute | solution.py:197
  95.7 1.7 %collective-permute-done.12.refs_5_ = bf16[1024,128]{1,0:T(8,128)(2,1)S(1)} collective-permute-done((bf16[1024,128]{1,0:T(8,128)(2,1)S(1)}, bf16[1024,128]{1,0:T(8,128)(2,1)S(1)}, u32[]{:S(2)}, u32[]{:S(2)}) %collective-permute-start.12) | collective-permute-done | bytes 262176 | tf_op jit(solution)/shard_map/ppermute | solution.py:217
  97.4 1.2 shard_map.114
  98.6 1.7 %collective-permute-start.20 = (bf16[256,512]{1,0:T(8,128)(2,1)S(1)}, bf16[256,512]{1,0:T(8,128)(2,1)S(1)}, u32[]{:S(2)}, u32[]{:S(2)}) collective-permute-start(bf16[256,512]{1,0:T(8,128)(2,1)S(1)} %get-tuple-element.69), channel_id=1, source_target_pairs={{0,8},{1,9},{2,10},{3,11},{4,12},{5,13},{6,14},{7,15},{8,16},{9,17... | collective-permute-start | bytes 786440 | tf_op jit(solution)/shard_map/ppermute | solution.py:217
  100.3 2.9 %collective-permute-start.21 = (bf16[256,512]{1,0:T(8,128)(2,1)S(1)}, bf16[256,512]{1,0:T(8,128)(2,1)S(1)}, u32[]{:S(2)}, u32[]{:S(2)}) collective-permute-start(bf16[256,512]{1,0:T(8,128)(2,1)S(1)} %get-tuple-element.70), channel_id=1, source_target_pairs={{0,16},{1,17},{2,18},{3,19},{4,20},{5,21},{6,22},{7,23},{8,24},{9,... | collective-permute-start | bytes 786440 | tf_op jit(solution)/shard_map/ppermute | solution.py:217
  103.2 1.3 %collective-permute-start.22 = (bf16[256,512]{1,0:T(8,128)(2,1)S(1)}, bf16[256,512]{1,0:T(8,128)(2,1)S(1)}, u32[]{:S(2)}, u32[]{:S(2)}) collective-permute-start(bf16[256,512]{1,0:T(8,128)(2,1)S(1)} %get-tuple-element.71), channel_id=1, source_target_pairs={{0,24},{1,25},{2,26},{3,27},{4,28},{5,29},{6,30},{7,31},{8,0},{9,1... | collective-permute-start | bytes 786440 | tf_op jit(solution)/shard_map/ppermute | solution.py:217
  106.7 2.1 %collective-permute-start.23 = (bf16[128,512]{1,0:T(8,128)(2,1)S(1)}, bf16[128,512]{1,0:T(8,128)(2,1)S(1)}, u32[]{:S(2)}, u32[]{:S(2)}) collective-permute-start(bf16[128,512]{1,0:T(8,128)(2,1)S(1)} %add_convert_fusion.6), channel_id=1, source_target_pairs={{0,32},{32,64},{64,96},{96,128},{128,160},{160,192},{192,224},{224... | collective-permute-start | bytes 393224 | tf_op jit(solution)/shard_map/ppermute | solution.py:197
  108.8 6.3 %collective-permute-done.21 = bf16[256,512]{1,0:T(8,128)(2,1)S(1)} collective-permute-done((bf16[256,512]{1,0:T(8,128)(2,1)S(1)}, bf16[256,512]{1,0:T(8,128)(2,1)S(1)}, u32[]{:S(2)}, u32[]{:S(2)}) %collective-permute-start.21) | collective-permute-done | bytes 262176 | tf_op jit(solution)/shard_map/ppermute | solution.py:217
  115.9 3.4 %all-to-all-start.1 = ((bf16[8,32,512]{2,1,0:T(8,128)(2,1)}), bf16[8,32,512]{2,1,0:T(8,128)(2,1)S(1)}, u32[]{:S(2)}, u32[]{:S(2)}) async-start(bf16[8,32,512]{2,1,0:T(8,128)(2,1)} %bitcast.11), calls=%async_computation.1 | async-start | bytes 524288 | tf_op jit(solution)/shard_map/all_to_all | solution.py:345
  119.4 3.2 %collective-permute-start.26 = (bf16[128,512]{1,0:T(8,128)(2,1)S(1)}, bf16[128,512]{1,0:T(8,128)(2,1)S(1)}, u32[]{:S(2)}, u32[]{:S(2)}) collective-permute-start(bf16[128,512]{1,0:T(8,128)(2,1)S(1)} %add_convert_fusion.3), channel_id=1, source_target_pairs={{0,224},{32,0},{64,32},{96,64},{128,96},{160,128},{192,160},{224,1... | collective-permute-start | bytes 393224 | tf_op jit(solution)/shard_map/ppermute | solution.py:197
  122.8 7.0 %collective-permute-done.26 = bf16[128,512]{1,0:T(8,128)(2,1)S(1)} collective-permute-done((bf16[128,512]{1,0:T(8,128)(2,1)S(1)}, bf16[128,512]{1,0:T(8,128)(2,1)S(1)}, u32[]{:S(2)}, u32[]{:S(2)}) %collective-permute-start.26) | collective-permute-done | bytes 131104 | tf_op jit(solution)/shard_map/ppermute | solution.py:197
  (75 shorter events, 14.9 us)
Async XLA Ops:
  1.6 11.5 %collective-permute-start.1 = (bf16[128,1024]{1,0:T(8,128)(2,1)S(1)}, bf16[128,1024]{1,0:T(8,128)(2,1)S(1)}, u32[]{:S(2)}, u32[]{:S(2)}) collective-permute-start(bf16[128,1024]{1,0:T(8,128)(2,1)S(1)} %pad_maximum_fusion.2.refs_0_.refs_8_), channel_id=1, source_target_pairs={{0,224},{32,0},{64,32},{96,64},{128,96},{160,128},{192,160},{224,1... | collective-permute-start | bytes 786440 | tf_op jit(solution)/shard_map/ppermute | solution.py:197
  7.6 9.0 %collective-permute-start = (bf16[128,1024]{1,0:T(8,128)(2,1)S(1)}, bf16[128,1024]{1,0:T(8,128)(2,1)S(1)}, u32[]{:S(2)}, u32[]{:S(2)}) collective-permute-start(bf16[128,1024]{1,0:T(8,128)(2,1)S(1)} %pad_maximum_fusion.2.refs_0_.refs_8_), channel_id=1, source_target_pairs={{0,32},{32,64},{64,96},{96,128},{128,160},{160,192},{192,224},{224... | collective-permute-start | bytes 786440 | tf_op jit(solution)/shard_map/ppermute | solution.py:197
  13.0 44.6 %copy-start = (bf16[2,1024,128]{2,1,0:T(8,128)(2,1)S(1)}, bf16[2,1024,128]{2,1,0:T(8,128)(2,1)}, u32[]{:S(2)}) copy-start(bf16[2,1024,128]{2,1,0:T(8,128)(2,1)} %get-tuple-element.50.refs_0_) | copy-start | bytes 1572868
  16.5 8.1 %collective-permute-start.2 = (bf16[128,1024]{1,0:T(8,128)(2,1)S(1)}, bf16[128,1024]{1,0:T(8,128)(2,1)S(1)}, u32[]{:S(2)}, u32[]{:S(2)}) collective-permute-start(bf16[128,1024]{1,0:T(8,128)(2,1)S(1)} %collective-permute-done.refs_1_.refs_9_), channel_id=1, source_target_pairs={{0,32},{32,64},{64,96},{96,128},{128,160},{160,192},{192,224},{224... | collective-permute-start | bytes 786440 | tf_op jit(solution)/shard_map/ppermute | solution.py:197
  16.6 8.1 %collective-permute-start.3 = (bf16[128,1024]{1,0:T(8,128)(2,1)S(1)}, bf16[128,1024]{1,0:T(8,128)(2,1)S(1)}, u32[]{:S(2)}, u32[]{:S(2)}) collective-permute-start(bf16[128,1024]{1,0:T(8,128)(2,1)S(1)} %collective-permute-done.1.refs_2_.refs_10_), channel_id=1, source_target_pairs={{0,224},{32,0},{64,32},{96,64},{128,96},{160,128},{192,160},{224,1... | collective-permute-start | bytes 786440 | tf_op jit(solution)/shard_map/ppermute | solution.py:197
  19.8 15.8 %collective-permute-start.8 = (bf16[2,1024,128]{2,1,0:T(8,128)(2,1)}, bf16[2,1024,128]{2,1,0:T(8,128)(2,1)S(1)}, u32[]{:S(2)}, u32[]{:S(2)}) collective-permute-start(bf16[2,1024,128]{2,1,0:T(8,128)(2,1)} %get-tuple-element.46), channel_id=1, source_target_pairs={{0,2},{1,3},{2,4},{3,5},{4,6},{5,7},{6,0},{7,1},{8,10},{9,11},{10,... | collective-permute-start | bytes 1572872 | tf_op jit(solution)/shard_map/ppermute | solution.py:217
  21.3 14.4 %collective-permute-start.9 = (bf16[2,1024,128]{2,1,0:T(8,128)(2,1)}, bf16[2,1024,128]{2,1,0:T(8,128)(2,1)S(1)}, u32[]{:S(2)}, u32[]{:S(2)}) collective-permute-start(bf16[2,1024,128]{2,1,0:T(8,128)(2,1)} %get-tuple-element.47), channel_id=1, source_target_pairs={{0,6},{1,7},{2,0},{3,1},{4,2},{5,3},{6,4},{7,5},{8,14},{9,15},{10,... | collective-permute-start | bytes 1572872 | tf_op jit(solution)/shard_map/ppermute | solution.py:217
  24.6 7.6 %collective-permute-start.4 = (bf16[128,1024]{1,0:T(8,128)(2,1)S(1)}, bf16[128,1024]{1,0:T(8,128)(2,1)S(1)}, u32[]{:S(2)}, u32[]{:S(2)}) collective-permute-start(bf16[128,1024]{1,0:T(8,128)(2,1)S(1)} %collective-permute-done.2.refs_3_.refs_11_), channel_id=1, source_target_pairs={{0,32},{32,64},{64,96},{96,128},{128,160},{160,192},{192,224},{224... | collective-permute-start | bytes 786440 | tf_op jit(solution)/shard_map/ppermute | solution.py:197
  24.6 7.7 %collective-permute-start.5 = (bf16[128,1024]{1,0:T(8,128)(2,1)S(1)}, bf16[128,1024]{1,0:T(8,128)(2,1)S(1)}, u32[]{:S(2)}, u32[]{:S(2)}) collective-permute-start(bf16[128,1024]{1,0:T(8,128)(2,1)S(1)} %collective-permute-done.3.refs_4_.refs_12_), channel_id=1, source_target_pairs={{0,224},{32,0},{64,32},{96,64},{128,96},{160,128},{192,160},{224,1... | collective-permute-start | bytes 786440 | tf_op jit(solution)/shard_map/ppermute | solution.py:197
  32.2 6.3 %collective-permute-start.6 = (bf16[128,512]{1,0:T(8,128)(2,1)S(1)}, bf16[128,512]{1,0:T(8,128)(2,1)S(1)}, u32[]{:S(2)}, u32[]{:S(2)}) collective-permute-start(bf16[128,512]{1,0:T(8,128)(2,1)S(1)} %slice.24), channel_id=1, source_target_pairs={{0,32},{32,64},{64,96},{96,128},{128,160},{160,192},{192,224},{224... | collective-permute-start | bytes 393224 | tf_op jit(solution)/shard_map/ppermute | solution.py:197
  32.3 6.1 %collective-permute-start.7 = (bf16[128,512]{1,0:T(8,128)(2,1)S(1)}, bf16[128,512]{1,0:T(8,128)(2,1)S(1)}, u32[]{:S(2)}, u32[]{:S(2)}) collective-permute-start(bf16[128,512]{1,0:T(8,128)(2,1)S(1)} %slice.25), channel_id=1, source_target_pairs={{0,224},{32,0},{64,32},{96,64},{128,96},{160,128},{192,160},{224,1... | collective-permute-start | bytes 393224 | tf_op jit(solution)/shard_map/ppermute | solution.py:197
  51.0 30.4 %all-to-all-start = ((bf16[8,128,512]{2,1,0:T(8,128)(2,1)}), bf16[8,128,512]{2,1,0:T(8,128)(2,1)}, u32[]{:S(2)}, u32[]{:S(2)}) async-start(bf16[8,128,512]{2,1,0:T(8,128)(2,1)} %get-tuple-element.61), calls=%async_computation | async-start | bytes 2097152 | tf_op jit(solution)/shard_map/all_to_all | solution.py:315
  55.2 16.1 %collective-permute-start.10 = (bf16[2,1024,128]{2,1,0:T(8,128)(2,1)}, bf16[2,1024,128]{2,1,0:T(8,128)(2,1)S(1)}, u32[]{:S(2)}, u32[]{:S(2)}) collective-permute-start(bf16[2,1024,128]{2,1,0:T(8,128)(2,1)} %get-tuple-element.57), channel_id=1, source_target_pairs={{0,4},{1,5},{2,6},{3,7},{4,0},{5,1},{6,2},{7,3},{8,12},{9,13},{10,... | collective-permute-start | bytes 1572872 | tf_op jit(solution)/shard_map/ppermute | solution.py:217
  71.3 48.0 %copy-start.3 = (bf16[128,512]{1,0:T(8,128)(2,1)S(1)}, bf16[128,512]{1,0:T(8,128)(2,1)}, u32[]{:S(2)}) copy-start(bf16[128,512]{1,0:T(8,128)(2,1)} %get-tuple-element.79) | copy-start | bytes 393220
  71.3 51.3 %copy-start.2 = (bf16[128,512]{1,0:T(8,128)(2,1)S(1)}, bf16[128,512]{1,0:T(8,128)(2,1)}, u32[]{:S(2)}) copy-start(bf16[128,512]{1,0:T(8,128)(2,1)} %get-tuple-element.77) | copy-start | bytes 393220
  71.3 8.8 %collective-permute-start.13 = (bf16[128,512]{1,0:T(8,128)(2,1)}, bf16[128,512]{1,0:T(8,128)(2,1)S(1)}, u32[]{:S(2)}, u32[]{:S(2)}) collective-permute-start(bf16[128,512]{1,0:T(8,128)(2,1)} %get-tuple-element.62), channel_id=1, source_target_pairs={{0,32},{32,64},{64,96},{96,128},{128,160},{160,192},{192,224},{224... | collective-permute-start | bytes 393224 | tf_op jit(solution)/shard_map/ppermute | solution.py:197
  73.0 18.2 %collective-permute-start.18 = (bf16[128,512]{1,0:T(8,128)(2,1)}, bf16[128,512]{1,0:T(8,128)(2,1)S(1)}, u32[]{:S(2)}, u32[]{:S(2)}) collective-permute-start(bf16[128,512]{1,0:T(8,128)(2,1)} %get-tuple-element.66), channel_id=1, source_target_pairs={{0,224},{32,0},{64,32},{96,64},{128,96},{160,128},{192,160},{224,1... | collective-permute-start | bytes 393224 | tf_op jit(solution)/shard_map/ppermute | solution.py:197
  74.7 22.7 %collective-permute-start.11 = (bf16[3,1024,128]{2,1,0:T(8,128)(2,1)}, bf16[3,1024,128]{2,1,0:T(8,128)(2,1)S(1)}, u32[]{:S(2)}, u32[]{:S(2)}) collective-permute-start(bf16[3,1024,128]{2,1,0:T(8,128)(2,1)} %pad_maximum_fusion), channel_id=1, source_target_pairs={{0,1},{1,0},{2,3},{3,2},{4,5},{5,4},{6,7},{7,6},{8,9},{9,8},{10,11... | collective-permute-start | bytes 2359304 | tf_op jit(solution)/shard_map/ppermute | solution.py:217
  82.7 6.1 %collective-permute-start.16 = (bf16[128,512]{1,0:T(8,128)(2,1)S(1)}, bf16[128,512]{1,0:T(8,128)(2,1)S(1)}, u32[]{:S(2)}, u32[]{:S(2)}) collective-permute-start(bf16[128,512]{1,0:T(8,128)(2,1)S(1)} %reduce_sum.21), channel_id=1, source_target_pairs={{0,6},{1,7},{2,0},{3,1},{4,2},{5,3},{6,4},{7,5},{8,14},{9,15},{10,... | collective-permute-start | bytes 393224 | tf_op jit(solution)/shard_map/ppermute | solution.py:217
  83.7 6.5 %collective-permute-start.15 = (bf16[128,512]{1,0:T(8,128)(2,1)S(1)}, bf16[128,512]{1,0:T(8,128)(2,1)S(1)}, u32[]{:S(2)}, u32[]{:S(2)}) collective-permute-start(bf16[128,512]{1,0:T(8,128)(2,1)S(1)} %reduce_sum.21), channel_id=1, source_target_pairs={{0,4},{1,5},{2,6},{3,7},{4,0},{5,1},{6,2},{7,3},{8,12},{9,13},{10,... | collective-permute-start | bytes 393224 | tf_op jit(solution)/shard_map/ppermute | solution.py:217
  85.7 5.5 %collective-permute-start.14 = (bf16[128,512]{1,0:T(8,128)(2,1)S(1)}, bf16[128,512]{1,0:T(8,128)(2,1)S(1)}, u32[]{:S(2)}, u32[]{:S(2)}) collective-permute-start(bf16[128,512]{1,0:T(8,128)(2,1)S(1)} %reduce_sum.21), channel_id=1, source_target_pairs={{0,2},{1,3},{2,4},{3,5},{4,6},{5,7},{6,0},{7,1},{8,10},{9,11},{10,... | collective-permute-start | bytes 393224 | tf_op jit(solution)/shard_map/ppermute | solution.py:217
  88.8 6.3 %collective-permute-start.17 = (bf16[128,512]{1,0:T(8,128)(2,1)S(1)}, bf16[128,512]{1,0:T(8,128)(2,1)S(1)}, u32[]{:S(2)}, u32[]{:S(2)}) collective-permute-start(bf16[128,512]{1,0:T(8,128)(2,1)S(1)} %add_convert_fusion.7), channel_id=1, source_target_pairs={{0,32},{32,64},{64,96},{96,128},{128,160},{160,192},{192,224},{224... | collective-permute-start | bytes 393224 | tf_op jit(solution)/shard_map/ppermute | solution.py:197
  95.1 2.3 %collective-permute-start.19 = (bf16[512,512]{1,0:T(8,128)(2,1)S(1)}, bf16[512,512]{1,0:T(8,128)(2,1)S(1)}, u32[]{:S(2)}, u32[]{:S(2)}) collective-permute-start(bf16[512,512]{1,0:T(8,128)(2,1)S(1)} %pad_maximum_fusion.1.refs_6_), channel_id=1, source_target_pairs={{0,1},{1,0},{2,3},{3,2},{4,5},{5,4},{6,7},{7,6},{8,9},{9,8},{10,11... | collective-permute-start | bytes 1572872 | tf_op jit(solution)/shard_map/ppermute | solution.py:217
  95.1 2.3 %collective-permute-start.12 = (bf16[1024,128]{1,0:T(8,128)(2,1)S(1)}, bf16[1024,128]{1,0:T(8,128)(2,1)S(1)}, u32[]{:S(2)}, u32[]{:S(2)}) collective-permute-start(bf16[1024,128]{1,0:T(8,128)(2,1)S(1)} %slice_bitcast_fusion), channel_id=1, source_target_pairs={{0,1},{1,0},{2,3},{3,2},{4,5},{5,4},{6,7},{7,6},{8,9},{9,8},{10,11... | collective-permute-start | bytes 786440 | tf_op jit(solution)/shard_map/ppermute | solution.py:217
  98.6 10.2 %collective-permute-start.20 = (bf16[256,512]{1,0:T(8,128)(2,1)S(1)}, bf16[256,512]{1,0:T(8,128)(2,1)S(1)}, u32[]{:S(2)}, u32[]{:S(2)}) collective-permute-start(bf16[256,512]{1,0:T(8,128)(2,1)S(1)} %get-tuple-element.69), channel_id=1, source_target_pairs={{0,8},{1,9},{2,10},{3,11},{4,12},{5,13},{6,14},{7,15},{8,16},{9,17... | collective-permute-start | bytes 786440 | tf_op jit(solution)/shard_map/ppermute | solution.py:217
  100.3 14.8 %collective-permute-start.21 = (bf16[256,512]{1,0:T(8,128)(2,1)S(1)}, bf16[256,512]{1,0:T(8,128)(2,1)S(1)}, u32[]{:S(2)}, u32[]{:S(2)}) collective-permute-start(bf16[256,512]{1,0:T(8,128)(2,1)S(1)} %get-tuple-element.70), channel_id=1, source_target_pairs={{0,16},{1,17},{2,18},{3,19},{4,20},{5,21},{6,22},{7,23},{8,24},{9,... | collective-permute-start | bytes 786440 | tf_op jit(solution)/shard_map/ppermute | solution.py:217
  103.2 11.9 %collective-permute-start.22 = (bf16[256,512]{1,0:T(8,128)(2,1)S(1)}, bf16[256,512]{1,0:T(8,128)(2,1)S(1)}, u32[]{:S(2)}, u32[]{:S(2)}) collective-permute-start(bf16[256,512]{1,0:T(8,128)(2,1)S(1)} %get-tuple-element.71), channel_id=1, source_target_pairs={{0,24},{1,25},{2,26},{3,27},{4,28},{5,29},{6,30},{7,31},{8,0},{9,1... | collective-permute-start | bytes 786440 | tf_op jit(solution)/shard_map/ppermute | solution.py:217
  105.4 10.5 %collective-permute-start.24 = (bf16[128,512]{1,0:T(8,128)(2,1)S(1)}, bf16[128,512]{1,0:T(8,128)(2,1)S(1)}, u32[]{:S(2)}, u32[]{:S(2)}) collective-permute-start(bf16[128,512]{1,0:T(8,128)(2,1)S(1)} %add_convert_fusion.5), channel_id=1, source_target_pairs={{0,224},{32,0},{64,32},{96,64},{128,96},{160,128},{192,160},{224,1... | collective-permute-start | bytes 393224 | tf_op jit(solution)/shard_map/ppermute | solution.py:197
  106.7 9.2 %collective-permute-start.23 = (bf16[128,512]{1,0:T(8,128)(2,1)S(1)}, bf16[128,512]{1,0:T(8,128)(2,1)S(1)}, u32[]{:S(2)}, u32[]{:S(2)}) collective-permute-start(bf16[128,512]{1,0:T(8,128)(2,1)S(1)} %add_convert_fusion.6), channel_id=1, source_target_pairs={{0,32},{32,64},{64,96},{96,128},{128,160},{160,192},{192,224},{224... | collective-permute-start | bytes 393224 | tf_op jit(solution)/shard_map/ppermute | solution.py:197
  115.9 15.9 %all-to-all-start.1 = ((bf16[8,32,512]{2,1,0:T(8,128)(2,1)}), bf16[8,32,512]{2,1,0:T(8,128)(2,1)S(1)}, u32[]{:S(2)}, u32[]{:S(2)}) async-start(bf16[8,32,512]{2,1,0:T(8,128)(2,1)} %bitcast.11), calls=%async_computation.1 | async-start | bytes 524288 | tf_op jit(solution)/shard_map/all_to_all | solution.py:345
  119.4 10.4 %collective-permute-start.26 = (bf16[128,512]{1,0:T(8,128)(2,1)S(1)}, bf16[128,512]{1,0:T(8,128)(2,1)S(1)}, u32[]{:S(2)}, u32[]{:S(2)}) collective-permute-start(bf16[128,512]{1,0:T(8,128)(2,1)S(1)} %add_convert_fusion.3), channel_id=1, source_target_pairs={{0,224},{32,0},{64,32},{96,64},{128,96},{160,128},{192,160},{224,1... | collective-permute-start | bytes 393224 | tf_op jit(solution)/shard_map/ppermute | solution.py:197
  122.7 8.0 %collective-permute-start.25 = (bf16[128,512]{1,0:T(8,128)(2,1)S(1)}, bf16[128,512]{1,0:T(8,128)(2,1)S(1)}, u32[]{:S(2)}, u32[]{:S(2)}) collective-permute-start(bf16[128,512]{1,0:T(8,128)(2,1)S(1)} %add_convert_fusion.4), channel_id=1, source_target_pairs={{0,32},{32,64},{64,96},{96,128},{128,160},{160,192},{192,224},{224... | collective-permute-start | bytes 393224 | tf_op jit(solution)/shard_map/ppermute | solution.py:197
  (10 other events, 158.3 us)
